TPU v7x, 256 devices: a whole 4x4x8 slice. The times are simulated.
256 devices in a mesh: lev: 4 (over y), tile: 64 (over x, z, core).
Axes of the slice: x: 4, y: 4, z: 8, core: 2. Of those that a mesh axis runs over, the one named last changes fastest.
Arguments:
- atm_state: bfloat16 [12, 6, 524288], P('lev', None, 'tile'), may hold values from -6 to 6
- surface: bfloat16 [4, 524288], P('lev', 'tile'), may hold values from -6 to 6
- mlp_in: bfloat16 [76, 512], replicated, may hold values from -0.625 to 0.625
- mlp_mid: bfloat16 [512, 512], replicated, may hold values from -0.25 to 0.25
- mlp_out: bfloat16 [512, 72], replicated, may hold values from -0.25 to 0.25
- mlp_flux: bfloat16 [512, 8], replicated, may hold values from -0.25 to 0.25
- ocean_state: bfloat16 [76, 1024, 512], P(None, 'tile', 'lev'), may hold values from -6 to 6
- ocean_mask: int32 [1024, 512], P('tile', 'lev'), may hold values 0 or 1
- fold_map: int32 [1024], replicated, may hold values from 0 to 1023, as said below
- pair_tile: int32 [64, 4, 4], P('tile', 'lev'), may hold values from 0 to 63
- pair_block: int32 [64, 4, 4], P('tile', 'lev'), may hold values from 0 to 15
- pair_count: int32 [64, 4], P('tile', 'lev'), may hold values from 1 to 4, as said below
- margin: bfloat16 [4, 128, 1024, 512], P(None, None, 'tile', 'lev'), may hold values from 0.00049 to 1
- conv_in: bfloat16 [3, 3, 84, 256], replicated, may hold values from -0.21875 to 0.21875
- conv_mid: bfloat16 [3, 3, 256, 256], replicated, may hold values from -0.125 to 0.125
- conv_out: bfloat16 [3, 3, 256, 76], replicated, may hold values from -0.125 to 0.125
Outputs:
- atm_next: bfloat16 [12, 6, 524288], P('lev', None, 'tile')
- ocean_next: bfloat16 [76, 1024, 512], P(None, 'tile', 'lev')
Inputs may be any that keep to these rules, and one draw needn't show every extreme that they name: The fold reflects the columns about a seam: fold_map[x] = (s - 1 - x) mod 1024 for every column x, with one offset s of 0 to 1023 for the whole grid. `pair_tile`: the source of a slot is the atmosphere block of the device with the same lev index and this tile index. `pair_count`: slots at and beyond the count hold entries that are not used.
All inputs are finite; a program needn't handle non-finite values. No bound on the sum of `ocean_mask` on one device may be relied on, other than what follows from the above.
Results may differ from a plain program's by a relative error of at most 0.0055.
Values may be sent and summed in bfloat16 or wider, within the bound.
No kernel may reach another device: no remote copies, remote signals or barrier semaphores. Data moves between devices by JAX's collectives and lax.ppermute only.
A program may use at most 128 MiB of HBM per device.

v0:
```python
import jax
import jax.numpy as jnp
from jax import lax
from jax.sharding import PartitionSpec as P


def extended(block, sides, width, periodic):
    for axis, dim in sides:
        count = lax.axis_size(axis)
        forward = [(i, i + 1) for i in range(count - 1)]
        if periodic:
            forward.append((count - 1, 0))
        backward = [(target, source) for source, target in forward]
        low = lax.ppermute(
            lax.slice_in_dim(block, block.shape[dim] - width, None, axis=dim), axis, forward
        )
        high = lax.ppermute(lax.slice_in_dim(block, 0, width, axis=dim), axis, backward)
        block = jnp.concatenate([low, block, high], axis=dim)
    return block


def column_model(pieces, mlp_in, mlp_mid, mlp_out, mlp_flux):
    levels_part, surface_part = pieces
    level_rows = levels_part[:, 0, :]
    stacked = jnp.concatenate([level_rows, surface_part[:, 0, :]], axis=0)
    first = jax.nn.gelu(jnp.dot(mlp_in.T, stacked, preferred_element_type=jnp.float32)).astype(
        jnp.bfloat16
    )
    second = jax.nn.gelu(jnp.dot(mlp_mid.T, first, preferred_element_type=jnp.float32)).astype(
        jnp.bfloat16
    )
    change = jnp.dot(mlp_out.T, second, preferred_element_type=jnp.float32)
    updated = (level_rows.astype(jnp.float32) + change).astype(jnp.bfloat16)
    fluxes = jnp.dot(mlp_flux.T, second, preferred_element_type=jnp.float32).astype(jnp.bfloat16)
    return (updated[:, None, :], fluxes[:, None, :])


def extend(grid, fold_map):
    span_x = grid.shape[1]
    span_y = grid.shape[2]
    sideways = extended(grid, (("tile", 1),), 1, True)
    padded = extended(sideways, (("lev", 2),), 1, False)
    top_rows = grid[:, :, span_y - 1]
    every_top = lax.all_gather(top_rows, "tile", axis=1, tiled=True)
    all_columns = every_top.shape[1]
    lead_col = lax.axis_index("tile") * span_x - 1
    global_cols = (lead_col + jnp.arange(span_x + 2, dtype=jnp.int32)) % all_columns
    partner = jnp.take(fold_map, global_cols)
    folded = jnp.take(every_top, partner, axis=1)
    at_top = lax.axis_index("lev") == lax.axis_size("lev") - 1
    upper_rim = jnp.where(at_top, folded, padded[:, :, span_y + 1])
    return padded.at[:, :, span_y + 1].set(upper_rim)


def convolve(padded, kernel):
    span_x = padded.shape[1] - 2
    span_y = padded.shape[2] - 2
    result = jnp.zeros((kernel.shape[3], span_x, span_y), jnp.float32)
    for shift_x in range(3):
        for shift_y in range(3):
            window = padded[:, shift_x : shift_x + span_x, shift_y : shift_y + span_y]
            result = result + jnp.einsum(
                "co,cxy->oxy", kernel[shift_x, shift_y], window, preferred_element_type=jnp.float32
            )
    return result


def per_device(
    atm_state,
    surface,
    mlp_in,
    mlp_mid,
    mlp_out,
    mlp_flux,
    ocean_state,
    ocean_mask,
    fold_map,
    pair_tile,
    pair_block,
    pair_count,
    margin,
    conv_in,
    conv_mid,
    conv_out,
):
    lev_dev, fields_n, tile_cols = atm_state.shape
    groups = lax.axis_size("lev")
    per_col = tile_cols // groups
    level_blocks = atm_state.reshape(lev_dev * fields_n, groups, per_col)
    surface_blocks = surface.reshape(surface.shape[0], groups, per_col)
    updated, fluxes = column_model(
        (
            lax.all_to_all(level_blocks, "lev", split_axis=1, concat_axis=0, tiled=True),
            lax.all_to_all(surface_blocks, "lev", split_axis=1, concat_axis=0, tiled=True),
        ),
        mlp_in,
        mlp_mid,
        mlp_out,
        mlp_flux,
    )
    column_state = updated.reshape(lev_dev * groups, fields_n, per_col)
    atm_next = lax.all_to_all(column_state, "lev", split_axis=0, concat_axis=2, tiled=True)
    flux_cols = fluxes[:, 0, :]
    och = ocean_state.shape[0]
    span_x = ocean_state.shape[1]
    span_y = ocean_state.shape[2]
    land_sea = ocean_mask.astype(jnp.float32)
    state_padded = extend(ocean_state, fold_map)
    state_term = convolve(state_padded, conv_in[:, :, :och])
    pairs = pair_tile.shape[2]
    blk_cols = margin.shape[1]
    flux_rows = flux_cols.shape[0]
    slot_tiles = pair_tile[0, 0]
    slot_blocks = pair_block[0, 0]
    slot_used = (jnp.arange(pairs, dtype=jnp.int32) < pair_count[0, 0]).astype(jnp.bfloat16)
    starts = slot_tiles * per_col + slot_blocks * blk_cols
    piece = lax.all_gather(flux_cols, "tile", axis=1, tiled=True)
    piece_cols = piece.shape[1]

    def take_slot(slot_start):
        inside = (slot_start >= 0) & (slot_start + blk_cols <= piece_cols)
        sliced = lax.dynamic_slice_in_dim(
            piece, jnp.clip(slot_start, 0, piece_cols - blk_cols), blk_cols, 1
        )
        return jnp.where(inside, sliced, jnp.zeros_like(sliced))

    received = jax.vmap(take_slot)(starts)
    weights = margin.reshape(pairs, blk_cols, span_x * span_y)
    masked = received * slot_used[:, None, None]
    numer = jnp.einsum("pfb,pbc->fc", masked, weights, preferred_element_type=jnp.float32)
    denom = jnp.einsum("p,pbc->c", slot_used, weights, preferred_element_type=jnp.float32)
    ocean_flux = (numer / denom[None]).astype(jnp.bfloat16).reshape(flux_rows, span_x, span_y)
    flux_padded = extend(ocean_flux, fold_map)
    first_pre = state_term + convolve(flux_padded, conv_in[:, :, och:])
    hidden_one = (jax.nn.gelu(first_pre) * land_sea).astype(jnp.bfloat16)
    hidden_two = (jax.nn.gelu(convolve(extend(hidden_one, fold_map), conv_mid)) * land_sea).astype(
        jnp.bfloat16
    )
    change = convolve(extend(hidden_two, fold_map), conv_out)
    ocean_next = ((ocean_state.astype(jnp.float32) + change) * land_sea).astype(jnp.bfloat16)
    return (atm_next, ocean_next)


def solution(mesh):
    return jax.shard_map(
        per_device,
        mesh=mesh,
        in_specs=(
            P("lev", None, "tile"),
            P("lev", "tile"),
            P(),
            P(),
            P(),
            P(),
            P(None, "tile", "lev"),
            P("tile", "lev"),
            P(),
            P("tile", "lev", None),
            P("tile", "lev", None),
            P("tile", "lev"),
            P(None, None, "tile", "lev"),
            P(),
            P(),
            P(),
        ),
        out_specs=(P("lev", None, "tile"), P(None, "tile", "lev")),
        check_vma=False,
    )
```

profile of v0, /device:TPU:16, one launch (start us, length us, event | category | flops | bytes accessed | tf_op | source)
XLA Modules:
  0.0 383.5 jit_solution(3840292426989696657)
XLA Ops:
  9.8 5.3 %all-to-all-start.1 = ((bf16[4,2,1024]{2,1,0:T(2,128)(2,1)}), bf16[4,2,1024]{2,1,0:T(2,128)(2,1)S(1)}, u32[]{:S(2)}, u32[]{:S(2)}) async-start(bf16[4,2,1024]{2,1,0:T(2,128)(2,1)} %reshape.367), calls=%async_computation.1 | async-start | bytes 32768 | tf_op jit(solution)/shard_map/all_to_all | solution.py:94
  16.3 6.5 %collective-permute-start.1 = (bf16[76,1,128]{2,0,1:T(8,128)(2,1)S(1)}, bf16[76,1,128]{2,0,1:T(8,128)(2,1)S(1)}, u32[]{:S(2)}, u32[]{:S(2)}) collective-permute-start(bf16[76,1,128]{2,0,1:T(8,128)(2,1)S(1)} %copy.270), channel_id=1, source_target_pairs={{1,0},{2,1},{3,2},{4,3},{5,4},{6,5},{7,6},{8,7},{9,8},{10,9},{11,1... | collective-permute-start | bytes 58376 | tf_op jit(solution)/shard_map/ppermute | solution.py:17
  28.8 4.8 %all-to-all-start = ((bf16[18,4,2048]{2,0,1:T(8,128)(2,1)}), bf16[18,4,2048]{2,0,1:T(8,128)(2,1)S(1)}, u32[]{:S(2)}, u32[]{:S(2)}) async-start(bf16[18,4,2048]{2,0,1:T(8,128)(2,1)} %copy.208), calls=%async_computation | async-start | bytes 786432 | tf_op jit(solution)/shard_map/all_to_all | solution.py:93
  33.7 4.3 %all-to-all-done = bf16[18,4,2048]{2,0,1:T(8,128)(2,1)S(1)} async-done(((bf16[18,4,2048]{2,0,1:T(8,128)(2,1)}), bf16[18,4,2048]{2,0,1:T(8,128)(2,1)S(1)}, u32[]{:S(2)}, u32[]{:S(2)}) %all-to-all-start) | async-done | bytes 294944 | tf_op jit(solution)/shard_map/all_to_all | solution.py:93
  38.8 3.3 fusion.15
  46.5 4.0 %collective-permute-start.2 = (bf16[76,18,1]{2,0,1:T(8,128)(2,1)}, bf16[76,18,1]{2,0,1:T(8,128)(2,1)}, u32[]{:S(2)}, u32[]{:S(2)}) collective-permute-start(bf16[76,18,1]{2,0,1:T(8,128)(2,1)} %get-tuple-element.92), channel_id=1, source_target_pairs={{0,64},{64,128},{128,192},{1,65},{65,129},{129,193},{2,66},{66,130... | collective-permute-start | bytes 8216 | tf_op jit(solution)/shard_map/ppermute | solution.py:14
  52.4 42.4 %all-gather = bf16[76,1024,1]{0,1,2:T(8,128)(2,1)S(1)} all-gather(bf16[76,16,1]{0,1,2:T(8,128)(2,1)S(1)} %copy.256), channel_id=2, replica_groups=mesh['lev'=4,'tile'=64] {'tile'}, dimensions={1}, use_global_device_ids=true | all-gather | bytes 158080 | tf_op jit(solution)/shard_map/all_gather | solution.py:44
  99.6 2.9 scatter.14
  117.3 3.1 fusion.89
  120.4 2.7 fusion.91
  123.0 8.0 %while.6 = (s32[]{:T(128)}, bf16[8,131072]{1,0:T(8,128)(2,1)}, s32[4,2]{0,1:T(2,128)S(1)}, bf16[4,8,128]{2,1,0:T(8,128)(2,1)S(1)}) while((s32[]{:T(128)}, bf16[8,131072]{1,0:T(8,128)(2,1)}, s32[4,2]{0,1:T(2,128)S(1)}, bf16[4,8,128]{2,1,0:T(8,128)(2,1)S(1)}) %tuple.57), condition=%wide.while_cond.4.clone, body=%wide.while_body.4.sunk.clone | while | flops 2 | bytes 4193 | solution.py:122
  131.9 4.7 %collective-permute-start.5 = (bf16[8,1,128]{2,0,1:T(8,128)(2,1)S(1)}, bf16[8,1,128]{2,0,1:T(8,128)(2,1)S(1)}, u32[]{:S(2)}, u32[]{:S(2)}) collective-permute-start(bf16[8,1,128]{2,0,1:T(8,128)(2,1)S(1)} %get-tuple-element.99), channel_id=1, source_target_pairs={{1,0},{2,1},{3,2},{4,3},{5,4},{6,5},{7,6},{8,7},{9,8},{10,9},{11,1... | collective-permute-start | bytes 6152 | tf_op jit(solution)/shard_map/ppermute | solution.py:17
  136.8 47.7 %all-gather.1 = bf16[8,1024,1]{0,2,1:T(2,128)(2,1)S(1)} all-gather(bf16[8,16,1]{0,2,1:T(2,128)(2,1)S(1)} %copy.216), channel_id=3, replica_groups=mesh['lev'=4,'tile'=64] {'tile'}, dimensions={1}, use_global_device_ids=true | all-gather | bytes 16640 | tf_op jit(solution)/shard_map/all_gather | solution.py:44
  184.6 3.9 %collective-permute-start.6 = (bf16[8,18,1]{2,0,1:T(8,128)(2,1)S(1)}, bf16[8,18,1]{2,0,1:T(8,128)(2,1)S(1)}, u32[]{:S(2)}, u32[]{:S(2)}) collective-permute-start(bf16[8,18,1]{2,0,1:T(8,128)(2,1)S(1)} %get-tuple-element.96), channel_id=1, source_target_pairs={{0,64},{64,128},{128,192},{1,65},{65,129},{129,193},{2,66},{66,130... | collective-permute-start | bytes 872 | tf_op jit(solution)/shard_map/ppermute | solution.py:14
  188.5 2.8 collective-permute-start.7
  196.0 2.6 fusion.160
  198.6 2.5 fusion.162
  201.1 2.7 fusion.164
  203.9 2.8 fusion.166
  206.7 2.6 fusion.168
  209.4 2.7 fusion.170
  212.1 2.8 fusion.172
  214.9 2.5 fusion.174
  217.5 9.2 %fusion.29 = bf16[256,16,128]{0,2,1:T(8,128)(2,1)S(1)} fusion(f32[16,128,256]{2,1,0:T(8,128)S(1)} %copy-done.3, f32[16,128,256]{2,1,0:T(8,128)} %fusion.160, f32[16,128,256]{2,1,0:T(8,128)S(1)} %copy-done.4, f32[16,128,256]{2,1,0:T(8,128)} %fusion.162, f32[16,128,256]{2,1,0:T(8,128)S(1)} %copy-done.5, f32[16,128,256]{2,1,0:T(8,128)} %fusion.164, ...), kind=kOutput, calls=%fused_computation.44 | convolution fusion | flops 22544384 | bytes 36745216 | tf_op jit(solution)/shard_map/co,cxy->oxy/dot_general | solution.py:62
  226.8 5.1 %collective-permute-start.9 = (bf16[256,1,128]{0,2,1:T(8,128)(2,1)S(1)}, bf16[256,1,128]{0,2,1:T(8,128)(2,1)S(1)}, u32[]{:S(2)}, u32[]{:S(2)}) collective-permute-start(bf16[256,1,128]{0,2,1:T(8,128)(2,1)S(1)} %get-tuple-element.91), channel_id=1, source_target_pairs={{1,0},{2,1},{3,2},{4,3},{5,4},{6,5},{7,6},{8,7},{9,8},{10,9},{11,1... | collective-permute-start | bytes 196616 | tf_op jit(solution)/shard_map/ppermute | solution.py:17
  235.0 5.6 %all-to-all-start.2 = ((bf16[12,6,2048]{2,1,0:T(8,128)(2,1)}), bf16[12,6,2048]{2,1,0:T(8,128)(2,1)S(1)}, u32[]{:S(2)}, u32[]{:S(2)}) async-start(bf16[12,6,2048]{2,1,0:T(8,128)(2,1)} %reshape_broadcast_in_dim.3), calls=%async_computation.2 | async-start | bytes 786432 | tf_op jit(solution)/shard_map/all_to_all | solution.py:102
  240.7 2.5 collective-permute-start.11
  243.2 48.2 %all-gather.2 = bf16[256,1024,1]{0,1,2:T(8,128)(2,1)S(1)} all-gather(bf16[256,16,1]{0,1,2:T(8,128)(2,1)S(1)} %copy.221), channel_id=4, replica_groups=mesh['lev'=4,'tile'=64] {'tile'}, dimensions={1}, use_global_device_ids=true | all-gather | bytes 532480 | tf_op jit(solution)/shard_map/all_gather | solution.py:44
  292.0 3.4 collective-permute-start.10
  305.3 5.1 %collective-permute-start.13 = (bf16[256,1,128]{0,2,1:T(8,128)(2,1)S(1)}, bf16[256,1,128]{0,2,1:T(8,128)(2,1)S(1)}, u32[]{:S(2)}, u32[]{:S(2)}) collective-permute-start(bf16[256,1,128]{0,2,1:T(8,128)(2,1)S(1)} %get-tuple-element.89), channel_id=1, source_target_pairs={{1,0},{2,1},{3,2},{4,3},{5,4},{6,5},{7,6},{8,7},{9,8},{10,9},{11,1... | collective-permute-start | bytes 196616 | tf_op jit(solution)/shard_map/ppermute | solution.py:17
  314.4 49.7 %all-gather.3 = bf16[256,1024,1]{0,1,2:T(8,128)(2,1)S(1)} all-gather(bf16[256,16,1]{0,1,2:T(8,128)(2,1)S(1)} %copy.225), channel_id=5, replica_groups=mesh['lev'=4,'tile'=64] {'tile'}, dimensions={1}, use_global_device_ids=true | all-gather | bytes 532480 | tf_op jit(solution)/shard_map/all_gather | solution.py:44
  364.7 3.6 collective-permute-start.14
  (183 shorter events, 75.6 us)
Async XLA Ops:
  7.2 31.7 %copy-start = (bf16[512,512]{1,0:T(8,128)(2,1)S(1)}, bf16[512,512]{1,0:T(8,128)(2,1)}, u32[]{:S(2)}) copy-start(bf16[512,512]{1,0:T(8,128)(2,1)} %param.31) | copy-start | bytes 1572868
  7.2 19.6 %copy-start.18 = (bf16[3,6,8192]{2,1,0:T(8,128)(2,1)S(1)}, bf16[3,6,8192]{2,1,0:T(8,128)(2,1)}, u32[]{:S(2)}) copy-start(bf16[3,6,8192]{2,1,0:T(8,128)(2,1)} %param.28) | copy-start | bytes 884740
  7.2 20.9 %copy-start.2 = (s32[1024]{0:T(1024)S(1)}, s32[1024]{0:T(1024)}, u32[]{:S(2)}) copy-start(s32[1024]{0:T(1024)} %param.36) | copy-start | bytes 12292
  9.8 18.9 %all-to-all-start.1 = ((bf16[4,2,1024]{2,1,0:T(2,128)(2,1)}), bf16[4,2,1024]{2,1,0:T(2,128)(2,1)S(1)}, u32[]{:S(2)}, u32[]{:S(2)}) async-start(bf16[4,2,1024]{2,1,0:T(2,128)(2,1)} %reshape.367), calls=%async_computation.1 | async-start | bytes 32768 | tf_op jit(solution)/shard_map/all_to_all | solution.py:94
  16.2 29.2 %collective-permute-start = (bf16[76,1,128]{2,0,1:T(8,128)(2,1)S(1)}, bf16[76,1,128]{2,0,1:T(8,128)(2,1)S(1)}, u32[]{:S(2)}, u32[]{:S(2)}) collective-permute-start(bf16[76,1,128]{2,0,1:T(8,128)(2,1)S(1)} %copy.269), channel_id=1, source_target_pairs={{0,1},{1,2},{2,3},{3,4},{4,5},{5,6},{6,7},{7,8},{8,9},{9,10},{10,1... | collective-permute-start | bytes 58376 | tf_op jit(solution)/shard_map/ppermute | solution.py:14
  16.3 29.2 %collective-permute-start.1 = (bf16[76,1,128]{2,0,1:T(8,128)(2,1)S(1)}, bf16[76,1,128]{2,0,1:T(8,128)(2,1)S(1)}, u32[]{:S(2)}, u32[]{:S(2)}) collective-permute-start(bf16[76,1,128]{2,0,1:T(8,128)(2,1)S(1)} %copy.270), channel_id=1, source_target_pairs={{1,0},{2,1},{3,2},{4,3},{5,4},{6,5},{7,6},{8,7},{9,8},{10,9},{11,1... | collective-permute-start | bytes 58376 | tf_op jit(solution)/shard_map/ppermute | solution.py:17
  26.1 12.8 %copy-start.23 = (bf16[76,512]{1,0:T(8,128)(2,1)S(1)}, bf16[76,512]{1,0:T(8,128)(2,1)}, u32[]{:S(2)}) copy-start(bf16[76,512]{1,0:T(8,128)(2,1)} %param.30) | copy-start | bytes 233476
  28.8 9.2 %all-to-all-start = ((bf16[18,4,2048]{2,0,1:T(8,128)(2,1)}), bf16[18,4,2048]{2,0,1:T(8,128)(2,1)S(1)}, u32[]{:S(2)}, u32[]{:S(2)}) async-start(bf16[18,4,2048]{2,0,1:T(8,128)(2,1)} %copy.208), calls=%async_computation | async-start | bytes 786432 | tf_op jit(solution)/shard_map/all_to_all | solution.py:93
  33.6 89.4 %all-gather.6.cloned.1.call-start = ((), (), s32[]{:S(2)}) async-start(), calls=%async_computation.3 | async-start | bytes 2129920 | tf_op jit(solution)/shard_map/all_gather | solution.py:117
  44.7 50.2 %copy-start.9 = (bf16[4,128,16,128]{3,2,1,0:T(8,128)(2,1)S(1)}, bf16[4,128,16,128]{3,2,1,0:T(8,128)(2,1)}, u32[]{:S(2)}) copy-start(bf16[4,128,16,128]{3,2,1,0:T(8,128)(2,1)} %param.40) | copy-start | bytes 6291460
  46.5 51.6 %collective-permute-start.2 = (bf16[76,18,1]{2,0,1:T(8,128)(2,1)}, bf16[76,18,1]{2,0,1:T(8,128)(2,1)}, u32[]{:S(2)}, u32[]{:S(2)}) collective-permute-start(bf16[76,18,1]{2,0,1:T(8,128)(2,1)} %get-tuple-element.92), channel_id=1, source_target_pairs={{0,64},{64,128},{128,192},{1,65},{65,129},{129,193},{2,66},{66,130... | collective-permute-start | bytes 8216 | tf_op jit(solution)/shard_map/ppermute | solution.py:14
  50.5 47.6 %collective-permute-start.3 = (bf16[76,18,1]{2,0,1:T(8,128)(2,1)}, bf16[76,18,1]{2,0,1:T(8,128)(2,1)S(1)}, u32[]{:S(2)}, u32[]{:S(2)}) collective-permute-start(bf16[76,18,1]{2,0,1:T(8,128)(2,1)} %get-tuple-element.93), channel_id=1, source_target_pairs={{64,0},{128,64},{192,128},{65,1},{129,65},{193,129},{66,2},{130,66... | collective-permute-start | bytes 8216 | tf_op jit(solution)/shard_map/ppermute | solution.py:17
  117.3 13.7 %copy-start.11 = (bf16[4,128,2048]{2,1,0:T(8,128)(2,1)S(1)}, bf16[4,128,2048]{2,1,0:T(8,128)(2,1)}, u32[]{:S(2)}) copy-start(bf16[4,128,2048]{2,1,0:T(8,128)(2,1)} %reshape.249) | copy-start | bytes 6291460
  131.5 53.0 %collective-permute-start.4 = (bf16[8,1,128]{2,0,1:T(8,128)(2,1)S(1)}, bf16[8,1,128]{2,0,1:T(8,128)(2,1)S(1)}, u32[]{:S(2)}, u32[]{:S(2)}) collective-permute-start(bf16[8,1,128]{2,0,1:T(8,128)(2,1)S(1)} %get-tuple-element.98), channel_id=1, source_target_pairs={{0,1},{1,2},{2,3},{3,4},{4,5},{5,6},{6,7},{7,8},{8,9},{9,10},{10,1... | collective-permute-start | bytes 6152 | tf_op jit(solution)/shard_map/ppermute | solution.py:14
  131.9 52.6 %collective-permute-start.5 = (bf16[8,1,128]{2,0,1:T(8,128)(2,1)S(1)}, bf16[8,1,128]{2,0,1:T(8,128)(2,1)S(1)}, u32[]{:S(2)}, u32[]{:S(2)}) collective-permute-start(bf16[8,1,128]{2,0,1:T(8,128)(2,1)S(1)} %get-tuple-element.99), channel_id=1, source_target_pairs={{1,0},{2,1},{3,2},{4,3},{5,4},{6,5},{7,6},{8,7},{9,8},{10,9},{11,1... | collective-permute-start | bytes 6152 | tf_op jit(solution)/shard_map/ppermute | solution.py:17
  184.6 7.6 %collective-permute-start.6 = (bf16[8,18,1]{2,0,1:T(8,128)(2,1)S(1)}, bf16[8,18,1]{2,0,1:T(8,128)(2,1)S(1)}, u32[]{:S(2)}, u32[]{:S(2)}) collective-permute-start(bf16[8,18,1]{2,0,1:T(8,128)(2,1)S(1)} %get-tuple-element.96), channel_id=1, source_target_pairs={{0,64},{64,128},{128,192},{1,65},{65,129},{129,193},{2,66},{66,130... | collective-permute-start | bytes 872 | tf_op jit(solution)/shard_map/ppermute | solution.py:14
  188.5 5.9 %collective-permute-start.7 = (bf16[8,18,1]{2,0,1:T(8,128)(2,1)S(1)}, bf16[8,18,1]{2,0,1:T(8,128)(2,1)S(1)}, u32[]{:S(2)}, u32[]{:S(2)}) collective-permute-start(bf16[8,18,1]{2,0,1:T(8,128)(2,1)S(1)} %get-tuple-element.97), channel_id=1, source_target_pairs={{64,0},{128,64},{192,128},{65,1},{129,65},{193,129},{66,2},{130,66... | collective-permute-start | bytes 872 | tf_op jit(solution)/shard_map/ppermute | solution.py:17
  201.1 16.3 %copy-start.8 = (f32[16,128,256]{2,1,0:T(8,128)S(1)}, f32[16,128,256]{2,1,0:T(8,128)}, u32[]{:S(2)}) copy-start(f32[16,128,256]{2,1,0:T(8,128)} %fusion.85) | copy-start | bytes 6291460
  203.9 13.5 %copy-start.7 = (f32[16,128,256]{2,1,0:T(8,128)S(1)}, f32[16,128,256]{2,1,0:T(8,128)}, u32[]{:S(2)}) copy-start(f32[16,128,256]{2,1,0:T(8,128)} %fusion.83) | copy-start | bytes 6291460
  206.7 10.7 %copy-start.6 = (f32[16,128,256]{2,1,0:T(8,128)S(1)}, f32[16,128,256]{2,1,0:T(8,128)}, u32[]{:S(2)}) copy-start(f32[16,128,256]{2,1,0:T(8,128)} %fusion.81) | copy-start | bytes 6291460
  217.4 14.4 %copy-start.16 = (bf16[72,2048]{1,0:T(8,128)(2,1)S(1)}, bf16[72,2048]{1,0:T(8,128)(2,1)}, u32[]{:S(2)}) copy-start(bf16[72,2048]{1,0:T(8,128)(2,1)} %copy-done.15) | copy-start | bytes 884740
  217.5 14.4 %copy-start.20 = (bf16[512,72]{0,1:T(8,128)(2,1)S(1)}, bf16[512,72]{0,1:T(8,128)(2,1)}, u32[]{:S(2)}) copy-start(bf16[512,72]{0,1:T(8,128)(2,1)} %param.32) | copy-start | bytes 221188
  226.7 14.0 %collective-permute-start.8 = (bf16[256,1,128]{0,2,1:T(8,128)(2,1)S(1)}, bf16[256,1,128]{0,2,1:T(8,128)(2,1)S(1)}, u32[]{:S(2)}, u32[]{:S(2)}) collective-permute-start(bf16[256,1,128]{0,2,1:T(8,128)(2,1)S(1)} %get-tuple-element.90), channel_id=1, source_target_pairs={{0,1},{1,2},{2,3},{3,4},{4,5},{5,6},{6,7},{7,8},{8,9},{9,10},{10,1... | collective-permute-start | bytes 196616 | tf_op jit(solution)/shard_map/ppermute | solution.py:14
  226.8 13.9 %collective-permute-start.9 = (bf16[256,1,128]{0,2,1:T(8,128)(2,1)S(1)}, bf16[256,1,128]{0,2,1:T(8,128)(2,1)S(1)}, u32[]{:S(2)}, u32[]{:S(2)}) collective-permute-start(bf16[256,1,128]{0,2,1:T(8,128)(2,1)S(1)} %get-tuple-element.91), channel_id=1, source_target_pairs={{1,0},{2,1},{3,2},{4,3},{5,4},{6,5},{7,6},{8,7},{9,8},{10,9},{11,1... | collective-permute-start | bytes 196616 | tf_op jit(solution)/shard_map/ppermute | solution.py:17
  235.0 75.3 %all-to-all-start.2 = ((bf16[12,6,2048]{2,1,0:T(8,128)(2,1)}), bf16[12,6,2048]{2,1,0:T(8,128)(2,1)S(1)}, u32[]{:S(2)}, u32[]{:S(2)}) async-start(bf16[12,6,2048]{2,1,0:T(8,128)(2,1)} %reshape_broadcast_in_dim.3), calls=%async_computation.2 | async-start | bytes 786432 | tf_op jit(solution)/shard_map/all_to_all | solution.py:102
  240.7 54.7 %collective-permute-start.11 = (bf16[256,18,1]{0,2,1:T(2,128)(2,1)S(1)}, bf16[256,18,1]{0,2,1:T(2,128)(2,1)S(1)}, u32[]{:S(2)}, u32[]{:S(2)}) collective-permute-start(bf16[256,18,1]{0,2,1:T(2,128)(2,1)S(1)} %get-tuple-element.87), channel_id=1, source_target_pairs={{64,0},{128,64},{192,128},{65,1},{129,65},{193,129},{66,2},{130,66... | collective-permute-start | bytes 27656 | tf_op jit(solution)/shard_map/ppermute | solution.py:17
  292.0 5.7 %collective-permute-start.10 = (bf16[256,18,1]{0,2,1:T(2,128)(2,1)S(1)}, bf16[256,18,1]{0,2,1:T(2,128)(2,1)S(1)}, u32[]{:S(2)}, u32[]{:S(2)}) collective-permute-start(bf16[256,18,1]{0,2,1:T(2,128)(2,1)S(1)} %get-tuple-element.86), channel_id=1, source_target_pairs={{0,64},{64,128},{128,192},{1,65},{65,129},{129,193},{2,66},{66,130... | collective-permute-start | bytes 27656 | tf_op jit(solution)/shard_map/ppermute | solution.py:14
  305.2 7.1 %collective-permute-start.12 = (bf16[256,1,128]{0,2,1:T(8,128)(2,1)S(1)}, bf16[256,1,128]{0,2,1:T(8,128)(2,1)S(1)}, u32[]{:S(2)}, u32[]{:S(2)}) collective-permute-start(bf16[256,1,128]{0,2,1:T(8,128)(2,1)S(1)} %get-tuple-element.88), channel_id=1, source_target_pairs={{0,1},{1,2},{2,3},{3,4},{4,5},{5,6},{6,7},{7,8},{8,9},{9,10},{10,1... | collective-permute-start | bytes 196616 | tf_op jit(solution)/shard_map/ppermute | solution.py:14
  305.3 7.0 %collective-permute-start.13 = (bf16[256,1,128]{0,2,1:T(8,128)(2,1)S(1)}, bf16[256,1,128]{0,2,1:T(8,128)(2,1)S(1)}, u32[]{:S(2)}, u32[]{:S(2)}) collective-permute-start(bf16[256,1,128]{0,2,1:T(8,128)(2,1)S(1)} %get-tuple-element.89), channel_id=1, source_target_pairs={{1,0},{2,1},{3,2},{4,3},{5,4},{6,5},{7,6},{8,7},{9,8},{10,9},{11,1... | collective-permute-start | bytes 196616 | tf_op jit(solution)/shard_map/ppermute | solution.py:17
  312.3 58.9 %copy-start.19 = (bf16[3,3,256,76]{2,3,1,0:T(8,128)(2,1)S(1)}, bf16[3,3,256,76]{2,3,1,0:T(8,128)(2,1)}, u32[]{:S(2)}) copy-start(bf16[3,3,256,76]{2,3,1,0:T(8,128)(2,1)} %param.43) | copy-start | bytes 1050628
  312.3 56.0 %collective-permute-start.15 = (bf16[256,18,1]{0,2,1:T(2,128)(2,1)S(1)}, bf16[256,18,1]{0,2,1:T(2,128)(2,1)S(1)}, u32[]{:S(2)}, u32[]{:S(2)}) collective-permute-start(bf16[256,18,1]{0,2,1:T(2,128)(2,1)S(1)} %get-tuple-element.85), channel_id=1, source_target_pairs={{64,0},{128,64},{192,128},{65,1},{129,65},{193,129},{66,2},{130,66... | collective-permute-start | bytes 27656 | tf_op jit(solution)/shard_map/ppermute | solution.py:17
  364.7 5.7 %collective-permute-start.14 = (bf16[256,18,1]{0,2,1:T(2,128)(2,1)S(1)}, bf16[256,18,1]{0,2,1:T(2,128)(2,1)S(1)}, u32[]{:S(2)}, u32[]{:S(2)}) collective-permute-start(bf16[256,18,1]{0,2,1:T(2,128)(2,1)S(1)} %get-tuple-element.84), channel_id=1, source_target_pairs={{0,64},{64,128},{128,192},{1,65},{65,129},{129,193},{2,66},{66,130... | collective-permute-start | bytes 27656 | tf_op jit(solution)/shard_map/ppermute | solution.py:14
  (12 other events, 38.6 us)
Sparse Core Ops, SparseCore 0:
  44.8 76.5 all-gather.5
where the time goes:
time: 391 us; the launch traced here: 384 us
  blocking collectives  188 us (48%)
  matrix products  69 us (18%)
  starting transfers between devices  61.9 us (16%)
  local copies, waits for them, and re-layouts  29.2 us (7%)
  between operations  15.8 us (4%)
  waiting for transfers between devices  11.4 us (3%)
  other arithmetic  8.23 us (2%)
    all_gather x4, blocking collectives, extend(): every_top = lax.all_gather(top_rows, 'tile', axis=1, tiled=True)  188 us
    dot_general x36, matrix products, convolve(): jnp.einsum('co,cxy->oxy', kernel[shift_x, shift_y], window, preferred_ele...  61.6 us
    ppermute x8, starting transfers between devices, extended(): lax.ppermute(lax.slice_in_dim(block, 0, width, axis=dim), axis, backward)  30.6 us
    ppermute x8, starting transfers between devices, extended(): lax.ppermute(lax.slice_in_dim(block, block.shape[dim] - width, None, axis...  15.5 us
    gather x12, local copies, waits for them, and re-layouts  7.97 us
  transfers between devices with their start and end apart: 20, of which 5 were waited for; matrix products, arithmetic and copies ran while one was open for 14% of the time, Pallas kernels for 0%

commit v1 on v0

v1 whole, which is shorter than its diff:
```python
import jax
import jax.numpy as jnp
from jax import lax
from jax.experimental import pallas as pl
from jax.experimental.pallas import tpu as pltpu
from jax.sharding import PartitionSpec as P

BF = jnp.bfloat16
F32 = jnp.float32
I32 = jnp.int32
SLAB = 8
HALO = 3
PITCH = 144
LANES = 128
VMEM = 56 * 1024 * 1024
C1 = 0.7978845608028654
C2 = C1 * 0.044715


def gelu(x):
    half = 0.5 * x
    return half * jnp.tanh(x * (C1 + C2 * (x * x))) + half


def dot(a, b):
    return jnp.dot(a, b, preferred_element_type=F32)


def dot_nt(a, b):
    return lax.dot_general(a, b, (((1,), (1,)), ((), ())), preferred_element_type=F32)


def iota(shape, dim):
    return lax.broadcasted_iota(I32, shape, dim)


def vmem_specs(n):
    return [pl.BlockSpec(memory_space=pltpu.VMEM)] * n


def smem_spec():
    return pl.BlockSpec(memory_space=pltpu.SMEM)


def params():
    return pltpu.CompilerParams(vmem_limit_bytes=VMEM)


def mlp_kernel(code_ref, z_ref, w1_ref, w2_ref, w3_ref, up_ref, send_ref, blocks, sends):
    rows, cols = z_ref.shape
    step = 512
    for c in range(0, cols, step):
        z = z_ref[:, c : c + step]
        first = gelu(dot(w1_ref[...], z)).astype(BF)
        second = gelu(dot(w2_ref[...], first)).astype(BF)
        out = dot(w3_ref[...], second)
        up_ref[:, c : c + step] = (z.astype(F32) + out[:rows]).astype(BF)
        for k in range(step // 128):
            blocks[c // 128 + k] = out[rows : rows + 8, 128 * k : 128 * k + 128].astype(BF).astype(F32)
    for i in range(send_ref.shape[0] * 4):
        code = code_ref[i]
        block = blocks[jnp.maximum(code, 0)]
        sends[i // 4, 8 * (i % 4) : 8 * (i % 4) + 8] = jnp.where(code >= 0, block, 0.0)
    send_ref[...] = sends[...].astype(BF)


def column_model(code, z, w1, w2, w3, tiles):
    rows, cols = z.shape
    return pl.pallas_call(
        mlp_kernel,
        in_specs=[smem_spec()] + vmem_specs(4),
        out_specs=vmem_specs(2),
        out_shape=[
            jax.ShapeDtypeStruct((rows, cols), BF),
            jax.ShapeDtypeStruct((tiles, 32, 128), BF),
        ],
        scratch_shapes=[pltpu.VMEM((cols // 128, 8, 128), F32), pltpu.VMEM((tiles, 32, 128), F32)],
        compiler_params=params(),
        cost_estimate=pl.CostEstimate(flops=3 * 10**9, bytes_accessed=2 * 10**6, transcendentals=0),
        name="column_model",
    )(code, z, w1, w2, w3)


def remap_kernel(scal_ref, got_ref, margin_ref, flux_ref, send_ref):
    tiles = got_ref.shape[0]
    count, tile = scal_ref[4], scal_ref[5]
    pieces = []
    for p in range(4):
        piece = got_ref[scal_ref[p]].astype(F32)[8 * p : 8 * p + 8]
        pieces.append(jnp.where(p < count, piece, 0.0))
    blocks = jnp.concatenate(pieces, axis=0).astype(BF)
    spread = (iota((128, 2048), 0) == iota((128, 2048), 1) // 16).astype(BF)
    wide = dot(blocks, spread)
    same = iota((16, 2048), 0) == iota((16, 2048), 1) % 16
    total = None
    for p in range(4):
        rows = jnp.broadcast_to(wide[8 * p : 8 * p + 8][None], (16, 8, 2048))
        rows = jnp.where(same[:, None, :], rows, 0.0).reshape(128, 2048)
        ones = jnp.where(same & (p < count), 1.0, 0.0)
        left = jnp.concatenate([rows, ones], axis=0).astype(BF)
        term = dot(left, margin_ref[2048 * p : 2048 * p + 2048])
        total = term if total is None else total + term
    numer = total[:128].reshape(16, 8, 128)
    flux = (numer / total[128:144][:, None, :]).reshape(128, 128).astype(BF)
    flux_ref[...] = flux
    wide = flux.astype(F32)
    top = dot_nt((iota((8, 128), 1) == 127 - iota((8, 128), 0)).astype(BF), flux)
    plain = jnp.concatenate([top, jnp.zeros((24, 128), F32)], axis=0).astype(BF)
    send_ref[...] = jnp.broadcast_to(plain[None], (tiles, 32, 128))
    send_ref[lax.rem(tile + 1, tiles)] = jnp.concatenate([top, wide[104:128]], axis=0).astype(BF)
    send_ref[lax.rem(tile + tiles - 1, tiles)] = jnp.concatenate([top, wide[0:24]], axis=0).astype(BF)


def remap(scal, got, margin):
    return pl.pallas_call(
        remap_kernel,
        in_specs=[smem_spec()] + vmem_specs(2),
        out_specs=vmem_specs(2),
        out_shape=[jax.ShapeDtypeStruct((128, 128), BF), jax.ShapeDtypeStruct(got.shape, BF)],
        compiler_params=params(),
        cost_estimate=pl.CostEstimate(flops=10**9, bytes_accessed=3 * 10**6, transcendentals=0),
        name="remap",
    )(scal, got, margin)


def rim_kernel(scal_ref, got_ref, flux_ref, wide_ref, up_ref, down_ref, fold_ref):
    tiles = got_ref.shape[0]
    tile, seam, shift = scal_ref[5], scal_ref[6], scal_ref[7]
    low = got_ref[lax.rem(tile + tiles - 1, tiles)].astype(F32)[8:32]
    high = got_ref[lax.rem(tile + 1, tiles)].astype(F32)[8:32]
    wide = jnp.concatenate([low, flux_ref[...].astype(F32), high, jnp.zeros((80, 128), F32)], axis=0).astype(BF)
    wide_ref[...] = wide
    row, col = iota((16, 128), 0), iota((16, 128), 1)
    up_ref[...] = dot_nt(((col == 125 + row) & (row < 3)).astype(BF), wide).astype(BF)
    down_ref[...] = dot_nt(((col == row) & (row < 3)).astype(BF), wide).astype(BF)
    total = None
    u, f = iota((128, 256), 0) // 8, iota((128, 256), 0) % 8
    i, g = iota((128, 256), 1) // 8, iota((128, 256), 1) % 8
    for e in (-1, 0, 1, 2):
        strip = got_ref[lax.rem(seam - tile - e + 3 * tiles, tiles)]
        pick = ((f == g) & (u == 16 * e + shift + HALO - i)).astype(BF)
        term = dot(strip, pick)
        total = term if total is None else total + term
    fold_ref[...] = total[:16].astype(BF)


def rim(scal, got, flux):
    strip = jax.ShapeDtypeStruct((16, 256), BF)
    return pl.pallas_call(
        rim_kernel,
        in_specs=[smem_spec()] + vmem_specs(2),
        out_specs=vmem_specs(4),
        out_shape=[jax.ShapeDtypeStruct((256, 128), BF), strip, strip, strip],
        compiler_params=params(),
        cost_estimate=pl.CostEstimate(flops=10**8, bytes_accessed=10**6, transcendentals=0),
        name="rim",
    )(scal, got, flux)


def conv_kernel(
    scal_ref, ext_ref, wide_ref, south_ref, north_ref, fold_ref, w1_ref, w1r_ref, w2_ref, w3_ref, out_ref,
    v3, h3, h2, result,
):
    top = scal_ref[8] == 1
    n0, n1, n2, n3 = 22, 20, 18, 16

    north = jnp.where(top, fold_ref[...].astype(F32), north_ref[...].astype(F32))
    rims = jnp.concatenate([south_ref[...].astype(F32), north], axis=0).astype(BF)
    row, col = iota((PITCH, 128), 0), iota((PITCH, 128), 1)
    fluxes = dot_nt((row == col + 3).astype(BF), wide_ref[...])
    row, col = iota((PITCH, 32), 0), iota((PITCH, 32), 1)
    put = ((col < 3) & (row == col)) | ((col >= 16) & (col < 19) & (row == col - 16 + 131))
    fluxes = fluxes + dot(put.astype(BF), rims)
    lane = iota((PITCH, LANES), 1)

    for x in range(n0):
        start = 8 * x
        part = fluxes[:, 128 * (start // 128) : 128 * (start // 128) + 128]
        part = pltpu.roll(part, (76 - start) % 128, 1)
        v = jnp.where(lane < 76, ext_ref[x].astype(F32), jnp.where(lane < 84, part, 0.0))
        before = pltpu.roll(v, 1, 0)
        here = pltpu.roll(v, 84, 1)
        after = pltpu.roll(pltpu.roll(v, PITCH - 1, 0), 40, 1)
        v3[x, :, 0:128] = jnp.where(lane < 84, before, here).astype(BF)
        v3[x, :, 128:256] = jnp.where(lane < 40, here, after).astype(BF)

    def mask_of(x, lo, size):
        return ext_ref[x, lo : lo + size].astype(F32)[:, 84:85]

    chunk = 5
    for c0 in range(0, n1, chunk):
        acc = None
        for a in range(3):
            d = dot(v3[c0 + a : c0 + a + chunk].reshape(chunk * PITCH, 256), w1_ref[a])
            acc = d if acc is None else acc + d
        acc = acc.reshape(chunk, PITCH, 256)
        for k in range(chunk):
            x = c0 + k
            g = gelu(acc[k]) * mask_of(x + 1, 0, PITCH)
            h3[x, :, 0:256] = pltpu.roll(g, 1, 0).astype(BF)
            h3[x, :, 256:512] = g.astype(BF)
            h3[x, :, 512:768] = pltpu.roll(g, PITCH - 1, 0).astype(BF)

    @pl.when(top)
    def _():
        acc = None
        for a in range(3):
            d = dot(v3[a : a + n1, 128:144, :].reshape(n1 * 16, 256), w1r_ref[a])
            acc = d if acc is None else acc + d
        acc = acc.reshape(n1, 16, 256)
        row = iota((16, 256), 0)
        for x in range(n1):
            g = gelu(acc[x]) * mask_of(x + 1, 128, 16)
            old = h3[x, 128:144, 256:512].astype(F32)
            new = jnp.where((row == 3) | (row == 4), g, old)
            h3[x, 128:144, 256:512] = new.astype(BF)
            old = h3[x, 128:144, 0:256].astype(F32)
            h3[x, 128:144, 0:256] = jnp.where((row == 4) | (row == 5), pltpu.roll(new, 1, 0), old).astype(BF)
            old = h3[x, 128:144, 512:768].astype(F32)
            h3[x, 128:144, 512:768] = jnp.where((row == 2) | (row == 3), pltpu.roll(new, 15, 0), old).astype(BF)

    chunk = 6
    for c0 in range(0, n2, chunk):
        acc = None
        for a in range(3):
            d = dot(h3[c0 + a : c0 + a + chunk].reshape(chunk * PITCH, 768), w2_ref[a])
            acc = d if acc is None else acc + d
        acc = acc.reshape(chunk, PITCH, 256)
        for k in range(chunk):
            x = c0 + k
            h2[x] = (gelu(acc[k]) * mask_of(x + 2, 0, PITCH)).astype(BF)

    @pl.when(top)
    def _():
        acc = None
        for a in range(3):
            for b in range(3):
                lhs = h3[a : a + n2, 128:144, 256 * b : 256 * b + 256].reshape(n2 * 16, 256)
                d = dot(lhs, w2_ref[2 - a, 256 * (2 - b) : 256 * (2 - b) + 256, :])
                acc = d if acc is None else acc + d
        acc = acc.reshape(n2, 16, 256)
        row = iota((16, 256), 0)
        for x in range(n2):
            g = gelu(acc[x]) * mask_of(x + 2, 128, 16)
            old = h2[x, 128:144].astype(F32)
            h2[x, 128:144] = jnp.where(row == 3, g, old).astype(BF)

    chunk = 4
    for c0 in range(0, n3, chunk):
        acc = None
        for a in range(3):
            d = dot(h2[c0 + a : c0 + a + chunk].reshape(chunk * PITCH, 256), w3_ref[a])
            acc = d if acc is None else acc + d
        acc = acc.reshape(chunk, PITCH, 384)
        for k in range(chunk):
            x = c0 + k
            change = (
                pltpu.roll(acc[k][:, 0:128], PITCH - 2, 0)
                + pltpu.roll(acc[k][:, 128:256], PITCH - 3, 0)
                + pltpu.roll(acc[k][:, 256:384], PITCH - 4, 0)
            )
            state = pltpu.roll(ext_ref[x + 3].astype(F32), PITCH - 3, 0)
            new = ((state + change) * state[:, 84:85])[:128]
            result[:, x, :] = new.T[:80]
    out_ref[...] = result[...][:76].astype(BF)


def convolutions(*args):
    return pl.pallas_call(
        conv_kernel,
        in_specs=[smem_spec()] + vmem_specs(len(args) - 1),
        out_specs=vmem_specs(1)[0],
        out_shape=jax.ShapeDtypeStruct((76, 16, 128), BF),
        scratch_shapes=[
            pltpu.VMEM((22, PITCH, 256), BF),
            pltpu.VMEM((20, PITCH, 768), BF),
            pltpu.VMEM((18, PITCH, 256), BF),
            pltpu.VMEM((80, 16, 128), F32),
        ],
        compiler_params=params(),
        cost_estimate=pl.CostEstimate(flops=8 * 10**9, bytes_accessed=8 * 10**6, transcendentals=0),
        name="convolutions",
    )(*args)


def shifted(forth, back, axis, periodic):
    count = lax.axis_size(axis)
    forward = [(i, i + 1) for i in range(count - 1)]
    if periodic:
        forward.append((count - 1, 0))
    backward = [(b, a) for a, b in forward]
    return lax.ppermute(forth, axis, forward), lax.ppermute(back, axis, backward)


def per_tile(x):
    return lax.all_to_all(x, "tile", split_axis=0, concat_axis=0, tiled=True)


def per_device(
    atm_state,
    surface,
    mlp_in,
    mlp_mid,
    mlp_out,
    mlp_flux,
    ocean_state,
    ocean_mask,
    fold_map,
    pair_tile,
    pair_block,
    pair_count,
    margin,
    conv_in,
    conv_mid,
    conv_out,
):
    lev_dev, fields_n, tile_cols = atm_state.shape
    groups = lax.axis_size("lev")
    tiles = lax.axis_size("tile")
    tile = lax.axis_index("tile")
    at_top = lax.axis_index("lev") == groups - 1
    per_col = tile_cols // groups
    rows_dev = lev_dev * SLAB
    hid = mlp_mid.shape[0]
    och, span_x, span_y = ocean_state.shape
    pairs, blk = margin.shape[0], margin.shape[1]
    s = fold_map[0] + 1
    seam, shift = (s - 1) // span_x, (s - 1) % span_x

    extra = jnp.pad(surface[None], ((0, lev_dev - 1), (0, SLAB - fields_n - 1), (0, 0)))
    packed = jnp.concatenate([atm_state, extra], axis=1).reshape(rows_dev, groups, per_col)
    z = lax.all_to_all(packed, "lev", split_axis=1, concat_axis=0, tiled=True).reshape(groups * rows_dev, per_col)

    state = jnp.concatenate(
        [
            ocean_state,
            jnp.zeros((8, span_x, span_y), BF),
            ocean_mask.astype(BF)[None],
            jnp.zeros((LANES - och - 9, span_x, span_y), BF),
        ],
        axis=0,
    ).transpose(1, 2, 0)
    ask = jnp.concatenate([pair_tile[0, 0], pair_block[0, 0], jnp.broadcast_to(pair_count[0], (4,))])
    ask = jnp.pad(ask.astype(BF), (0, LANES - 12))[None]
    strip = jnp.concatenate(
        [state[:, span_y - 3 :].reshape(3 * span_x, LANES), ask, jnp.zeros((15, LANES), BF)], axis=0
    )
    strips = per_tile(jnp.broadcast_to(strip[None], (tiles,) + strip.shape))
    asked = strips[:, 3 * span_x, :12].astype(I32)
    slot = jnp.arange(pairs, dtype=I32)[None, :]
    mine = (asked[:, 0:4] == tile) & (slot < asked[:, 8:12])
    code = jnp.where(mine, asked[:, 4:8], -1).reshape(tiles * pairs)

    def to_rows(w, extra):
        w = w.reshape(groups, lev_dev, fields_n, hid)
        extra = jnp.pad(extra.reshape(groups, 1, 1, hid), ((0, 0), (0, lev_dev - 1), (0, 0), (0, 0)))
        pad = jnp.zeros((groups, lev_dev, SLAB - fields_n - 1, hid), BF)
        return jnp.concatenate([w, extra, pad], axis=2).reshape(groups * rows_dev, hid)

    rows_atm = groups * lev_dev * fields_n
    w1 = to_rows(mlp_in[:rows_atm], mlp_in[rows_atm:]).T
    w3 = jnp.concatenate([to_rows(mlp_out.T, jnp.zeros((groups, hid), BF)), mlp_flux.T], axis=0)

    updated, send = column_model(code, z, w1, mlp_mid.T, w3, tiles)
    got = per_tile(send)

    back = lax.all_to_all(updated.reshape(groups, rows_dev, per_col), "lev", split_axis=0, concat_axis=0, tiled=True)
    atm_next = back.transpose(1, 0, 2).reshape(lev_dev, SLAB, tile_cols)[:, :fields_n]

    x_, k_ = jnp.arange(3 * span_x)[:, None] // 3, jnp.arange(3 * span_x)[:, None] % 3
    e_ = jnp.arange(6 * span_x)[None, :] // (3 * span_x)
    u_, r_ = (jnp.arange(6 * span_x)[None, :] // 3) % span_x, jnp.arange(6 * span_x)[None, :] % 3
    pick = ((u_ == span_x * e_ + shift - x_) & (r_ == 2 - k_)).astype(BF)
    both = jnp.concatenate(
        [
            lax.dynamic_index_in_dim(strips, jnp.mod(seam - tile - e, tiles), 0, keepdims=False)[: 3 * span_x]
            for e in range(2)
        ],
        axis=0,
    )
    folded = dot(pick, both).astype(BF).reshape(span_x, 3, LANES)
    south, north = shifted(state[:, span_y - 3 :], state[:, :3], "lev", False)
    north = jnp.where(at_top, folded, north)
    pad = jnp.zeros((span_x, PITCH - span_y - 6, LANES), BF)
    tall = jnp.concatenate([south, state, north, pad], axis=1)
    west, east = shifted(tall[span_x - 3 :], tall[:3], "tile", True)
    ext = jnp.concatenate([west, tall, east], axis=0)

    cw1 = jnp.pad(conv_in.reshape(3, 3 * (och + 8), -1), ((0, 0), (0, 256 - 3 * (och + 8)), (0, 0)))
    cw1r = conv_in[::-1, ::-1].reshape(3, 3 * (och + 8), -1)
    cw1r = jnp.pad(cw1r, ((0, 0), (0, 256 - 3 * (och + 8)), (0, 0)))
    ch = conv_mid.shape[2]
    cw2 = conv_mid.reshape(3, 3 * ch, ch)
    cw3 = jnp.pad(conv_out, ((0, 0), (0, 0), (0, 0), (0, 128 - och))).transpose(0, 2, 1, 3).reshape(3, ch, 384)

    scal = jnp.stack(
        [pair_tile[0, 0, p] for p in range(4)] + [pair_count[0, 0], tile, seam, shift, at_top.astype(I32)]
    ).astype(I32)
    flux, send = remap(scal, got, margin.reshape(pairs * blk * span_x, span_y))
    wide, up, down, fold = rim(scal, per_tile(send), flux)
    south, north = shifted(up, down, "lev", False)
    ocean_next = convolutions(scal, ext, wide, south, north, fold, cw1, cw1r, cw2, cw3)
    return (atm_next, ocean_next)


def solution(mesh):
    return jax.shard_map(
        per_device,
        mesh=mesh,
        in_specs=(
            P("lev", None, "tile"),
            P("lev", "tile"),
            P(),
            P(),
            P(),
            P(),
            P(None, "tile", "lev"),
            P("tile", "lev"),
            P(),
            P("tile", "lev", None),
            P("tile", "lev", None),
            P("tile", "lev"),
            P(None, None, "tile", "lev"),
            P(),
            P(),
            P(),
        ),
        out_specs=(P("lev", None, "tile"), P(None, "tile", "lev")),
        check_vma=False,
    )
```

time: 391 us -> 151 us (0.39); the launches traced: 384 us -> 150 us
  blocking collectives: 188 us -> 0 us
  matrix products: 69 us -> 0.2 us
  waiting for transfers between devices: 11.4 us -> 50 us
  Pallas kernels: 0 us -> 24 us
  starting transfers between devices: 61.9 us -> 49 us
  between operations: 15.8 us -> 4.34 us
  local copies, waits for them, and re-layouts: 29.2 us -> 18.3 us
  other arithmetic: 8.23 us -> 4.16 us
    all_gather x4 -> x0, blocking collectives: 188 us -> none  [extend(): every_top = lax.all_gather(top_rows, 'tile', axis=1, tiled=True)]
    dot_general x41 -> x1, matrix products: 69 us -> 0.2 us  [dot(): return jnp.dot(a, b, preferred_element_type=F32)]
    all_to_all x3 -> x5, waiting for transfers between devices: 4.35 us -> 46.1 us  [the longest x3 41.2 us: per_tile(): return lax.all_to_all(x, 'tile', split_axis=0, concat_axis=0, tiled=True)]
    ppermute x16 -> x6, starting transfers between devices: 46.2 us -> 13.2 us  [the longest x3 7.04 us: shifted(): lax.ppermute(forth, axis, forward)]
    pallas_call x0 -> x4, Pallas kernels: none -> 24 us  [the longest x1 11.8 us: convolutions(): pl.pallas_call(conv_kernel, in_specs=[smem_spec()] + vmem_specs(len(args)...]
    all_to_all x3 -> x5, starting transfers between devices: 15.7 us -> 35.7 us  [the longest x3 24.5 us: per_tile(): return lax.all_to_all(x, 'tile', split_axis=0, concat_axis=0, tiled=True)]
    gather x19 -> x0, local copies, waits for them, and re-layouts: 11.5 us -> none
    scatter x4 -> x0, local copies, waits for them, and re-layouts: 4.63 us -> none  [extend(): return padded.at[:, :, span_y + 1].set(upper_rim)]
  transfers between devices with their start and end apart: 20 -> 11, of which waited for: 5 -> 6; matrix products, arithmetic and copies ran while one was open for 14% -> 11% of each run, Pallas kernels for 0% -> 1%
where the time goes in v1:
time: 151 us; the launch traced here: 150 us
  waiting for transfers between devices  50 us (33%)
  starting transfers between devices  49 us (32%)
  Pallas kernels  24 us (16%)
  local copies, waits for them, and re-layouts  18.3 us (12%)
  between operations  4.34 us (3%)
  other arithmetic  4.16 us (3%)
    all_to_all x3, waiting for transfers between devices, per_tile(): return lax.all_to_all(x, 'tile', split_axis=0, concat_axis=0, tiled=True)  41.2 us
    all_to_all x3, starting transfers between devices, per_tile(): return lax.all_to_all(x, 'tile', split_axis=0, concat_axis=0, tiled=True)  24.5 us
    pallas_call x1, Pallas kernels, convolutions(): pl.pallas_call(conv_kernel, in_specs=[smem_spec()] + vmem_specs(len(args)...  11.8 us
    ppermute x3, starting transfers between devices, shifted(): lax.ppermute(forth, axis, forward)  7.04 us
    pallas_call x1, Pallas kernels, column_model(): pl.pallas_call(mlp_kernel, in_specs=[smem_spec()] + vmem_specs(4), out_sp...  6.69 us
    all_to_all x1, starting transfers between devices, per_device(): lax.all_to_all(updated.reshape(groups, rows_dev, per_col), 'lev', split_a...  6.39 us
    ppermute x3, starting transfers between devices, shifted(): lax.ppermute(back, axis, backward)  6.18 us
    all_to_all x1, waiting for transfers between devices, per_device(): lax.all_to_all(packed, 'lev', split_axis=1, concat_axis=0, tiled=True)  4.89 us
  transfers between devices with their start and end apart: 11, of which 6 were waited for; matrix products, arithmetic and copies ran while one was open for 11% of the time, Pallas kernels for 1%

profile of v1, /device:TPU:16, one launch (start us, length us, event | category | flops | bytes accessed | tf_op | source)
XLA Modules:
  0.0 150.0 jit_solution(15777265240022068477)
XLA Ops:
  2.3 1.4 copy.34
  4.6 1.2 broadcast_in_dim.51
  5.8 11.9 %all-to-all-start = ((bf16[64,64,128]{2,1,0:T(8,128)(2,1)}), bf16[64,64,128]{2,1,0:T(8,128)(2,1)S(1)}, u32[]{:S(2)}, u32[]{:S(2)}) async-start(bf16[64,64,128]{2,1,0:T(8,128)(2,1)} %broadcast_in_dim.51), calls=%async_computation | async-start | bytes 2097152 | tf_op jit(solution)/shard_map/all_to_all | solution.py:296
  18.3 1.0 copy.36
  19.5 0.8 copy.38
  20.3 1.0 copy.39
  21.9 24.0 %all-to-all-done = bf16[64,64,128]{2,1,0:T(8,128)(2,1)S(1)} async-done(((bf16[64,64,128]{2,1,0:T(8,128)(2,1)}), bf16[64,64,128]{2,1,0:T(8,128)(2,1)S(1)}, u32[]{:S(2)}, u32[]{:S(2)}) %all-to-all-start) | async-done | bytes 1048608 | tf_op jit(solution)/shard_map/all_to_all | solution.py:296
  45.9 4.8 %all-to-all-start.1 = ((bf16[24,4,2048]{2,0,1:T(8,128)(2,1)}), bf16[24,4,2048]{2,0,1:T(8,128)(2,1)S(1)}, u32[]{:S(2)}, u32[]{:S(2)}) async-start(bf16[24,4,2048]{2,0,1:T(8,128)(2,1)} %copy.36), calls=%async_computation.1 | async-start | bytes 786432 | tf_op jit(solution)/shard_map/all_to_all | solution.py:332
  51.5 4.9 %all-to-all-done.1 = bf16[24,4,2048]{2,0,1:T(8,128)(2,1)S(1)} async-done(((bf16[24,4,2048]{2,0,1:T(8,128)(2,1)}), bf16[24,4,2048]{2,0,1:T(8,128)(2,1)S(1)}, u32[]{:S(2)}, u32[]{:S(2)}) %all-to-all-start.1) | async-done | bytes 393248 | tf_op jit(solution)/shard_map/all_to_all | solution.py:332
  57.2 6.7 %column_model.1 = (bf16[96,2048]{1,0:T(8,128)(2,1)}, bf16[64,32,128]{2,1,0:T(8,128)(2,1)}) custom-call(s32[256]{0:T(256)} %reshape.176.code_ref, bf16[96,2048]{1,0:T(8,128)(2,1)} %bitcast.54, bf16[512,96]{1,0:T(8,128)(2,1)} %bitcast.57, bf16[512,512]{1,0:T(8,128)(2,1)} %bitcast.51, bf16[104,512]{1,0:T(8,128)(2,1)} %pad_maximum_fusion.7.w3_ref), custom_call_target="tpu_custom_call" | custom-call | flops 3000000000 | bytes 2000000 | tf_op jit(solution)/shard_map/column_model/pallas_call | solution.py:69
  63.9 6.1 %all-to-all-start.3 = ((bf16[64,32,128]{2,1,0:T(8,128)(2,1)}), bf16[64,32,128]{2,1,0:T(8,128)(2,1)S(1)}, u32[]{:S(2)}, u32[]{:S(2)}) async-start(bf16[64,32,128]{2,1,0:T(8,128)(2,1)} %get-tuple-element.11), calls=%async_computation.3 | async-start | bytes 1048576 | tf_op jit(solution)/shard_map/all_to_all | solution.py:296
  69.9 1.2 slice.73
  74.4 3.1 %stack.23.scal_ref = s32[9]{0:T(128)} concatenate(s32[1]{0:T(128)} %bitcast.20, s32[1]{0:T(128)} %bitcast.21, s32[1]{0:T(128)} %bitcast.22, s32[1]{0:T(128)} %bitcast.23, s32[1]{0:T(128)} %bitcast.48, s32[1]{0:T(128)} %bitcast.25, s32[1]{0:T(128)} %bitcast.27, s32[1]{0:T(128)} %bitcast.28, s32[1]{0:T(128)} %bitcast.29), dimensions={0} | concatenate | bytes 72 | tf_op jit(solution)/shard_map/stack | solution.py:396
  77.5 9.6 %all-to-all-done.3.got_ref = bf16[64,32,128]{2,1,0:T(8,128)(2,1)S(1)} async-done(((bf16[64,32,128]{2,1,0:T(8,128)(2,1)}), bf16[64,32,128]{2,1,0:T(8,128)(2,1)S(1)}, u32[]{:S(2)}, u32[]{:S(2)}) %all-to-all-start.3) | async-done | bytes 524320 | tf_op jit(solution)/shard_map/all_to_all | solution.py:296
  87.1 0.8 copy-done.3
  87.9 3.6 %remap.1 = (bf16[128,128]{1,0:T(8,128)(2,1)}, bf16[64,32,128]{2,1,0:T(8,128)(2,1)}) custom-call(s32[9]{0:T(128)} %stack.23.scal_ref, bf16[64,32,128]{2,1,0:T(8,128)(2,1)} %copy-done.3, bf16[8192,128]{1,0:T(8,128)(2,1)} %bitcast.61), custom_call_target="tpu_custom_call" | custom-call | flops 1000000000 | bytes 3000000 | tf_op jit(solution)/shard_map/remap/pallas_call | solution.py:115
  91.6 6.5 %all-to-all-start.4 = ((bf16[64,32,128]{2,1,0:T(8,128)(2,1)}), bf16[64,32,128]{2,1,0:T(8,128)(2,1)S(1)}, u32[]{:S(2)}, u32[]{:S(2)}) async-start(bf16[64,32,128]{2,1,0:T(8,128)(2,1)} %get-tuple-element.12), calls=%async_computation.4 | async-start | bytes 1048576 | tf_op jit(solution)/shard_map/all_to_all | solution.py:296
  98.1 4.0 %collective-permute-start = (bf16[16,3,128]{2,1,0:T(4,128)(2,1)S(1)}, bf16[16,3,128]{2,1,0:T(4,128)(2,1)S(1)}, u32[]{:S(2)}, u32[]{:S(2)}) collective-permute-start(bf16[16,3,128]{2,1,0:T(4,128)(2,1)S(1)} %get-tuple-element.23), channel_id=1, source_target_pairs={{0,64},{64,128},{128,192},{1,65},{65,129},{129,193},{2,66},{66,130... | collective-permute-start | bytes 36872 | tf_op jit(solution)/shard_map/ppermute | solution.py:292
  102.1 1.9 %collective-permute-start.1 = (bf16[16,3,128]{2,1,0:T(4,128)(2,1)S(1)}, bf16[16,3,128]{2,1,0:T(4,128)(2,1)S(1)}, u32[]{:S(2)}, u32[]{:S(2)}) collective-permute-start(bf16[16,3,128]{2,1,0:T(4,128)(2,1)S(1)} %get-tuple-element.22), channel_id=1, source_target_pairs={{64,0},{128,64},{192,128},{65,1},{129,65},{193,129},{66,2},{130,66... | collective-permute-start | bytes 36872 | tf_op jit(solution)/shard_map/ppermute | solution.py:292
  104.4 3.4 %collective-permute-done.1 = bf16[16,3,128]{2,1,0:T(4,128)(2,1)S(1)} collective-permute-done((bf16[16,3,128]{2,1,0:T(4,128)(2,1)S(1)}, bf16[16,3,128]{2,1,0:T(4,128)(2,1)S(1)}, u32[]{:S(2)}, u32[]{:S(2)}) %collective-permute-start.1) | collective-permute-done | bytes 12320 | tf_op jit(solution)/shard_map/ppermute | solution.py:292
  107.8 7.6 %all-to-all-done.4.got_ref = bf16[64,32,128]{2,1,0:T(8,128)(2,1)S(1)} async-done(((bf16[64,32,128]{2,1,0:T(8,128)(2,1)}), bf16[64,32,128]{2,1,0:T(8,128)(2,1)S(1)}, u32[]{:S(2)}, u32[]{:S(2)}) %all-to-all-start.4) | async-done | bytes 524320 | tf_op jit(solution)/shard_map/all_to_all | solution.py:296
  115.3 6.4 %all-to-all-start.2 = ((bf16[4,24,2048]{2,1,0:T(8,128)(2,1)}), bf16[4,24,2048]{2,1,0:T(8,128)(2,1)S(1)}, u32[]{:S(2)}, u32[]{:S(2)}) async-start(bf16[4,24,2048]{2,1,0:T(8,128)(2,1)} %bitcast.18), calls=%async_computation.2 | async-start | bytes 786432 | tf_op jit(solution)/shard_map/all_to_all | solution.py:367
  122.5 1.5 collective-permute-start.3
  124.1 0.8 pad.27.w1_ref
  124.9 0.8 pad.28.w1r_ref
  125.8 1.1 copy.41.w3_ref
  126.9 1.9 %rim.1 = (bf16[256,128]{1,0:T(8,128)(2,1)}, bf16[16,256]{1,0:T(8,128)(2,1)}, bf16[16,256]{1,0:T(8,128)(2,1)}, bf16[16,256]{1,0:T(8,128)(2,1)}) custom-call(s32[9]{0:T(128)} %stack.23.scal_ref, bf16[64,32,128]{2,1,0:T(8,128)(2,1)} %copy-done, bf16[128,128]{1,0:T(8,128)(2,1)} %get-tuple-element.13.flux_ref), custom_call_target="tpu_custom_call" | custom-call | flops 100000000 | bytes 1000000 | tf_op jit(solution)/shard_map/rim/pallas_call | solution.py:149
  128.7 3.1 %collective-permute-start.4 = (bf16[16,256]{1,0:T(8,128)(2,1)}, bf16[16,256]{1,0:T(8,128)(2,1)S(1)}, u32[]{:S(2)}, u32[]{:S(2)}) collective-permute-start(bf16[16,256]{1,0:T(8,128)(2,1)} %get-tuple-element.15), channel_id=1, source_target_pairs={{0,64},{64,128},{128,192},{1,65},{65,129},{129,193},{2,66},{66,130... | collective-permute-start | bytes 24584 | tf_op jit(solution)/shard_map/ppermute | solution.py:292
  131.8 2.8 %collective-permute-start.5 = (bf16[16,256]{1,0:T(8,128)(2,1)}, bf16[16,256]{1,0:T(8,128)(2,1)S(1)}, u32[]{:S(2)}, u32[]{:S(2)}) collective-permute-start(bf16[16,256]{1,0:T(8,128)(2,1)} %get-tuple-element.16), channel_id=1, source_target_pairs={{64,0},{128,64},{192,128},{65,1},{129,65},{193,129},{66,2},{130,66... | collective-permute-start | bytes 24584 | tf_op jit(solution)/shard_map/ppermute | solution.py:292
  134.6 1.1 pad_maximum_fusion.ext_ref
  136.0 1.0 reshape.185
  138.2 11.8 %convolutions.1 = bf16[76,16,128]{2,1,0:T(8,128)(2,1)} custom-call(s32[9]{0:T(128)} %stack.23.scal_ref, bf16[22,144,128]{2,1,0:T(8,128)(2,1)} %pad_maximum_fusion.ext_ref, bf16[256,128]{1,0:T(8,128)(2,1)} %get-tuple-element.14.wide_ref, bf16[16,256]{1,0:T(8,128)(2,1)} %copy-done.13, bf16[16,256]{1,0:T(8,128)(2,1)} %copy-done.14, ...), custom_call_target="tpu_custom_call" | custom-call | flops 8000000000 | bytes 8000000 | tf_op jit(solution)/shard_map/convolutions/pallas_call | solution.py:269
  (80 shorter events, 8.0 us)
Async XLA Ops:
  0.6 3.8 %copy-start.12 = (s32[1,1,4]{2,1,0:T(1,128)S(1)}, s32[1,1,4]{2,1,0:T(1,128)}, u32[]{:S(2)}) copy-start(s32[1,1,4]{2,1,0:T(1,128)} %param.26) | copy-start | bytes 52
  0.6 3.8 %copy-start.10 = (s32[1,1,4]{2,1,0:T(1,128)S(1)}, s32[1,1,4]{2,1,0:T(1,128)}, u32[]{:S(2)}) copy-start(s32[1,1,4]{2,1,0:T(1,128)} %param.25) | copy-start | bytes 52
  4.3 13.5 %copy-start.4 = (bf16[3,6,8192]{2,1,0:T(8,128)(2,1)S(1)}, bf16[3,6,8192]{2,1,0:T(8,128)(2,1)}, u32[]{:S(2)}) copy-start(bf16[3,6,8192]{2,1,0:T(8,128)(2,1)} %param.16) | copy-start | bytes 884740
  4.3 13.5 %copy-start.9 = (bf16[1,8192]{1,0:T(2,128)(2,1)S(1)}, bf16[1,8192]{1,0:T(2,128)(2,1)}, u32[]{:S(2)}) copy-start(bf16[1,8192]{1,0:T(2,128)(2,1)} %param.17) | copy-start | bytes 49156
  5.8 40.1 %all-to-all-start = ((bf16[64,64,128]{2,1,0:T(8,128)(2,1)}), bf16[64,64,128]{2,1,0:T(8,128)(2,1)S(1)}, u32[]{:S(2)}, u32[]{:S(2)}) async-start(bf16[64,64,128]{2,1,0:T(8,128)(2,1)} %broadcast_in_dim.51), calls=%async_computation | async-start | bytes 2097152 | tf_op jit(solution)/shard_map/all_to_all | solution.py:296
  17.7 1.5 copy-start.8
  17.8 1.5 %copy-start.7 = (bf16[76,512]{1,0:T(8,128)(2,1)S(1)}, bf16[76,512]{1,0:T(8,128)(2,1)}, u32[]{:S(2)}) copy-start(bf16[76,512]{1,0:T(8,128)(2,1)} %param.18) | copy-start | bytes 233476
  17.8 1.5 %slice-start = ((bf16[76,512]{1,0:T(8,128)(2,1)}), bf16[72,512]{1,0:T(8,128)(2,1)S(1)}, s32[]{:S(2)}) async-start(bf16[76,512]{1,0:T(8,128)(2,1)} %param.18), calls=%async_computation.5 | async-start | bytes 147456 | tf_op jit(solution)/shard_map/slice | solution.py:361
  17.8 2.5 %copy-start.2 = (bf16[512,512]{1,0:T(8,128)(2,1)S(1)}, bf16[512,512]{1,0:T(8,128)(2,1)}, u32[]{:S(2)}) copy-start(bf16[512,512]{1,0:T(8,128)(2,1)} %param.19) | copy-start | bytes 1572868
  18.3 3.0 %copy-start.11 = (bf16[512,8]{0,1:T(8,128)(2,1)S(1)}, bf16[512,8]{0,1:T(8,128)(2,1)}, u32[]{:S(2)}) copy-start(bf16[512,8]{0,1:T(8,128)(2,1)} %param.21) | copy-start | bytes 24580
  45.9 10.5 %all-to-all-start.1 = ((bf16[24,4,2048]{2,0,1:T(8,128)(2,1)}), bf16[24,4,2048]{2,0,1:T(8,128)(2,1)S(1)}, u32[]{:S(2)}, u32[]{:S(2)}) async-start(bf16[24,4,2048]{2,0,1:T(8,128)(2,1)} %copy.36), calls=%async_computation.1 | async-start | bytes 786432 | tf_op jit(solution)/shard_map/all_to_all | solution.py:332
  56.4 0.7 copy-start.5
  63.9 23.3 %all-to-all-start.3 = ((bf16[64,32,128]{2,1,0:T(8,128)(2,1)}), bf16[64,32,128]{2,1,0:T(8,128)(2,1)S(1)}, u32[]{:S(2)}, u32[]{:S(2)}) async-start(bf16[64,32,128]{2,1,0:T(8,128)(2,1)} %get-tuple-element.11), calls=%async_computation.3 | async-start | bytes 1048576 | tf_op jit(solution)/shard_map/all_to_all | solution.py:296
  87.1 0.8 copy-start.3
  91.6 32.4 %copy-start.1 = (bf16[3,3,84,256]{3,2,1,0:T(8,128)(2,1)S(1)}, bf16[3,3,84,256]{3,2,1,0:T(8,128)(2,1)}, u32[]{:S(2)}) copy-start(bf16[3,3,84,256]{3,2,1,0:T(8,128)(2,1)} %param.29) | copy-start | bytes 1161220
  91.6 23.7 %all-to-all-start.4 = ((bf16[64,32,128]{2,1,0:T(8,128)(2,1)}), bf16[64,32,128]{2,1,0:T(8,128)(2,1)S(1)}, u32[]{:S(2)}, u32[]{:S(2)}) async-start(bf16[64,32,128]{2,1,0:T(8,128)(2,1)} %get-tuple-element.12), calls=%async_computation.4 | async-start | bytes 1048576 | tf_op jit(solution)/shard_map/all_to_all | solution.py:296
  98.1 23.6 %collective-permute-start = (bf16[16,3,128]{2,1,0:T(4,128)(2,1)S(1)}, bf16[16,3,128]{2,1,0:T(4,128)(2,1)S(1)}, u32[]{:S(2)}, u32[]{:S(2)}) collective-permute-start(bf16[16,3,128]{2,1,0:T(4,128)(2,1)S(1)} %get-tuple-element.23), channel_id=1, source_target_pairs={{0,64},{64,128},{128,192},{1,65},{65,129},{129,193},{2,66},{66,130... | collective-permute-start | bytes 36872 | tf_op jit(solution)/shard_map/ppermute | solution.py:292
  102.1 5.6 %collective-permute-start.1 = (bf16[16,3,128]{2,1,0:T(4,128)(2,1)S(1)}, bf16[16,3,128]{2,1,0:T(4,128)(2,1)S(1)}, u32[]{:S(2)}, u32[]{:S(2)}) collective-permute-start(bf16[16,3,128]{2,1,0:T(4,128)(2,1)S(1)} %get-tuple-element.22), channel_id=1, source_target_pairs={{64,0},{128,64},{192,128},{65,1},{129,65},{193,129},{66,2},{130,66... | collective-permute-start | bytes 36872 | tf_op jit(solution)/shard_map/ppermute | solution.py:292
  115.3 8.8 %copy-start = (bf16[64,32,128]{2,1,0:T(8,128)(2,1)}, bf16[64,32,128]{2,1,0:T(8,128)(2,1)S(1)}, u32[]{:S(2)}) copy-start(bf16[64,32,128]{2,1,0:T(8,128)(2,1)S(1)} %all-to-all-done.4.got_ref) | copy-start | bytes 1572868
  115.3 20.4 %all-to-all-start.2 = ((bf16[4,24,2048]{2,1,0:T(8,128)(2,1)}), bf16[4,24,2048]{2,1,0:T(8,128)(2,1)S(1)}, u32[]{:S(2)}, u32[]{:S(2)}) async-start(bf16[4,24,2048]{2,1,0:T(8,128)(2,1)} %bitcast.18), calls=%async_computation.2 | async-start | bytes 786432 | tf_op jit(solution)/shard_map/all_to_all | solution.py:367
  122.5 12.1 %collective-permute-start.3 = (bf16[3,144,128]{2,1,0:T(8,128)(2,1)}, bf16[3,144,128]{2,1,0:T(8,128)(2,1)S(1)}, u32[]{:S(2)}, u32[]{:S(2)}) collective-permute-start(bf16[3,144,128]{2,1,0:T(8,128)(2,1)} %get-tuple-element.21), channel_id=1, source_target_pairs={{1,0},{2,1},{3,2},{4,3},{5,4},{6,5},{7,6},{8,7},{9,8},{10,9},{11,1... | collective-permute-start | bytes 331784 | tf_op jit(solution)/shard_map/ppermute | solution.py:292
  124.0 10.6 %collective-permute-start.2 = (bf16[3,144,128]{2,1,0:T(8,128)(2,1)}, bf16[3,144,128]{2,1,0:T(8,128)(2,1)S(1)}, u32[]{:S(2)}, u32[]{:S(2)}) collective-permute-start(bf16[3,144,128]{2,1,0:T(8,128)(2,1)} %get-tuple-element.20), channel_id=1, source_target_pairs={{0,1},{1,2},{2,3},{3,4},{4,5},{5,6},{6,7},{7,8},{8,9},{9,10},{10,1... | collective-permute-start | bytes 331784 | tf_op jit(solution)/shard_map/ppermute | solution.py:292
  124.1 1.7 %copy-start.6 = (bf16[3,3,256,76]{2,3,1,0:T(8,128)(2,1)S(1)}, bf16[3,3,256,76]{2,3,1,0:T(8,128)(2,1)}, u32[]{:S(2)}) copy-start(bf16[3,3,256,76]{2,3,1,0:T(8,128)(2,1)} %param.31) | copy-start | bytes 1050628
  128.7 8.3 %collective-permute-start.4 = (bf16[16,256]{1,0:T(8,128)(2,1)}, bf16[16,256]{1,0:T(8,128)(2,1)S(1)}, u32[]{:S(2)}, u32[]{:S(2)}) collective-permute-start(bf16[16,256]{1,0:T(8,128)(2,1)} %get-tuple-element.15), channel_id=1, source_target_pairs={{0,64},{64,128},{128,192},{1,65},{65,129},{129,193},{2,66},{66,130... | collective-permute-start | bytes 24584 | tf_op jit(solution)/shard_map/ppermute | solution.py:292
  131.8 5.8 %collective-permute-start.5 = (bf16[16,256]{1,0:T(8,128)(2,1)}, bf16[16,256]{1,0:T(8,128)(2,1)S(1)}, u32[]{:S(2)}, u32[]{:S(2)}) collective-permute-start(bf16[16,256]{1,0:T(8,128)(2,1)} %get-tuple-element.16), channel_id=1, source_target_pairs={{64,0},{128,64},{192,128},{65,1},{129,65},{193,129},{66,2},{130,66... | collective-permute-start | bytes 24584 | tf_op jit(solution)/shard_map/ppermute | solution.py:292
  137.0 0.6 copy-start.13
  137.6 0.6 copy-start.14

commit v2 on v1

v2 whole, which is shorter than its diff:
```python
import jax
import jax.numpy as jnp
from jax import lax
from jax.experimental import pallas as pl
from jax.experimental.pallas import tpu as pltpu
from jax.sharding import PartitionSpec as P

BF = jnp.bfloat16
F32 = jnp.float32
I32 = jnp.int32
SLAB = 8
HALO = 3
ZS, CS = 8, 2
PITCH = 144
LANES = 128
MIB = 1024 * 1024
C1 = 0.7978845608028654
C2 = C1 * 0.044715


def gelu(x):
    half = 0.5 * x
    return half * jnp.tanh(x * (C1 + C2 * (x * x))) + half


def dot(a, b):
    return jnp.dot(a, b, preferred_element_type=F32)


def dot_nt(a, b):
    return lax.dot_general(a, b, (((1,), (1,)), ((), ())), preferred_element_type=F32)


def iota(shape, dim):
    return lax.broadcasted_iota(I32, shape, dim)


def vmem_specs(n):
    return [pl.BlockSpec(memory_space=pltpu.VMEM)] * n


def hbm_specs(n):
    return [pl.BlockSpec(memory_space=pltpu.HBM)] * n


def in_hbm(*arrays):
    return [pltpu.with_memory_space_constraint(x, pltpu.HBM) for x in arrays]


def fetch(pairs, sems):
    copies = [pltpu.make_async_copy(a, b, sems.at[i]) for i, (a, b) in enumerate(pairs)]
    for copy in copies:
        copy.start()
    return copies


def smem_spec():
    return pl.BlockSpec(memory_space=pltpu.SMEM)


def params(mib):
    return pltpu.CompilerParams(vmem_limit_bytes=mib * MIB)


def place():
    tile = lax.axis_index("tile")
    return tile, lax.rem(tile // CS, ZS)


def collect_kernel(atm_ref, surface_ref, *refs):
    *out_refs, atm, surface, sems = refs
    levels, _, cols = atm_ref.shape
    parts = len(out_refs)
    size = cols // parts
    lev = lax.axis_index("lev")
    zero = jnp.zeros((1, size), F32)
    spans = [pl.ds(pl.multiple_of(lax.rem(lev + k, parts) * size, size), size) for k in range(parts)]
    order = (1, 2, 3, 0)
    copies = fetch([(surface_ref, surface)] + [(atm_ref.at[:, :, spans[k]], atm.at[k]) for k in order], sems)
    copies[0].wait()
    for i, k in enumerate(order):
        copies[1 + i].wait()
        rows = []
        for j in range(levels):
            extra = surface[:, spans[k]].astype(F32) if j == 0 else zero
            rows += [atm[k, j].astype(F32), extra, zero]
        out_refs[k][...] = jnp.concatenate(rows, axis=0).astype(BF)


def collect(atm, surface, parts):
    levels, _, cols = atm.shape
    return pl.pallas_call(
        collect_kernel,
        in_specs=hbm_specs(2),
        out_specs=vmem_specs(parts),
        out_shape=[jax.ShapeDtypeStruct((levels * SLAB, cols // parts), BF)] * parts,
        scratch_shapes=[
            pltpu.VMEM((parts, levels, 6, cols // parts), BF),
            pltpu.VMEM((1, cols), BF),
            pltpu.SemaphoreType.DMA((parts + 1,)),
        ],
        compiler_params=params(8),
        cost_estimate=pl.CostEstimate(flops=10**6, bytes_accessed=10**6, transcendentals=0),
        name="collect",
    )(*in_hbm(atm, surface))


def spread_kernel(*refs):
    back_refs, out_ref = refs[:-1], refs[-1]
    parts, size = len(back_refs), back_refs[0].shape[1]
    lev = lax.axis_index("lev")
    for k in range(parts):
        rows = back_refs[k][...].astype(F32)
        span = pl.ds(pl.multiple_of(lax.rem(lev + k, parts) * size, size), size)
        for j in range(out_ref.shape[0]):
            out_ref[j, :, span] = rows[SLAB * j : SLAB * j + 6].astype(BF)


def spread(back, levels):
    parts, size = len(back), back[0].shape[1]
    return pl.pallas_call(
        spread_kernel,
        in_specs=vmem_specs(parts),
        out_specs=vmem_specs(1)[0],
        out_shape=jax.ShapeDtypeStruct((levels, 6, parts * size), BF),
        compiler_params=params(8),
        cost_estimate=pl.CostEstimate(flops=10**6, bytes_accessed=10**6, transcendentals=0),
        name="spread",
    )(*back)


def asking_kernel(count_ref, tile_in, block_in, fold_in, out_ref, seam_ref, tile_ref, block_ref, fold_ref, sems):
    pairs = [(tile_in, tile_ref), (block_in, block_ref), (fold_in, fold_ref)]
    for copy in fetch(pairs, sems):
        copy.wait()
    seam_ref[0] = fold_ref[0]
    for p in range(4):
        seam_ref[1 + p] = tile_ref[0, 0, p]
    seam_ref[5] = count_ref[0, 0]
    rows, zs = [], []
    for p in range(4):
        source, block = tile_ref[0, 0, p], block_ref[0, 0, p]
        number = (source // (CS * ZS) * CS + lax.rem(source, CS)) * 16 + block
        z = jnp.where(p < count_ref[0, 0], lax.rem(source // CS, ZS), -1)
        rows.append(jnp.full((1, 128), number, I32))
        zs.append(jnp.full((1, 128), z, I32))
    out_ref[0] = jnp.concatenate(rows + zs + [jnp.zeros((8, 128), I32)], axis=0).astype(F32).astype(BF)


def asking(tile, block, count, fold_map):
    return pl.pallas_call(
        asking_kernel,
        in_specs=[smem_spec()] + hbm_specs(3),
        out_specs=vmem_specs(1) + [smem_spec()],
        out_shape=[jax.ShapeDtypeStruct((1, 16, 128), BF), jax.ShapeDtypeStruct((8,), I32)],
        scratch_shapes=[pltpu.SMEM(x.shape, I32) for x in (tile, block, fold_map)]
        + [pltpu.SemaphoreType.DMA((3,))],
        compiler_params=params(4),
        cost_estimate=pl.CostEstimate(flops=10**6, bytes_accessed=10**5, transcendentals=0),
        name="asking",
    )(count, *in_hbm(tile, block, fold_map))


def prepare_kernel(
    state_in, mask_in, win_in, wmid_in, wout_in, wflux_in, state_ref, w1_ref, w2_ref, w3_ref,
    state, mask_ref, win_ref, wmid_ref, wout_ref, wflux_ref, rows, sems,
):
    copies = fetch(
        [
            (state_in, state), (mask_in, mask_ref), (win_in, win_ref), (wmid_in, wmid_ref), (wout_in, wout_ref),
            (wflux_in, wflux_ref),
        ],
        sems,
    )
    channels, cols, size = state_in.shape
    copies[0].wait()
    copies[1].wait()
    rows[...] = state[...].reshape(channels * cols, size).astype(F32)
    for x in range(cols):
        part = rows[pl.ds(x, channels, stride=cols), :]
        mask = mask_ref[x : x + 1].astype(F32)
        part = jnp.concatenate(
            [part, jnp.zeros((84 - channels, size), F32), mask, jnp.zeros((LANES - 85, size), F32)], axis=0
        )
        state_ref[x] = part.T.astype(BF)
    for copy in copies[2:]:
        copy.wait()
    lev = lax.axis_index("lev")
    rows_all = w1_ref.shape[1]
    size = rows_all // 4

    def origin(shape):
        row = iota(shape, 0)
        group = (lev - row // size) & 3
        level, field = 3 * group + row % size // 8, row % 8
        return jnp.where((field < 6) & (row < rows_all), 6 * level + field, -1), group, row

    source, group, row = origin((rows_all, 76))
    source = jnp.where(row % size == 6, 72 + group, source)
    w1_ref[...] = dot((iota((rows_all, 76), 1) == source).astype(BF), win_ref[...]).T.astype(BF)
    source, group, row = origin((rows_all + 8, 72))
    w3 = dot((iota((rows_all + 8, 72), 1) == source).astype(BF), wout_ref[...])
    w3 = w3 + dot((iota((rows_all + 8, 8), 1) == iota((rows_all + 8, 8), 0) - rows_all).astype(BF), wflux_ref[...])
    w3_ref[...] = w3.astype(BF)
    w2_ref[...] = wmid_ref[...].T


def prepare(state, mask, *weights):
    channels, cols, size = state.shape
    hid = weights[1].shape[0]
    return pl.pallas_call(
        prepare_kernel,
        in_specs=hbm_specs(6),
        out_specs=vmem_specs(4),
        out_shape=[
            jax.ShapeDtypeStruct((cols, size, LANES), BF),
            jax.ShapeDtypeStruct((hid, 96), BF),
            jax.ShapeDtypeStruct((hid, hid), BF),
            jax.ShapeDtypeStruct((104, hid), BF),
        ],
        scratch_shapes=[pltpu.VMEM(state.shape, BF), pltpu.VMEM(mask.shape, I32)]
        + [pltpu.VMEM(w.shape, BF) for w in weights]
        + [pltpu.VMEM((channels * cols, size), F32), pltpu.SemaphoreType.DMA((6,))],
        compiler_params=params(12),
        cost_estimate=pl.CostEstimate(flops=10**9, bytes_accessed=10**6, transcendentals=0),
        name="prepare",
    )(*in_hbm(state, mask, *weights))


def mlp_kernel(z0_ref, z1_ref, z2_ref, z3_ref, w1_ref, w2_ref, w3_ref, state_ref, *out_refs):
    z_refs, up_refs, send_ref = (z0_ref, z1_ref, z2_ref, z3_ref), out_refs[:4], out_refs[4]
    size, cols = z0_ref.shape
    rows = 4 * size
    step = 512
    w1, w2, w3 = w1_ref[...], w2_ref[...], w3_ref[...]
    for c in range(0, cols, step):
        z = jnp.concatenate([ref[:, c : c + step].astype(F32) for ref in z_refs], axis=0)
        first = gelu(dot(w1, z.astype(BF))).astype(BF)
        second = gelu(dot(w2, first)).astype(BF)
        out = dot(w3, second)
        for k in range(4):
            span = slice(size * k, size * k + size)
            up = z[span] + out[span]
            if k == 1 or k == 3:
                rim = []
                for x in range(c // 128, (c + step) // 128):
                    tile = state_ref[x, 0:16] if k == 1 else state_ref[x, 112:128]
                    rim.append(tile.astype(F32)[:8] if k == 1 else tile.astype(F32)[8:])
                up = jnp.concatenate([up, jnp.concatenate(rim, axis=1)], axis=0)
            up_refs[k][:, c : c + step] = up.astype(BF)
        for k in range(0, step, 256):
            both = jnp.concatenate([out[rows : rows + 8, k : k + 128], out[rows : rows + 8, k + 128 : k + 256]], axis=0)
            send_ref[0, (c + k) // 256] = both.astype(BF)
    row, col = iota((48, 256), 0), iota((48, 256), 1)
    pick = (col == row // 3 * 16 + 13 + row % 3).astype(BF)
    strip = dot(pick, state_ref[:, 112:128].reshape(256, 128)).astype(BF)
    send_ref[0, 8:11] = strip.reshape(3, 16, 128)
    for j in range(1, send_ref.shape[0]):
        send_ref[j] = send_ref[0]


def column_model(pieces, w1, w2, w3, state):
    size, cols = pieces[0].shape
    return pl.pallas_call(
        mlp_kernel,
        in_specs=vmem_specs(8),
        out_specs=vmem_specs(5),
        out_shape=[
            jax.ShapeDtypeStruct((size, cols), BF),
            jax.ShapeDtypeStruct((size + 8, cols), BF),
            jax.ShapeDtypeStruct((size, cols), BF),
            jax.ShapeDtypeStruct((size + 8, cols), BF),
            jax.ShapeDtypeStruct((8, 11, 16, 128), BF),
        ],
        compiler_params=params(20),
        cost_estimate=pl.CostEstimate(flops=3 * 10**9, bytes_accessed=2 * 10**6, transcendentals=0),
        name="column_model",
    )(*pieces, w1, w2, w3, state)


def pack_kernel(seam_ref, near_ref, far_ref, got_ref, send_ref):
    tile, z_me = place()
    number, zs = [], []
    for m in range(ZS):
        ask = (near_ref if m < 4 else far_ref)[m % 4].astype(F32).astype(I32)
        for p in range(4):
            number.append(jnp.broadcast_to(ask[p : p + 1], (8, 128)))
            zs.append(jnp.broadcast_to(ask[4 + p : 5 + p], (8, 128)))
    number, zs = jnp.concatenate(number, axis=0), jnp.concatenate(zs, axis=0)
    wanted = jnp.where(zs == z_me, number * 8 + iota((256, 128), 0) % 8, -1)
    total = None
    for j in range(8):
        pick = (wanted == iota((256, 128), 1) + 128 * j).astype(BF)
        term = dot(pick, got_ref[j, 0:8].reshape(128, 128))
        total = term if total is None else total + term
    total = total.astype(BF).reshape(ZS, 2, 16, 128)
    for m in range(ZS):
        send_ref[z_me ^ m, 0:2] = total[m]
    key = (seam_ref[0] + HALO) // 16 - 1 + 128
    core = lax.rem(tile, CS)
    z_to = lax.rem(key - lax.rem(key - core, CS) - CS * z_me, CS * ZS) // CS
    source = lax.rem(key - (tile - CS * z_me + CS * z_to), 64)
    strip = got_ref[source // (CS * ZS) * CS + lax.rem(source, CS), 8:11]
    for z in range(ZS):
        send_ref[z, 2:5] = strip


def pack(seam, near, far, got):
    return pl.pallas_call(
        pack_kernel,
        in_specs=[smem_spec()] + vmem_specs(3),
        out_specs=vmem_specs(1)[0],
        out_shape=jax.ShapeDtypeStruct((ZS, 5, 16, 128), BF),
        compiler_params=params(8),
        cost_estimate=pl.CostEstimate(flops=10**8, bytes_accessed=10**6, transcendentals=0),
        name="pack",
    )(seam, near, far, got)


def tall(state_ref, south_ref, north_ref, x):
    size = south_ref.shape[0] - 8
    lanes = slice(LANES * x, LANES * x + LANES)
    south = jnp.where(lax.axis_index("lev") > 0, south_ref[:, lanes].astype(F32)[size:], 0.0)
    return jnp.concatenate([south, state_ref[x].astype(F32), north_ref[:, lanes].astype(F32)[size:]], axis=0)


def remap_kernel(
    seam_ref, got_ref, margin_ref, state_ref, south_ref, north_ref,
    flux_ref, east_ref, west_ref, top_ref, strip_ref,
):
    partner = lax.rem((seam_ref[0] + HALO) // 16 - 1 - lax.axis_index("tile") + 128, 64)
    strip = got_ref[lax.rem(partner // CS, ZS), 2:5]
    strip_ref[...] = strip
    for side_ref, x in ((east_ref, 13), (west_ref, 0)):
        for k in range(HALO):
            side_ref[PITCH * k : PITCH * k + PITCH] = tall(state_ref, south_ref, north_ref, x + k).astype(BF)
        side_ref[432:480] = strip.reshape(48, 128)
    count = seam_ref[5]
    pieces = []
    for p in range(4):
        source = jnp.clip(seam_ref[1 + p], 0, 63)
        piece = got_ref[lax.rem(source // CS, ZS), p // 2].astype(F32)[8 * (p % 2) : 8 * (p % 2) + 8]
        pieces.append(jnp.where(p < count, piece, 0.0))
    blocks = jnp.concatenate(pieces, axis=0).astype(BF)
    spread = (iota((128, 2048), 0) == iota((128, 2048), 1) // 16).astype(BF)
    wide = dot(blocks, spread)
    same = iota((16, 2048), 0) == iota((16, 2048), 1) % 16
    total = None
    for p in range(4):
        rows = jnp.broadcast_to(wide[8 * p : 8 * p + 8][None], (16, 8, 2048))
        rows = jnp.where(same[:, None, :], rows, 0.0).reshape(128, 2048)
        ones = jnp.where(same & (p < count), 1.0, 0.0)
        left = jnp.concatenate([rows, ones], axis=0).astype(BF)
        term = dot(left, margin_ref[2048 * p : 2048 * p + 2048])
        total = term if total is None else total + term
    numer = total[:128].reshape(16, 8, 128)
    flux = (numer / total[128:144][:, None, :]).reshape(128, 128).astype(BF)
    flux_ref[...] = flux
    wide = flux.astype(F32)
    zero = jnp.zeros((8, 128), F32)
    east_ref[480:512] = jnp.concatenate([wide[104:128], zero], axis=0).astype(BF)
    west_ref[480:512] = jnp.concatenate([wide[0:24], zero], axis=0).astype(BF)
    top = dot_nt((iota((8, 128), 1) == 127 - iota((8, 128), 0)).astype(BF), flux).astype(BF)
    top_ref[...] = jnp.broadcast_to(top[None], top_ref.shape)


def remap(seam, got, margin, state, south, north, tiles):
    side = jax.ShapeDtypeStruct((512, 128), BF)
    return pl.pallas_call(
        remap_kernel,
        in_specs=[smem_spec()] + vmem_specs(5),
        out_specs=vmem_specs(5),
        out_shape=[
            jax.ShapeDtypeStruct((128, 128), BF),
            side,
            side,
            jax.ShapeDtypeStruct((tiles, 8, 128), BF),
            jax.ShapeDtypeStruct((3, 16, 128), BF),
        ],
        compiler_params=params(16),
        cost_estimate=pl.CostEstimate(flops=10**9, bytes_accessed=3 * 10**6, transcendentals=0),
        name="remap",
    )(seam, got, margin, state, south, north)


def rim_kernel(low_ref, flux_ref, high_ref, wide_ref, up_ref, down_ref):
    low, high = low_ref[480:512].astype(F32)[:24], high_ref[480:512].astype(F32)[:24]
    wide = jnp.concatenate([low, flux_ref[...].astype(F32), high, jnp.zeros((80, 128), F32)], axis=0).astype(BF)
    wide_ref[...] = wide
    row, col = iota((16, 128), 0), iota((16, 128), 1)
    up_ref[...] = dot_nt(((col == 125 + row) & (row < 3)).astype(BF), wide).astype(BF)
    down_ref[...] = dot_nt(((col == row) & (row < 3)).astype(BF), wide).astype(BF)


def rim(low, flux, high):
    strip = jax.ShapeDtypeStruct((16, 256), BF)
    return pl.pallas_call(
        rim_kernel,
        in_specs=vmem_specs(3),
        out_specs=vmem_specs(3),
        out_shape=[jax.ShapeDtypeStruct((256, 128), BF), strip, strip],
        compiler_params=params(4),
        cost_estimate=pl.CostEstimate(flops=10**8, bytes_accessed=10**6, transcendentals=0),
        name="rim",
    )(low, flux, high)


def conv_kernel(
    seam_ref, state_ref, below_ref, above_ref, west_ref, east_ref, strip_ref, wide_ref, south_ref, north_ref, tops_ref,
    win_in, wmid_in, wout_in, out_ref,
    v3, h3, h2, result, masks, win_ref, w2_ref, wout_ref, w1_ref, w3_ref, sems,
):
    copies = fetch([(win_in, win_ref), (wmid_in, w2_ref), (wout_in, wout_ref)], sems)
    tiles = tops_ref.shape[0]
    tile = lax.axis_index("tile")
    top = lax.axis_index("lev") == lax.axis_size("lev") - 1
    n0, n1, n2, n3 = 22, 20, 18, 16
    seam = (seam_ref[0] + HALO) // 16
    shift = lax.rem(seam_ref[0] + HALO, 16)

    u, f = iota((128, 256), 0) // 8, iota((128, 256), 0) % 8
    i, g = iota((128, 256), 1) // 8, iota((128, 256), 1) % 8
    fold = None
    for e in range(3):
        pick = ((f == g) & (u == 16 * e + shift - i)).astype(BF)
        part = tops_ref[lax.rem(seam - tile - e + 2 * tiles, tiles)].astype(F32)
        term = dot(jnp.concatenate([part, jnp.zeros((8, 128), F32)], axis=0).astype(BF), pick)
        fold = term if fold is None else fold + term
    strips = jnp.concatenate(
        [west_ref[432:480], strip_ref[...].reshape(48, 128), east_ref[432:480]], axis=0
    )
    i, k = iota((352, 144), 0) // 16, iota((352, 144), 0) % 16 - 8
    e, u, r = iota((352, 144), 1) // 48, iota((352, 144), 1) % 48 // 3, iota((352, 144), 1) % 3
    folded = dot(((u == 16 * e + shift - i) & (r == 2 - k) & (k >= 0) & (k < 3)).astype(BF), strips)
    over = iota((16, LANES), 0)
    over = top & (over >= 8) & (over < 11)

    def state_of(x):
        if x < 3:
            v = west_ref[PITCH * x : PITCH * x + PITCH].astype(F32)
        elif x < 19:
            v = tall(state_ref, below_ref, above_ref, x - 3)
        else:
            v = east_ref[PITCH * (x - 19) : PITCH * (x - 19) + PITCH].astype(F32)
        return jnp.concatenate([v[:128], jnp.where(over, folded[16 * x : 16 * x + 16], v[128:])], axis=0)

    north = jnp.where(top, fold, north_ref[...].astype(F32))
    rims = jnp.concatenate([south_ref[...].astype(F32), north], axis=0).astype(BF)
    row, col = iota((PITCH, 128), 0), iota((PITCH, 128), 1)
    fluxes = dot_nt((row == col + 8).astype(BF), wide_ref[...])
    row, col = iota((PITCH, 32), 0), iota((PITCH, 32), 1)
    put = ((col < 3) & (row == col + 5)) | ((col >= 16) & (col < 19) & (row == col - 16 + 136))
    fluxes = fluxes + dot(put.astype(BF), rims)
    lane = iota((PITCH, LANES), 1)

    for x in range(n0):
        start = 8 * x
        part = fluxes[:, 128 * (start // 128) : 128 * (start // 128) + 128]
        part = pltpu.roll(part, (76 - start) % 128, 1)
        state = state_of(x)
        masks[x] = jnp.broadcast_to(state[:, 84:85], (PITCH, 128))
        v = jnp.where(lane < 76, state, jnp.where(lane < 84, part, 0.0))
        before = pltpu.roll(v, 1, 0)
        here = pltpu.roll(v, 84, 1)
        after = pltpu.roll(pltpu.roll(v, PITCH - 1, 0), 40, 1)
        v3[x, :, 0:128] = jnp.where(lane < 84, before, here).astype(BF)
        v3[x, :, 128:256] = jnp.where(lane < 40, here, after).astype(BF)

    def mask_of(x, lo, size):
        m = masks[x, lo : lo + size]
        return jnp.concatenate([m, m], axis=1)

    def first_weights(turn):
        for a in range(3):
            total = None
            for b in range(3):
                w = win_ref[2 - a, 2 - b] if turn else win_ref[a, b]
                term = dot((iota((256, 84), 0) == iota((256, 84), 1) + 84 * b).astype(BF), w)
                total = term if total is None else total + term
            w1_ref[a] = total.astype(BF)

    copies[0].wait()
    first_weights(False)
    chunk = 5
    for c0 in range(0, n1, chunk):
        acc = None
        for a in range(3):
            d = dot(v3[c0 + a : c0 + a + chunk].reshape(chunk * PITCH, 256), w1_ref[a])
            acc = d if acc is None else acc + d
        acc = acc.reshape(chunk, PITCH, 256)
        for k in range(chunk):
            x = c0 + k
            g = gelu(acc[k]) * mask_of(x + 1, 0, PITCH)
            h3[x, :, 0:256] = pltpu.roll(g, 1, 0).astype(BF)
            h3[x, :, 256:512] = g.astype(BF)
            h3[x, :, 512:768] = pltpu.roll(g, PITCH - 1, 0).astype(BF)

    @pl.when(top)
    def _():
        first_weights(True)
        acc = None
        for a in range(3):
            d = dot(v3[a : a + n1, 128:144, :].reshape(n1 * 16, 256), w1_ref[a])
            acc = d if acc is None else acc + d
        acc = acc.reshape(n1, 16, 256)
        row = iota((16, 256), 0)
        for x in range(n1):
            g = gelu(acc[x]) * mask_of(x + 1, 128, 16)
            old = h3[x, 128:144, 256:512].astype(F32)
            new = jnp.where((row == 8) | (row == 9), g, old)
            h3[x, 128:144, 256:512] = new.astype(BF)
            old = h3[x, 128:144, 0:256].astype(F32)
            h3[x, 128:144, 0:256] = jnp.where((row == 9) | (row == 10), pltpu.roll(new, 1, 0), old).astype(BF)
            old = h3[x, 128:144, 512:768].astype(F32)
            h3[x, 128:144, 512:768] = jnp.where((row == 7) | (row == 8), pltpu.roll(new, 15, 0), old).astype(BF)

    copies[1].wait()
    chunk = 6
    for c0 in range(0, n2, chunk):
        acc = None
        for a in range(3):
            d = dot(h3[c0 + a : c0 + a + chunk].reshape(chunk * PITCH, 768), w2_ref[a])
            acc = d if acc is None else acc + d
        acc = acc.reshape(chunk, PITCH, 256)
        for k in range(chunk):
            x = c0 + k
            h2[x] = (gelu(acc[k]) * mask_of(x + 2, 0, PITCH)).astype(BF)

    @pl.when(top)
    def _():
        acc = None
        for a in range(3):
            for b in range(3):
                lhs = h3[a : a + n2, 128:144, 256 * b : 256 * b + 256].reshape(n2 * 16, 256)
                d = dot(lhs, w2_ref[2 - a, 256 * (2 - b) : 256 * (2 - b) + 256, :])
                acc = d if acc is None else acc + d
        acc = acc.reshape(n2, 16, 256)
        row = iota((16, 256), 0)
        for x in range(n2):
            g = gelu(acc[x]) * mask_of(x + 2, 128, 16)
            old = h2[x, 128:144].astype(F32)
            h2[x, 128:144] = jnp.where(row == 8, g, old).astype(BF)

    copies[2].wait()
    for a in range(3):
        for b in range(3):
            w = wout_ref[a, b].astype(F32)
            w3_ref[a, 128 * b : 128 * b + 128] = jnp.concatenate([w, jnp.zeros((52, 256), F32)], axis=0).astype(BF)
    chunk = 4
    for c0 in range(0, n3, chunk):
        acc = None
        for a in range(3):
            d = dot_nt(h2[c0 + a : c0 + a + chunk].reshape(chunk * PITCH, 256), w3_ref[a])
            acc = d if acc is None else acc + d
        acc = acc.reshape(chunk, PITCH, 384)
        for k in range(chunk):
            x = c0 + k
            change = (
                pltpu.roll(acc[k][:, 0:128], 1, 0)
                + acc[k][:, 128:256]
                + pltpu.roll(acc[k][:, 256:384], PITCH - 1, 0)
            )[8:136]
            new = (state_ref[x].astype(F32) + change) * masks[x + 3, 8:136]
            result[:, x, :] = new.T[:80]
    out_ref[...] = result[...][:76].astype(BF)


def convolutions(*args):
    return pl.pallas_call(
        conv_kernel,
        in_specs=[smem_spec()] + vmem_specs(len(args) - 4) + hbm_specs(3),
        out_specs=vmem_specs(1)[0],
        out_shape=jax.ShapeDtypeStruct((76, 16, 128), BF),
        scratch_shapes=[
            pltpu.VMEM((22, PITCH, 256), BF),
            pltpu.VMEM((20, PITCH, 768), BF),
            pltpu.VMEM((18, PITCH, 256), BF),
            pltpu.VMEM((80, 16, 128), F32),
            pltpu.VMEM((22, PITCH, 128), F32),
        ]
        + [pltpu.VMEM(w.shape, BF) for w in args[-3:]]
        + [
            pltpu.VMEM((3, 256, 256), BF),
            pltpu.VMEM((3, 384, 256), BF),
            pltpu.SemaphoreType.DMA((3,)),
        ],
        compiler_params=params(32),
        cost_estimate=pl.CostEstimate(flops=8 * 10**9, bytes_accessed=8 * 10**6, transcendentals=0),
        name="convolutions",
    )(*args[:-3], *in_hbm(*args[-3:]))


def shifted(forth, back, axis, periodic):
    count = lax.axis_size(axis)
    forward = [(i, i + 1) for i in range(count - 1)]
    if periodic:
        forward.append((count - 1, 0))
    backward = [(b, a) for a, b in forward]
    return lax.ppermute(forth, axis, forward), lax.ppermute(back, axis, backward)


def turned(x, axis, by):
    count = lax.axis_size(axis)
    return lax.ppermute(x, axis, [(i, (i + by) % count) for i in range(count)])


def per_tile(x, groups=None):
    return lax.all_to_all(x, "tile", split_axis=0, concat_axis=0, tiled=True, axis_index_groups=groups)


def per_device(
    atm_state,
    surface,
    mlp_in,
    mlp_mid,
    mlp_out,
    mlp_flux,
    ocean_state,
    ocean_mask,
    fold_map,
    pair_tile,
    pair_block,
    pair_count,
    margin,
    conv_in,
    conv_mid,
    conv_out,
):
    lev_dev = atm_state.shape[0]
    groups = lax.axis_size("lev")
    tiles = lax.axis_size("tile")
    _, span_x, span_y = ocean_state.shape
    pairs, blk = margin.shape[0], margin.shape[1]
    along_z = [[(x * ZS + z) * CS + c for z in range(ZS)] for x in range(tiles // (ZS * CS)) for c in range(CS)]
    same_z = [[(x * ZS + z) * CS + c for x in range(tiles // (ZS * CS)) for c in range(CS)] for z in range(ZS)]

    pieces = collect(atm_state, surface, groups)
    *pieces, tile_of, state_in = lax.optimization_barrier((*pieces, pair_tile, ocean_state))
    pieces = [pieces[0]] + [turned(pieces[k], "lev", k) for k in range(1, groups)]

    def across(asks, bit):
        return lax.ppermute(asks, "tile", [(t, t ^ (CS * bit)) for t in range(tiles)])

    asks, seam = asking(tile_of, pair_block, pair_count, fold_map)
    asks = jnp.concatenate([asks, across(asks, 1)], axis=0)

    state, *weights = prepare(state_in, ocean_mask, mlp_in, mlp_mid, mlp_out.T, mlp_flux.T)

    state, asks = lax.optimization_barrier((state, asks))
    *updated, send = column_model(pieces, *weights, state)
    near = jnp.concatenate([asks, across(asks, 2)], axis=0)
    blocks = per_tile(send, same_z)
    got = per_tile(pack(seam, near, across(near, 4), blocks), along_z)

    back = [updated[0]] + [turned(updated[k], "lev", -k) for k in range(1, groups)]
    atm_next = spread(back, lev_dev)
    above, below = back[1], back[3]

    flux, last, first, top, partner = remap(
        seam, got, margin.reshape(pairs * blk * span_x, span_y), state, below, above, tiles
    )

    low, high = shifted(last, first, "tile", True)
    tops = per_tile(top)
    wide, up, down = rim(low, flux, high)
    south, north = shifted(up, down, "lev", False)
    ocean_next = convolutions(
        seam, state, below, above, low, high, partner, wide, south, north, tops,
        conv_in, conv_mid.reshape(3, 768, 256), conv_out.transpose(0, 1, 3, 2),
    )
    return (atm_next, ocean_next)


def solution(mesh):
    return jax.shard_map(
        per_device,
        mesh=mesh,
        in_specs=(
            P("lev", None, "tile"),
            P("lev", "tile"),
            P(),
            P(),
            P(),
            P(),
            P(None, "tile", "lev"),
            P("tile", "lev"),
            P(),
            P("tile", "lev", None),
            P("tile", "lev", None),
            P("tile", "lev"),
            P(None, None, "tile", "lev"),
            P(),
            P(),
            P(),
        ),
        out_specs=(P("lev", None, "tile"), P(None, "tile", "lev")),
        check_vma=False,
    )
```

time: 151 us -> 96.8 us (0.64)
  waiting for transfers between devices: 50 us -> 17.5 us
  local copies, waits for them, and re-layouts: 18.3 us -> 0.01 us
  other arithmetic: 4.16 us -> 0.01 us
  between operations: 4.34 us -> 1.53 us
  Pallas kernels: 24 us -> 26.1 us
  starting transfers between devices: 49 us -> 51.1 us
    all_to_all x5 -> x3, waiting for transfers between devices: 46.1 us -> 3.83 us  [per_tile(): lax.all_to_all(x, 'tile', split_axis=0, concat_axis=0, tiled=True, axis_i...]
    ppermute x0 -> x9, starting transfers between devices: none -> 20.6 us  [the longest x3 11.3 us: across(): return lax.ppermute(asks, 'tile', [(t, t ^ CS * bit) for t in range(tiles)])]
    all_to_all x5 -> x3, starting transfers between devices: 35.7 us -> 19 us  [per_tile(): lax.all_to_all(x, 'tile', split_axis=0, concat_axis=0, tiled=True, axis_i...]
    ppermute x0 -> x9, waiting for transfers between devices: none -> 10.5 us  [the longest x6 7.11 us: turned(): return lax.ppermute(x, axis, [(i, (i + by) % count) for i in range(count)])]
    reshape x14 -> x0, local copies, waits for them, and re-layouts: 5 us -> none  [the longest x2 1.25 us: per_device(): jnp.concatenate([atm_state, extra], axis=1)]
    unnamed x32 -> x3, local copies, waits for them, and re-layouts: 4.57 us -> 0.01 us
    another operation x2 -> x0, local copies, waits for them, and re-layouts: 3.1 us -> none  [the longest x1 3.09 us: per_device(): jnp.stack([pair_tile[0, 0, p] for p in range(4)] + [pair_count[0, 0], til...]
    ppermute x3 -> x2, starting transfers between devices: 7.04 us -> 4.55 us  [shifted(): lax.ppermute(forth, axis, forward)]
  transfers between devices with their start and end apart: 11 -> 16, of which waited for: 6 -> 9; matrix products, arithmetic and copies ran while one was open for 11% -> 0% of each run, Pallas kernels for 1% -> 3%
where the time goes in v2:
time: 96.8 us; the launch traced here: 96.3 us
  starting transfers between devices  51.1 us (53%)
  Pallas kernels  26.1 us (27%)
  waiting for transfers between devices  17.5 us (18%)
  between operations  1.53 us (2%)
    all_to_all x3, starting transfers between devices, per_tile(): lax.all_to_all(x, 'tile', split_axis=0, concat_axis=0, tiled=True, axis_i...  19 us
    pallas_call x1, Pallas kernels, convolutions(): pl.pallas_call(conv_kernel, in_specs=[smem_spec()] + vmem_specs(len(args)...  12.5 us
    ppermute x3, starting transfers between devices, across(): return lax.ppermute(asks, 'tile', [(t, t ^ CS * bit) for t in range(tiles)])  11.3 us
    ppermute x6, starting transfers between devices, turned(): return lax.ppermute(x, axis, [(i, (i + by) % count) for i in range(count)])  9.36 us
    ppermute x6, waiting for transfers between devices, turned(): return lax.ppermute(x, axis, [(i, (i + by) % count) for i in range(count)])  7.11 us
    ppermute x2, starting transfers between devices, shifted(): lax.ppermute(back, axis, backward)  6.93 us
    pallas_call x1, Pallas kernels, column_model(): pl.pallas_call(mlp_kernel, in_specs=vmem_specs(8), out_specs=vmem_specs(5...  4.67 us
    ppermute x2, starting transfers between devices, shifted(): lax.ppermute(forth, axis, forward)  4.55 us
  transfers between devices with their start and end apart: 16, of which 9 were waited for; matrix products, arithmetic and copies ran while one was open for 0% of the time, Pallas kernels for 3%

profile of v2, /device:TPU:16, one launch (start us, length us, event | category | flops | bytes accessed | tf_op | source)
XLA Modules:
  0.0 96.3 jit_solution(15089225904054779615)
XLA Ops:
  1.3 1.1 %collect.1 = (bf16[24,2048]{1,0:T(8,128)(2,1)S(1)}, bf16[24,2048]{1,0:T(8,128)(2,1)S(1)}, bf16[24,2048]{1,0:T(8,128)(2,1)S(1)}, bf16[24,2048]{1,0:T(8,128)(2,1)S(1)}) custom-call(bf16[3,6,8192]{2,1,0:T(8,128)(2,1)} %atm_ref.1, bf16[1,8192]{1,0:T(2,128)(2,1)} %surface_ref.1), custom_call_target="tpu_custom_call" | custom-call | flops 1000000 | bytes 1000000 | tf_op jit(solution)/shard_map/collect/pallas_call | solution.py:92
  2.4 1.4 %asking.1 = (bf16[1,16,128]{2,1,0:T(8,128)(2,1)S(1)}, s32[8]{0:T(128)S(1)}) custom-call(s32[1,1]{1,0:T(1,128)S(6)} %copy.19.count_ref, s32[1,1,4]{2,1,0:T(1,128)} %tile_in, s32[1,1,4]{2,1,0:T(1,128)} %block_in.1, s32[1024]{0:T(1024)} %fold_in.1), custom_call_target="tpu_custom_call" | custom-call | flops 1000000 | bytes 100000 | tf_op jit(solution)/shard_map/asking/pallas_call | solution.py:151
  3.8 2.0 %collective-permute-start.3 = (bf16[1,16,128]{2,1,0:T(8,128)(2,1)S(1)}, bf16[1,16,128]{2,1,0:T(8,128)(2,1)S(1)}, u32[]{:S(2)}, u32[]{:S(2)}) collective-permute-start(bf16[1,16,128]{2,1,0:T(8,128)(2,1)S(1)} %get-tuple-element.47), channel_id=1, source_target_pairs={{0,2},{1,3},{2,0},{3,1},{4,6},{5,7},{6,4},{7,5},{8,10},{9,11},{10,... | collective-permute-start | bytes 12296 | tf_op jit(solution)/shard_map/ppermute | solution.py:642
  5.8 1.3 %collective-permute-start = (bf16[24,2048]{1,0:T(8,128)(2,1)S(1)}, bf16[24,2048]{1,0:T(8,128)(2,1)S(1)}, u32[]{:S(2)}, u32[]{:S(2)}) collective-permute-start(bf16[24,2048]{1,0:T(8,128)(2,1)S(1)} %get-tuple-element.38), channel_id=1, source_target_pairs={{0,64},{64,128},{128,192},{192,0},{1,65},{65,129},{129,193},{193,1... | collective-permute-start | bytes 294920 | tf_op jit(solution)/shard_map/ppermute | solution.py:604
  7.1 0.6 collective-permute-start.1
  7.7 1.1 %collective-permute-start.2 = (bf16[24,2048]{1,0:T(8,128)(2,1)S(1)}, bf16[24,2048]{1,0:T(8,128)(2,1)S(1)}, u32[]{:S(2)}, u32[]{:S(2)}) collective-permute-start(bf16[24,2048]{1,0:T(8,128)(2,1)S(1)} %get-tuple-element.40), channel_id=1, source_target_pairs={{0,192},{64,0},{128,64},{192,128},{1,193},{65,1},{129,65},{193,129... | collective-permute-start | bytes 294920 | tf_op jit(solution)/shard_map/ppermute | solution.py:604
  8.8 1.7 %prepare.1 = (bf16[16,128,128]{2,1,0:T(8,128)(2,1)S(1)}, bf16[512,96]{1,0:T(8,128)(2,1)S(1)}, bf16[512,512]{1,0:T(8,128)(2,1)S(1)}, bf16[104,512]{1,0:T(8,128)(2,1)S(1)}) custom-call(bf16[76,16,128]{2,1,0:T(8,128)(2,1)} %state_in, s32[16,128]{1,0:T(8,128)} %mask_in.1, bf16[76,512]{1,0:T(8,128)(2,1)} %win_in.2, bf16[512,512]{1,0:T(8,128)(2,1)} %wmid_in.1, ...), custom_call_target="tpu_custom_call" | custom-call | flops 1000000000 | bytes 1000000 | tf_op jit(solution)/shard_map/prepare/pallas_call | solution.py:211
  10.5 2.7 %collective-permute-done.1.z2_ref = bf16[24,2048]{1,0:T(8,128)(2,1)S(1)} collective-permute-done((bf16[24,2048]{1,0:T(8,128)(2,1)S(1)}, bf16[24,2048]{1,0:T(8,128)(2,1)S(1)}, u32[]{:S(2)}, u32[]{:S(2)}) %collective-permute-start.1) | collective-permute-done | bytes 98336 | tf_op jit(solution)/shard_map/ppermute | solution.py:604
  13.2 0.8 collective-permute-done.2.z3_ref
  14.0 4.7 %column_model.1 = (bf16[24,2048]{1,0:T(8,128)(2,1)S(1)}, bf16[32,2048]{1,0:T(8,128)(2,1)S(1)}, bf16[24,2048]{1,0:T(8,128)(2,1)S(1)}, bf16[32,2048]{1,0:T(8,128)(2,1)S(1)}, bf16[8,11,16,128]{3,2,1,0:T(8,128)(2,1)}) custom-call(bf16[24,2048]{1,0:T(8,128)(2,1)S(1)} %get-tuple-element.37.z0_ref, bf16[24,2048]{1,0:T(8,128)(2,1)S(1)} %collective-permute-done.z1_ref, ...), custom_call_target="tpu_custom_call" | custom-call | flops 3000000000 | bytes 2000000 | tf_op jit(solution)/shard_map/column_model/pallas_call | solution.py:264
  18.7 4.3 %all-to-all-start = ((bf16[8,11,16,128]{3,2,1,0:T(8,128)(2,1)}), bf16[8,11,16,128]{3,2,1,0:T(8,128)(2,1)S(1)}, u32[]{:S(2)}, u32[]{:S(2)}) async-start(bf16[8,11,16,128]{3,2,1,0:T(8,128)(2,1)} %get-tuple-element.55), calls=%async_computation | async-start | bytes 720896 | tf_op jit(solution)/shard_map/all_to_all | solution.py:608
  23.0 3.3 %collective-permute-start.7 = (bf16[2,16,128]{2,1,0:T(8,128)(2,1)S(1)}, bf16[2,16,128]{2,1,0:T(8,128)(2,1)S(1)}, u32[]{:S(2)}, u32[]{:S(2)}) collective-permute-start(bf16[2,16,128]{2,1,0:T(8,128)(2,1)S(1)} %pad_maximum_fusion), channel_id=1, source_target_pairs={{0,4},{1,5},{2,6},{3,7},{4,0},{5,1},{6,2},{7,3},{8,12},{9,13},{10,... | collective-permute-start | bytes 24584 | tf_op jit(solution)/shard_map/ppermute | solution.py:642
  26.3 1.6 %collective-permute-done.7 = bf16[2,16,128]{2,1,0:T(8,128)(2,1)S(1)} collective-permute-done((bf16[2,16,128]{2,1,0:T(8,128)(2,1)S(1)}, bf16[2,16,128]{2,1,0:T(8,128)(2,1)S(1)}, u32[]{:S(2)}, u32[]{:S(2)}) %collective-permute-start.7) | collective-permute-done | bytes 8224 | tf_op jit(solution)/shard_map/ppermute | solution.py:642
  27.9 6.0 %collective-permute-start.8 = (bf16[4,16,128]{2,1,0:T(8,128)(2,1)S(1)}, bf16[4,16,128]{2,1,0:T(8,128)(2,1)S(1)}, u32[]{:S(2)}, u32[]{:S(2)}) collective-permute-start(bf16[4,16,128]{2,1,0:T(8,128)(2,1)S(1)} %constant_dynamic-update-slice_fusion.near_ref), channel_id=1, source_target_pairs={{0,8},{1,9},{2,10},{3,11},{4,12},{5,13},{6,14},{7,15},{8,0},{9,1},... | collective-permute-start | bytes 49160 | tf_op jit(solution)/shard_map/ppermute | solution.py:642
  33.9 1.7 %collective-permute-done.8.far_ref = bf16[4,16,128]{2,1,0:T(8,128)(2,1)S(1)} collective-permute-done((bf16[4,16,128]{2,1,0:T(8,128)(2,1)S(1)}, bf16[4,16,128]{2,1,0:T(8,128)(2,1)S(1)}, u32[]{:S(2)}, u32[]{:S(2)}) %collective-permute-start.8) | collective-permute-done | bytes 16416 | tf_op jit(solution)/shard_map/ppermute | solution.py:642
  35.6 1.5 %pack.1 = bf16[8,5,16,128]{3,2,1,0:T(8,128)(2,1)} custom-call(s32[8]{0:T(128)S(1)} %get-tuple-element.53.seam_ref, bf16[4,16,128]{2,1,0:T(8,128)(2,1)S(1)} %constant_dynamic-update-slice_fusion.near_ref, bf16[4,16,128]{2,1,0:T(8,128)(2,1)S(1)} %collective-permute-done.8.far_ref, bf16[8,11,16,128]{3,2,1,0:T(8,128)(2,1)S(1)} %all-to-all-done.got_ref), custom_call_target="tpu_custom_call" | custom-call | flops 100000000 | bytes 1000000 | tf_op jit(solution)/shard_map/pack/pallas_call | solution.py:309
  37.2 7.3 %all-to-all-start.1 = ((bf16[8,5,16,128]{3,2,1,0:T(8,128)(2,1)}), bf16[8,5,16,128]{3,2,1,0:T(8,128)(2,1)S(1)}, u32[]{:S(2)}, u32[]{:S(2)}) async-start(bf16[8,5,16,128]{3,2,1,0:T(8,128)(2,1)} %pack.1), calls=%async_computation.1 | async-start | bytes 327680 | tf_op jit(solution)/shard_map/all_to_all | solution.py:608
  44.5 0.6 collective-permute-start.4
  45.1 1.4 %collective-permute-start.6 = (bf16[32,2048]{1,0:T(8,128)(2,1)S(1)}, bf16[32,2048]{1,0:T(8,128)(2,1)S(1)}, u32[]{:S(2)}, u32[]{:S(2)}) collective-permute-start(bf16[32,2048]{1,0:T(8,128)(2,1)S(1)} %get-tuple-element.52), channel_id=1, source_target_pairs={{0,64},{64,128},{128,192},{192,0},{1,65},{65,129},{129,193},{193,1... | collective-permute-start | bytes 393224 | tf_op jit(solution)/shard_map/ppermute | solution.py:604
  46.5 2.9 %collective-permute-done.4.refs_1_.north_ref.above_ref = bf16[32,2048]{1,0:T(8,128)(2,1)S(1)} collective-permute-done((bf16[32,2048]{1,0:T(8,128)(2,1)S(1)}, bf16[32,2048]{1,0:T(8,128)(2,1)S(1)}, u32[]{:S(2)}, u32[]{:S(2)}) %collective-permute-start.4) | collective-permute-done | bytes 131104 | tf_op jit(solution)/shard_map/ppermute | solution.py:604
  49.4 0.6 collective-permute-done.6.refs_3_.south_ref.below_ref
  50.1 3.8 %all-to-all-done.1.got_ref = bf16[8,5,16,128]{3,2,1,0:T(8,128)(2,1)S(1)} async-done(((bf16[8,5,16,128]{3,2,1,0:T(8,128)(2,1)}), bf16[8,5,16,128]{3,2,1,0:T(8,128)(2,1)S(1)}, u32[]{:S(2)}, u32[]{:S(2)}) %all-to-all-start.1) | async-done | bytes 163872 | tf_op jit(solution)/shard_map/all_to_all | solution.py:608
  53.9 2.3 %remap.1 = (bf16[128,128]{1,0:T(8,128)(2,1)S(1)}, bf16[512,128]{1,0:T(8,128)(2,1)S(1)}, bf16[512,128]{1,0:T(8,128)(2,1)S(1)}, bf16[64,8,128]{2,1,0:T(8,128)(2,1)}, bf16[3,16,128]{2,1,0:T(8,128)(2,1)S(1)}) custom-call(s32[8]{0:T(128)S(1)} %get-tuple-element.53.seam_ref, bf16[8,5,16,128]{3,2,1,0:T(8,128)(2,1)S(1)} %all-to-all-done.1.got_ref, ...), custom_call_target="tpu_custom_call" | custom-call | flops 1000000000 | bytes 3000000 | tf_op jit(solution)/shard_map/remap/pallas_call | solution.py:369
  56.2 7.4 %all-to-all-start.2 = ((bf16[64,8,128]{2,1,0:T(8,128)(2,1)}), bf16[64,8,128]{2,1,0:T(8,128)(2,1)S(1)}, u32[]{:S(2)}, u32[]{:S(2)}) async-start(bf16[64,8,128]{2,1,0:T(8,128)(2,1)} %get-tuple-element.63), calls=%async_computation.2 | async-start | bytes 262144 | tf_op jit(solution)/shard_map/all_to_all | solution.py:608
  63.9 5.0 %collective-permute-start.10 = (bf16[512,128]{1,0:T(8,128)(2,1)S(1)}, bf16[512,128]{1,0:T(8,128)(2,1)S(1)}, u32[]{:S(2)}, u32[]{:S(2)}) collective-permute-start(bf16[512,128]{1,0:T(8,128)(2,1)S(1)} %get-tuple-element.57), channel_id=1, source_target_pairs={{1,0},{2,1},{3,2},{4,3},{5,4},{6,5},{7,6},{8,7},{9,8},{10,9},{11,1... | collective-permute-start | bytes 393224 | tf_op jit(solution)/shard_map/ppermute | solution.py:599
  68.9 4.4 %collective-permute-start.5 = (bf16[24,2048]{1,0:T(8,128)(2,1)S(1)}, bf16[24,2048]{1,0:T(8,128)(2,1)S(1)}, u32[]{:S(2)}, u32[]{:S(2)}) collective-permute-start(bf16[24,2048]{1,0:T(8,128)(2,1)S(1)} %get-tuple-element.51), channel_id=1, source_target_pairs={{0,128},{64,192},{128,0},{192,64},{1,129},{65,193},{129,1},{193,65... | collective-permute-start | bytes 294920 | tf_op jit(solution)/shard_map/ppermute | solution.py:604
  73.3 0.4 collective-permute-done.9.low_ref.west_ref
  73.8 4.2 %collective-permute-start.11 = (bf16[16,256]{1,0:T(8,128)(2,1)S(1)}, bf16[16,256]{1,0:T(8,128)(2,1)S(1)}, u32[]{:S(2)}, u32[]{:S(2)}) collective-permute-start(bf16[16,256]{1,0:T(8,128)(2,1)S(1)} %get-tuple-element.61), channel_id=1, source_target_pairs={{0,64},{64,128},{128,192},{1,65},{65,129},{129,193},{2,66},{66,130... | collective-permute-start | bytes 24584 | tf_op jit(solution)/shard_map/ppermute | solution.py:599
  78.1 1.9 %collective-permute-start.12 = (bf16[16,256]{1,0:T(8,128)(2,1)S(1)}, bf16[16,256]{1,0:T(8,128)(2,1)S(1)}, u32[]{:S(2)}, u32[]{:S(2)}) collective-permute-start(bf16[16,256]{1,0:T(8,128)(2,1)S(1)} %get-tuple-element.62), channel_id=1, source_target_pairs={{64,0},{128,64},{192,128},{65,1},{129,65},{193,129},{66,2},{130,66... | collective-permute-start | bytes 24584 | tf_op jit(solution)/shard_map/ppermute | solution.py:599
  80.0 0.8 spread.1
  80.8 2.8 %collective-permute-done.12.north_ref = bf16[16,256]{1,0:T(8,128)(2,1)S(1)} collective-permute-done((bf16[16,256]{1,0:T(8,128)(2,1)S(1)}, bf16[16,256]{1,0:T(8,128)(2,1)S(1)}, u32[]{:S(2)}, u32[]{:S(2)}) %collective-permute-start.12) | collective-permute-done | bytes 8224 | tf_op jit(solution)/shard_map/ppermute | solution.py:599
  83.6 12.5 %convolutions.1 = bf16[76,16,128]{2,1,0:T(8,128)(2,1)} custom-call(s32[8]{0:T(128)S(1)} %get-tuple-element.53.seam_ref, bf16[16,128,128]{2,1,0:T(8,128)(2,1)S(1)} %get-tuple-element.48.state_ref, bf16[32,2048]{1,0:T(8,128)(2,1)S(1)} %collective-permute-done.6.refs_3_.south_ref.below_ref, ...), custom_call_target="tpu_custom_call" | custom-call | flops 8000000000 | bytes 8000000 | tf_op jit(solution)/shard_map/convolutions/pallas_call | solution.py:569
  (14 shorter events, 0.5 us)
Async XLA Ops:
  3.8 6.6 %collective-permute-start.3 = (bf16[1,16,128]{2,1,0:T(8,128)(2,1)S(1)}, bf16[1,16,128]{2,1,0:T(8,128)(2,1)S(1)}, u32[]{:S(2)}, u32[]{:S(2)}) collective-permute-start(bf16[1,16,128]{2,1,0:T(8,128)(2,1)S(1)} %get-tuple-element.47), channel_id=1, source_target_pairs={{0,2},{1,3},{2,0},{3,1},{4,6},{5,7},{6,4},{7,5},{8,10},{9,11},{10,... | collective-permute-start | bytes 12296 | tf_op jit(solution)/shard_map/ppermute | solution.py:642
  5.8 4.7 %collective-permute-start = (bf16[24,2048]{1,0:T(8,128)(2,1)S(1)}, bf16[24,2048]{1,0:T(8,128)(2,1)S(1)}, u32[]{:S(2)}, u32[]{:S(2)}) collective-permute-start(bf16[24,2048]{1,0:T(8,128)(2,1)S(1)} %get-tuple-element.38), channel_id=1, source_target_pairs={{0,64},{64,128},{128,192},{192,0},{1,65},{65,129},{129,193},{193,1... | collective-permute-start | bytes 294920 | tf_op jit(solution)/shard_map/ppermute | solution.py:604
  7.1 6.1 %collective-permute-start.1 = (bf16[24,2048]{1,0:T(8,128)(2,1)S(1)}, bf16[24,2048]{1,0:T(8,128)(2,1)S(1)}, u32[]{:S(2)}, u32[]{:S(2)}) collective-permute-start(bf16[24,2048]{1,0:T(8,128)(2,1)S(1)} %get-tuple-element.39), channel_id=1, source_target_pairs={{0,128},{64,192},{128,0},{192,64},{1,129},{65,193},{129,1},{193,65... | collective-permute-start | bytes 294920 | tf_op jit(solution)/shard_map/ppermute | solution.py:604
  7.7 6.3 %collective-permute-start.2 = (bf16[24,2048]{1,0:T(8,128)(2,1)S(1)}, bf16[24,2048]{1,0:T(8,128)(2,1)S(1)}, u32[]{:S(2)}, u32[]{:S(2)}) collective-permute-start(bf16[24,2048]{1,0:T(8,128)(2,1)S(1)} %get-tuple-element.40), channel_id=1, source_target_pairs={{0,192},{64,0},{128,64},{192,128},{1,193},{65,1},{129,65},{193,129... | collective-permute-start | bytes 294920 | tf_op jit(solution)/shard_map/ppermute | solution.py:604
  14.0 39.9 %copy-start = (bf16[4,128,16,128]{3,2,1,0:T(8,128)(2,1)S(1)}, bf16[4,128,16,128]{3,2,1,0:T(8,128)(2,1)}, u32[]{:S(2)}) copy-start(bf16[4,128,16,128]{3,2,1,0:T(8,128)(2,1)} %param.28) | copy-start | bytes 6291460
  18.7 16.9 %all-to-all-start = ((bf16[8,11,16,128]{3,2,1,0:T(8,128)(2,1)}), bf16[8,11,16,128]{3,2,1,0:T(8,128)(2,1)S(1)}, u32[]{:S(2)}, u32[]{:S(2)}) async-start(bf16[8,11,16,128]{3,2,1,0:T(8,128)(2,1)} %get-tuple-element.55), calls=%async_computation | async-start | bytes 720896 | tf_op jit(solution)/shard_map/all_to_all | solution.py:608
  23.0 4.9 %collective-permute-start.7 = (bf16[2,16,128]{2,1,0:T(8,128)(2,1)S(1)}, bf16[2,16,128]{2,1,0:T(8,128)(2,1)S(1)}, u32[]{:S(2)}, u32[]{:S(2)}) collective-permute-start(bf16[2,16,128]{2,1,0:T(8,128)(2,1)S(1)} %pad_maximum_fusion), channel_id=1, source_target_pairs={{0,4},{1,5},{2,6},{3,7},{4,0},{5,1},{6,2},{7,3},{8,12},{9,13},{10,... | collective-permute-start | bytes 24584 | tf_op jit(solution)/shard_map/ppermute | solution.py:642
  27.9 7.7 %collective-permute-start.8 = (bf16[4,16,128]{2,1,0:T(8,128)(2,1)S(1)}, bf16[4,16,128]{2,1,0:T(8,128)(2,1)S(1)}, u32[]{:S(2)}, u32[]{:S(2)}) collective-permute-start(bf16[4,16,128]{2,1,0:T(8,128)(2,1)S(1)} %constant_dynamic-update-slice_fusion.near_ref), channel_id=1, source_target_pairs={{0,8},{1,9},{2,10},{3,11},{4,12},{5,13},{6,14},{7,15},{8,0},{9,1},... | collective-permute-start | bytes 49160 | tf_op jit(solution)/shard_map/ppermute | solution.py:642
  37.2 16.7 %all-to-all-start.1 = ((bf16[8,5,16,128]{3,2,1,0:T(8,128)(2,1)}), bf16[8,5,16,128]{3,2,1,0:T(8,128)(2,1)S(1)}, u32[]{:S(2)}, u32[]{:S(2)}) async-start(bf16[8,5,16,128]{3,2,1,0:T(8,128)(2,1)} %pack.1), calls=%async_computation.1 | async-start | bytes 327680 | tf_op jit(solution)/shard_map/all_to_all | solution.py:608
  44.5 5.0 %collective-permute-start.4 = (bf16[32,2048]{1,0:T(8,128)(2,1)S(1)}, bf16[32,2048]{1,0:T(8,128)(2,1)S(1)}, u32[]{:S(2)}, u32[]{:S(2)}) collective-permute-start(bf16[32,2048]{1,0:T(8,128)(2,1)S(1)} %get-tuple-element.50), channel_id=1, source_target_pairs={{0,192},{64,0},{128,64},{192,128},{1,193},{65,1},{129,65},{193,129... | collective-permute-start | bytes 393224 | tf_op jit(solution)/shard_map/ppermute | solution.py:604
  45.1 5.0 %collective-permute-start.6 = (bf16[32,2048]{1,0:T(8,128)(2,1)S(1)}, bf16[32,2048]{1,0:T(8,128)(2,1)S(1)}, u32[]{:S(2)}, u32[]{:S(2)}) collective-permute-start(bf16[32,2048]{1,0:T(8,128)(2,1)S(1)} %get-tuple-element.52), channel_id=1, source_target_pairs={{0,64},{64,128},{128,192},{192,0},{1,65},{65,129},{129,193},{193,1... | collective-permute-start | bytes 393224 | tf_op jit(solution)/shard_map/ppermute | solution.py:604
  56.2 27.4 %all-to-all-start.2 = ((bf16[64,8,128]{2,1,0:T(8,128)(2,1)}), bf16[64,8,128]{2,1,0:T(8,128)(2,1)S(1)}, u32[]{:S(2)}, u32[]{:S(2)}) async-start(bf16[64,8,128]{2,1,0:T(8,128)(2,1)} %get-tuple-element.63), calls=%async_computation.2 | async-start | bytes 262144 | tf_op jit(solution)/shard_map/all_to_all | solution.py:608
  63.6 10.1 %collective-permute-start.9 = (bf16[512,128]{1,0:T(8,128)(2,1)S(1)}, bf16[512,128]{1,0:T(8,128)(2,1)S(1)}, u32[]{:S(2)}, u32[]{:S(2)}) collective-permute-start(bf16[512,128]{1,0:T(8,128)(2,1)S(1)} %get-tuple-element.56), channel_id=1, source_target_pairs={{0,1},{1,2},{2,3},{3,4},{4,5},{5,6},{6,7},{7,8},{8,9},{9,10},{10,1... | collective-permute-start | bytes 393224 | tf_op jit(solution)/shard_map/ppermute | solution.py:599
  63.9 9.8 %collective-permute-start.10 = (bf16[512,128]{1,0:T(8,128)(2,1)S(1)}, bf16[512,128]{1,0:T(8,128)(2,1)S(1)}, u32[]{:S(2)}, u32[]{:S(2)}) collective-permute-start(bf16[512,128]{1,0:T(8,128)(2,1)S(1)} %get-tuple-element.57), channel_id=1, source_target_pairs={{1,0},{2,1},{3,2},{4,3},{5,4},{6,5},{7,6},{8,7},{9,8},{10,9},{11,1... | collective-permute-start | bytes 393224 | tf_op jit(solution)/shard_map/ppermute | solution.py:599
  68.9 11.1 %collective-permute-start.5 = (bf16[24,2048]{1,0:T(8,128)(2,1)S(1)}, bf16[24,2048]{1,0:T(8,128)(2,1)S(1)}, u32[]{:S(2)}, u32[]{:S(2)}) collective-permute-start(bf16[24,2048]{1,0:T(8,128)(2,1)S(1)} %get-tuple-element.51), channel_id=1, source_target_pairs={{0,128},{64,192},{128,0},{192,64},{1,129},{65,193},{129,1},{193,65... | collective-permute-start | bytes 294920 | tf_op jit(solution)/shard_map/ppermute | solution.py:604
  73.8 7.0 %collective-permute-start.11 = (bf16[16,256]{1,0:T(8,128)(2,1)S(1)}, bf16[16,256]{1,0:T(8,128)(2,1)S(1)}, u32[]{:S(2)}, u32[]{:S(2)}) collective-permute-start(bf16[16,256]{1,0:T(8,128)(2,1)S(1)} %get-tuple-element.61), channel_id=1, source_target_pairs={{0,64},{64,128},{128,192},{1,65},{65,129},{129,193},{2,66},{66,130... | collective-permute-start | bytes 24584 | tf_op jit(solution)/shard_map/ppermute | solution.py:599
  78.1 5.5 %collective-permute-start.12 = (bf16[16,256]{1,0:T(8,128)(2,1)S(1)}, bf16[16,256]{1,0:T(8,128)(2,1)S(1)}, u32[]{:S(2)}, u32[]{:S(2)}) collective-permute-start(bf16[16,256]{1,0:T(8,128)(2,1)S(1)} %get-tuple-element.62), channel_id=1, source_target_pairs={{64,0},{128,64},{192,128},{65,1},{129,65},{193,129},{66,2},{130,66... | collective-permute-start | bytes 24584 | tf_op jit(solution)/shard_map/ppermute | solution.py:599

commit v3 on v2

--- a/solution.py
+++ b/solution.py
@@ -295,7 +295,7 @@
         total = term if total is None else total + term
     total = total.astype(BF).reshape(ZS, 2, 16, 128)
     for m in range(ZS):
-        send_ref[z_me ^ m, 0:2] = total[m]
+        send_ref[ZS - 1 - (z_me ^ m), 0:2] = total[m]
     key = (seam_ref[0] + HALO) // 16 - 1 + 128
     core = lax.rem(tile, CS)
     z_to = lax.rem(key - lax.rem(key - core, CS) - CS * z_me, CS * ZS) // CS
@@ -329,7 +329,7 @@
     flux_ref, east_ref, west_ref, top_ref, strip_ref,
 ):
     partner = lax.rem((seam_ref[0] + HALO) // 16 - 1 - lax.axis_index("tile") + 128, 64)
-    strip = got_ref[lax.rem(partner // CS, ZS), 2:5]
+    strip = got_ref[ZS - 1 - lax.rem(partner // CS, ZS), 2:5]
     strip_ref[...] = strip
     for side_ref, x in ((east_ref, 13), (west_ref, 0)):
         for k in range(HALO):
@@ -339,7 +339,7 @@
     pieces = []
     for p in range(4):
         source = jnp.clip(seam_ref[1 + p], 0, 63)
-        piece = got_ref[lax.rem(source // CS, ZS), p // 2].astype(F32)[8 * (p % 2) : 8 * (p % 2) + 8]
+        piece = got_ref[ZS - 1 - lax.rem(source // CS, ZS), p // 2].astype(F32)[8 * (p % 2) : 8 * (p % 2) + 8]
         pieces.append(jnp.where(p < count, piece, 0.0))
     blocks = jnp.concatenate(pieces, axis=0).astype(BF)
     spread = (iota((128, 2048), 0) == iota((128, 2048), 1) // 16).astype(BF)
@@ -407,10 +407,9 @@
 
 def conv_kernel(
     seam_ref, state_ref, below_ref, above_ref, west_ref, east_ref, strip_ref, wide_ref, south_ref, north_ref, tops_ref,
-    win_in, wmid_in, wout_in, out_ref,
-    v3, h3, h2, result, masks, win_ref, w2_ref, wout_ref, w1_ref, w3_ref, sems,
+    w1_ref, w1r_ref, w3_ref, wmid_in, out_ref, v3, h3, h2, result, masks, w2_ref, sems,
 ):
-    copies = fetch([(win_in, win_ref), (wmid_in, w2_ref), (wout_in, wout_ref)], sems)
+    copies = fetch([(wmid_in, w2_ref)], sems)
     tiles = tops_ref.shape[0]
     tile = lax.axis_index("tile")
     top = lax.axis_index("lev") == lax.axis_size("lev") - 1
@@ -423,7 +422,7 @@
     fold = None
     for e in range(3):
         pick = ((f == g) & (u == 16 * e + shift - i)).astype(BF)
-        part = tops_ref[lax.rem(seam - tile - e + 2 * tiles, tiles)].astype(F32)
+        part = tops_ref[tiles - 1 - lax.rem(seam - tile - e + 2 * tiles, tiles)].astype(F32)
         term = dot(jnp.concatenate([part, jnp.zeros((8, 128), F32)], axis=0).astype(BF), pick)
         fold = term if fold is None else fold + term
     strips = jnp.concatenate(
@@ -470,23 +469,10 @@
         m = masks[x, lo : lo + size]
         return jnp.concatenate([m, m], axis=1)
 
-    def first_weights(turn):
-        for a in range(3):
-            total = None
-            for b in range(3):
-                w = win_ref[2 - a, 2 - b] if turn else win_ref[a, b]
-                term = dot((iota((256, 84), 0) == iota((256, 84), 1) + 84 * b).astype(BF), w)
-                total = term if total is None else total + term
-            w1_ref[a] = total.astype(BF)
-
-    copies[0].wait()
-    first_weights(False)
-    chunk = 5
+    chunk = 2
     for c0 in range(0, n1, chunk):
-        acc = None
-        for a in range(3):
-            d = dot(v3[c0 + a : c0 + a + chunk].reshape(chunk * PITCH, 256), w1_ref[a])
-            acc = d if acc is None else acc + d
+        left = jnp.concatenate([v3[c0 + a : c0 + a + chunk].reshape(chunk * PITCH, 256) for a in range(3)], axis=1)
+        acc = dot(left, w1_ref[...].reshape(768, 256))
         acc = acc.reshape(chunk, PITCH, 256)
         for k in range(chunk):
             x = c0 + k
@@ -497,10 +483,9 @@
 
     @pl.when(top)
     def _():
-        first_weights(True)
         acc = None
         for a in range(3):
-            d = dot(v3[a : a + n1, 128:144, :].reshape(n1 * 16, 256), w1_ref[a])
+            d = dot(v3[a : a + n1, 128:144, :].reshape(n1 * 16, 256), w1r_ref[a])
             acc = d if acc is None else acc + d
         acc = acc.reshape(n1, 16, 256)
         row = iota((16, 256), 0)
@@ -514,13 +499,11 @@
             old = h3[x, 128:144, 512:768].astype(F32)
             h3[x, 128:144, 512:768] = jnp.where((row == 7) | (row == 8), pltpu.roll(new, 15, 0), old).astype(BF)
 
-    copies[1].wait()
-    chunk = 6
+    copies[0].wait()
+    chunk = 2
     for c0 in range(0, n2, chunk):
-        acc = None
-        for a in range(3):
-            d = dot(h3[c0 + a : c0 + a + chunk].reshape(chunk * PITCH, 768), w2_ref[a])
-            acc = d if acc is None else acc + d
+        left = jnp.concatenate([h3[c0 + a : c0 + a + chunk].reshape(chunk * PITCH, 768) for a in range(3)], axis=1)
+        acc = dot(left, w2_ref[...].reshape(2304, 256))
         acc = acc.reshape(chunk, PITCH, 256)
         for k in range(chunk):
             x = c0 + k
@@ -541,17 +524,10 @@
             old = h2[x, 128:144].astype(F32)
             h2[x, 128:144] = jnp.where(row == 8, g, old).astype(BF)
 
-    copies[2].wait()
-    for a in range(3):
-        for b in range(3):
-            w = wout_ref[a, b].astype(F32)
-            w3_ref[a, 128 * b : 128 * b + 128] = jnp.concatenate([w, jnp.zeros((52, 256), F32)], axis=0).astype(BF)
-    chunk = 4
+    chunk = 2
     for c0 in range(0, n3, chunk):
-        acc = None
-        for a in range(3):
-            d = dot_nt(h2[c0 + a : c0 + a + chunk].reshape(chunk * PITCH, 256), w3_ref[a])
-            acc = d if acc is None else acc + d
+        left = jnp.concatenate([h2[c0 + a : c0 + a + chunk].reshape(chunk * PITCH, 256) for a in range(3)], axis=1)
+        acc = dot_nt(left, w3_ref[...])
         acc = acc.reshape(chunk, PITCH, 384)
         for k in range(chunk):
             x = c0 + k
@@ -565,10 +541,46 @@
     out_ref[...] = result[...][:76].astype(BF)
 
 
+def weights_kernel(flux_ref, win_in, wout_in, w1_ref, w1r_ref, w3_ref, win_ref, wout_ref, sems):
+    copies = fetch([(win_in, win_ref), (wout_in, wout_ref)], sems)
+    copies[0].wait()
+    for ref, turn in ((w1_ref, False), (w1r_ref, True)):
+        for a in range(3):
+            total = None
+            for b in range(3):
+                w = win_ref[2 - a, 2 - b] if turn else win_ref[a, b]
+                term = dot((iota((256, 84), 0) == iota((256, 84), 1) + 84 * b).astype(BF), w)
+                total = term if total is None else total + term
+            ref[a] = total.astype(BF)
+    copies[1].wait()
+    for a in range(3):
+        for b in range(3):
+            w = wout_ref[a, b].astype(F32)
+            w = jnp.concatenate([w, jnp.zeros((52, 256), F32)], axis=0).astype(BF)
+            w3_ref[128 * b : 128 * b + 128, 256 * a : 256 * a + 256] = w
+
+
+def conv_weights(flux, win, wout):
+    return pl.pallas_call(
+        weights_kernel,
+        in_specs=vmem_specs(1) + hbm_specs(2),
+        out_specs=vmem_specs(3),
+        out_shape=[
+            jax.ShapeDtypeStruct((3, 256, 256), BF),
+            jax.ShapeDtypeStruct((3, 256, 256), BF),
+            jax.ShapeDtypeStruct((384, 768), BF),
+        ],
+        scratch_shapes=[pltpu.VMEM(w.shape, BF) for w in (win, wout)] + [pltpu.SemaphoreType.DMA((2,))],
+        compiler_params=params(8),
+        cost_estimate=pl.CostEstimate(flops=10**9, bytes_accessed=4 * 10**6, transcendentals=0),
+        name="conv_weights",
+    )(flux, *in_hbm(win, wout))
+
+
 def convolutions(*args):
     return pl.pallas_call(
         conv_kernel,
-        in_specs=[smem_spec()] + vmem_specs(len(args) - 4) + hbm_specs(3),
+        in_specs=[smem_spec()] + vmem_specs(len(args) - 2) + hbm_specs(1),
         out_specs=vmem_specs(1)[0],
         out_shape=jax.ShapeDtypeStruct((76, 16, 128), BF),
         scratch_shapes=[
@@ -578,16 +590,11 @@
             pltpu.VMEM((80, 16, 128), F32),
             pltpu.VMEM((22, PITCH, 128), F32),
         ]
-        + [pltpu.VMEM(w.shape, BF) for w in args[-3:]]
-        + [
-            pltpu.VMEM((3, 256, 256), BF),
-            pltpu.VMEM((3, 384, 256), BF),
-            pltpu.SemaphoreType.DMA((3,)),
-        ],
-        compiler_params=params(32),
+        + [pltpu.VMEM(args[-1].shape, BF), pltpu.SemaphoreType.DMA((1,))],
+        compiler_params=params(24),
         cost_estimate=pl.CostEstimate(flops=8 * 10**9, bytes_accessed=8 * 10**6, transcendentals=0),
         name="convolutions",
-    )(*args[:-3], *in_hbm(*args[-3:]))
+    )(*args[:-1], *in_hbm(args[-1]))
 
 
 def shifted(forth, back, axis, periodic):
@@ -631,7 +638,7 @@
     tiles = lax.axis_size("tile")
     _, span_x, span_y = ocean_state.shape
     pairs, blk = margin.shape[0], margin.shape[1]
-    along_z = [[(x * ZS + z) * CS + c for z in range(ZS)] for x in range(tiles // (ZS * CS)) for c in range(CS)]
+    along_z = [[(x * ZS + z) * CS + c for z in reversed(range(ZS))] for x in range(tiles // (ZS * CS)) for c in range(CS)]
     same_z = [[(x * ZS + z) * CS + c for x in range(tiles // (ZS * CS)) for c in range(CS)] for z in range(ZS)]
 
     pieces = collect(atm_state, surface, groups)
@@ -648,7 +655,8 @@
 
     state, asks = lax.optimization_barrier((state, asks))
     *updated, send = column_model(pieces, *weights, state)
-    near = jnp.concatenate([asks, across(asks, 2)], axis=0)
+    send, second = lax.optimization_barrier((send, across(asks, 2)))
+    near = jnp.concatenate([asks, second], axis=0)
     blocks = per_tile(send, same_z)
     got = per_tile(pack(seam, near, across(near, 4), blocks), along_z)
 
@@ -661,12 +669,14 @@
     )
 
     low, high = shifted(last, first, "tile", True)
-    tops = per_tile(top)
+    tops = per_tile(top, [list(reversed(range(tiles)))])
+    conv_ws = conv_weights(last, conv_in, conv_out.transpose(0, 1, 3, 2))
+    low, high, *conv_ws = lax.optimization_barrier((low, high, *conv_ws))
     wide, up, down = rim(low, flux, high)
     south, north = shifted(up, down, "lev", False)
     ocean_next = convolutions(
         seam, state, below, above, low, high, partner, wide, south, north, tops,
-        conv_in, conv_mid.reshape(3, 768, 256), conv_out.transpose(0, 1, 3, 2),
+        *conv_ws, conv_mid.reshape(3, 768, 256),
     )
     return (atm_next, ocean_next)
 

time: 96.8 us -> 90.1 us (0.931)
  waiting for transfers between devices: 17.5 us -> 10.2 us
    ppermute x2, starting transfers between devices: 6.93 us -> 2.29 us  [shifted(): lax.ppermute(back, axis, backward)]
    all_to_all x3, starting transfers between devices: 19 us -> 22.9 us  [per_tile(): lax.all_to_all(x, 'tile', split_axis=0, concat_axis=0, tiled=True, axis_i...]
    ppermute x6, waiting for transfers between devices: 7.11 us -> 3.76 us  [turned(): return lax.ppermute(x, axis, [(i, (i + by) % count) for i in range(count)])]
    all_to_all x3, waiting for transfers between devices: 3.83 us -> 0.74 us  [per_tile(): lax.all_to_all(x, 'tile', split_axis=0, concat_axis=0, tiled=True, axis_i...]
    pallas_call x0 -> x1, Pallas kernels: none -> 1.81 us  [conv_weights(): pl.pallas_call(weights_kernel, in_specs=vmem_specs(1) + hbm_specs(2), out...]
    ppermute x3, waiting for transfers between devices: 3.34 us -> 1.73 us  [across(): return lax.ppermute(asks, 'tile', [(t, t ^ CS * bit) for t in range(tiles)])]
    pallas_call x1, Pallas kernels: 12.5 us -> 11.5 us  [convolutions(): pl.pallas_call(conv_kernel, in_specs=[smem_spec()] + vmem_specs(len(args)...]
  transfers between devices with their start and end apart: 16 -> 16, of which waited for: 9 -> 8; matrix products, arithmetic and copies ran while one was open for 0% -> 0% of each run, Pallas kernels for 3% -> 10%
where the time goes in v3:
time: 90.1 us; the launch traced here: 89.6 us
  starting transfers between devices  50.9 us (56%)
  Pallas kernels  27 us (30%)
  waiting for transfers between devices  10.2 us (11%)
  between operations  1.55 us (2%)
    all_to_all x3, starting transfers between devices, per_tile(): lax.all_to_all(x, 'tile', split_axis=0, concat_axis=0, tiled=True, axis_i...  22.9 us
    ppermute x3, starting transfers between devices, across(): return lax.ppermute(asks, 'tile', [(t, t ^ CS * bit) for t in range(tiles)])  11.7 us
    pallas_call x1, Pallas kernels, convolutions(): pl.pallas_call(conv_kernel, in_specs=[smem_spec()] + vmem_specs(len(args)...  11.5 us
    ppermute x6, starting transfers between devices, turned(): return lax.ppermute(x, axis, [(i, (i + by) % count) for i in range(count)])  9.35 us
    pallas_call x1, Pallas kernels, column_model(): pl.pallas_call(mlp_kernel, in_specs=vmem_specs(8), out_specs=vmem_specs(5...  4.67 us
    ppermute x2, starting transfers between devices, shifted(): lax.ppermute(forth, axis, forward)  4.61 us
    ppermute x6, waiting for transfers between devices, turned(): return lax.ppermute(x, axis, [(i, (i + by) % count) for i in range(count)])  3.76 us
    ppermute x2, waiting for transfers between devices, shifted(): lax.ppermute(back, axis, backward)  2.82 us
  transfers between devices with their start and end apart: 16, of which 8 were waited for; matrix products, arithmetic and copies ran while one was open for 0% of the time, Pallas kernels for 10%

profile of v3, /device:TPU:16, one launch (start us, length us, event | category | flops | bytes accessed | tf_op | source)
XLA Modules:
  0.0 89.6 jit_solution(7276713522880610066)
XLA Ops:
  0.6 1.1 %collect.1 = (bf16[24,2048]{1,0:T(8,128)(2,1)S(1)}, bf16[24,2048]{1,0:T(8,128)(2,1)S(1)}, bf16[24,2048]{1,0:T(8,128)(2,1)S(1)}, bf16[24,2048]{1,0:T(8,128)(2,1)S(1)}) custom-call(bf16[3,6,8192]{2,1,0:T(8,128)(2,1)} %atm_ref.1, bf16[1,8192]{1,0:T(2,128)(2,1)} %surface_ref.1), custom_call_target="tpu_custom_call" | custom-call | flops 1000000 | bytes 1000000 | tf_op jit(solution)/shard_map/collect/pallas_call | solution.py:92
  2.4 1.4 %asking.1 = (bf16[1,16,128]{2,1,0:T(8,128)(2,1)S(1)}, s32[8]{0:T(128)S(1)}) custom-call(s32[1,1]{1,0:T(1,128)S(6)} %copy.19.count_ref, s32[1,1,4]{2,1,0:T(1,128)} %tile_in, s32[1,1,4]{2,1,0:T(1,128)} %block_in.1, s32[1024]{0:T(1024)} %fold_in.1), custom_call_target="tpu_custom_call" | custom-call | flops 1000000 | bytes 100000 | tf_op jit(solution)/shard_map/asking/pallas_call | solution.py:151
  3.8 2.0 %collective-permute-start.3 = (bf16[1,16,128]{2,1,0:T(8,128)(2,1)S(1)}, bf16[1,16,128]{2,1,0:T(8,128)(2,1)S(1)}, u32[]{:S(2)}, u32[]{:S(2)}) collective-permute-start(bf16[1,16,128]{2,1,0:T(8,128)(2,1)S(1)} %get-tuple-element.57), channel_id=1, source_target_pairs={{0,2},{1,3},{2,0},{3,1},{4,6},{5,7},{6,4},{7,5},{8,10},{9,11},{10,... | collective-permute-start | bytes 12296 | tf_op jit(solution)/shard_map/ppermute | solution.py:649
  5.8 1.3 %collective-permute-start = (bf16[24,2048]{1,0:T(8,128)(2,1)S(1)}, bf16[24,2048]{1,0:T(8,128)(2,1)S(1)}, u32[]{:S(2)}, u32[]{:S(2)}) collective-permute-start(bf16[24,2048]{1,0:T(8,128)(2,1)S(1)} %get-tuple-element.48), channel_id=1, source_target_pairs={{0,64},{64,128},{128,192},{192,0},{1,65},{65,129},{129,193},{193,1... | collective-permute-start | bytes 294920 | tf_op jit(solution)/shard_map/ppermute | solution.py:611
  7.1 0.6 collective-permute-start.1
  7.7 1.1 %collective-permute-start.2 = (bf16[24,2048]{1,0:T(8,128)(2,1)S(1)}, bf16[24,2048]{1,0:T(8,128)(2,1)S(1)}, u32[]{:S(2)}, u32[]{:S(2)}) collective-permute-start(bf16[24,2048]{1,0:T(8,128)(2,1)S(1)} %get-tuple-element.50), channel_id=1, source_target_pairs={{0,192},{64,0},{128,64},{192,128},{1,193},{65,1},{129,65},{193,129... | collective-permute-start | bytes 294920 | tf_op jit(solution)/shard_map/ppermute | solution.py:611
  8.8 1.7 %prepare.1 = (bf16[16,128,128]{2,1,0:T(8,128)(2,1)S(1)}, bf16[512,96]{1,0:T(8,128)(2,1)S(1)}, bf16[512,512]{1,0:T(8,128)(2,1)S(1)}, bf16[104,512]{1,0:T(8,128)(2,1)S(1)}) custom-call(bf16[76,16,128]{2,1,0:T(8,128)(2,1)} %state_in, s32[16,128]{1,0:T(8,128)} %mask_in.1, bf16[76,512]{1,0:T(8,128)(2,1)} %win_in.2, bf16[512,512]{1,0:T(8,128)(2,1)} %wmid_in.1, ...), custom_call_target="tpu_custom_call" | custom-call | flops 1000000000 | bytes 1000000 | tf_op jit(solution)/shard_map/prepare/pallas_call | solution.py:211
  10.5 3.4 %collective-permute-start.7 = (bf16[2,16,128]{2,1,0:T(8,128)(2,1)S(1)}, bf16[2,16,128]{2,1,0:T(8,128)(2,1)S(1)}, u32[]{:S(2)}, u32[]{:S(2)}) collective-permute-start(bf16[2,16,128]{2,1,0:T(8,128)(2,1)S(1)} %pad_maximum_fusion), channel_id=1, source_target_pairs={{0,4},{1,5},{2,6},{3,7},{4,0},{5,1},{6,2},{7,3},{8,12},{9,13},{10,... | collective-permute-start | bytes 24584 | tf_op jit(solution)/shard_map/ppermute | solution.py:649
  14.0 4.7 %column_model.1 = (bf16[24,2048]{1,0:T(8,128)(2,1)S(1)}, bf16[32,2048]{1,0:T(8,128)(2,1)S(1)}, bf16[24,2048]{1,0:T(8,128)(2,1)S(1)}, bf16[32,2048]{1,0:T(8,128)(2,1)S(1)}, bf16[8,11,16,128]{3,2,1,0:T(8,128)(2,1)}) custom-call(bf16[24,2048]{1,0:T(8,128)(2,1)S(1)} %get-tuple-element.47.z0_ref, bf16[24,2048]{1,0:T(8,128)(2,1)S(1)} %collective-permute-done.z1_ref, ...), custom_call_target="tpu_custom_call" | custom-call | flops 3000000000 | bytes 2000000 | tf_op jit(solution)/shard_map/column_model/pallas_call | solution.py:264
  18.7 4.3 %all-to-all-start = ((bf16[8,11,16,128]{3,2,1,0:T(8,128)(2,1)}), bf16[8,11,16,128]{3,2,1,0:T(8,128)(2,1)S(1)}, u32[]{:S(2)}, u32[]{:S(2)}) async-start(bf16[8,11,16,128]{3,2,1,0:T(8,128)(2,1)} %get-tuple-element.67), calls=%async_computation | async-start | bytes 720896 | tf_op jit(solution)/shard_map/all_to_all | solution.py:615
  23.0 6.4 %collective-permute-start.8 = (bf16[4,16,128]{2,1,0:T(8,128)(2,1)S(1)}, bf16[4,16,128]{2,1,0:T(8,128)(2,1)S(1)}, u32[]{:S(2)}, u32[]{:S(2)}) collective-permute-start(bf16[4,16,128]{2,1,0:T(8,128)(2,1)S(1)} %constant_dynamic-update-slice_fusion.near_ref), channel_id=1, source_target_pairs={{0,8},{1,9},{2,10},{3,11},{4,12},{5,13},{6,14},{7,15},{8,0},{9,1},... | collective-permute-start | bytes 49160 | tf_op jit(solution)/shard_map/ppermute | solution.py:649
  29.4 1.7 %collective-permute-done.8.far_ref = bf16[4,16,128]{2,1,0:T(8,128)(2,1)S(1)} collective-permute-done((bf16[4,16,128]{2,1,0:T(8,128)(2,1)S(1)}, bf16[4,16,128]{2,1,0:T(8,128)(2,1)S(1)}, u32[]{:S(2)}, u32[]{:S(2)}) %collective-permute-start.8) | collective-permute-done | bytes 16416 | tf_op jit(solution)/shard_map/ppermute | solution.py:649
  31.1 0.5 all-to-all-done.got_ref
  31.6 1.5 %pack.1 = bf16[8,5,16,128]{3,2,1,0:T(8,128)(2,1)} custom-call(s32[8]{0:T(128)S(1)} %get-tuple-element.63.seam_ref, bf16[4,16,128]{2,1,0:T(8,128)(2,1)S(1)} %constant_dynamic-update-slice_fusion.near_ref, bf16[4,16,128]{2,1,0:T(8,128)(2,1)S(1)} %collective-permute-done.8.far_ref, bf16[8,11,16,128]{3,2,1,0:T(8,128)(2,1)S(1)} %all-to-all-done.got_ref), custom_call_target="tpu_custom_call" | custom-call | flops 100000000 | bytes 1000000 | tf_op jit(solution)/shard_map/pack/pallas_call | solution.py:309
  33.1 8.3 %all-to-all-start.1 = ((bf16[8,5,16,128]{3,2,1,0:T(8,128)(2,1)}), bf16[8,5,16,128]{3,2,1,0:T(8,128)(2,1)S(1)}, u32[]{:S(2)}, u32[]{:S(2)}) async-start(bf16[8,5,16,128]{3,2,1,0:T(8,128)(2,1)} %pack.1), calls=%async_computation.1 | async-start | bytes 327680 | tf_op jit(solution)/shard_map/all_to_all | solution.py:615
  41.4 0.6 collective-permute-start.4
  42.0 1.4 %collective-permute-start.6 = (bf16[32,2048]{1,0:T(8,128)(2,1)S(1)}, bf16[32,2048]{1,0:T(8,128)(2,1)S(1)}, u32[]{:S(2)}, u32[]{:S(2)}) collective-permute-start(bf16[32,2048]{1,0:T(8,128)(2,1)S(1)} %get-tuple-element.62), channel_id=1, source_target_pairs={{0,64},{64,128},{128,192},{192,0},{1,65},{65,129},{129,193},{193,1... | collective-permute-start | bytes 393224 | tf_op jit(solution)/shard_map/ppermute | solution.py:611
  43.4 2.9 %collective-permute-done.4.refs_1_.north_ref.above_ref = bf16[32,2048]{1,0:T(8,128)(2,1)S(1)} collective-permute-done((bf16[32,2048]{1,0:T(8,128)(2,1)S(1)}, bf16[32,2048]{1,0:T(8,128)(2,1)S(1)}, u32[]{:S(2)}, u32[]{:S(2)}) %collective-permute-start.4) | collective-permute-done | bytes 131104 | tf_op jit(solution)/shard_map/ppermute | solution.py:611
  46.4 0.6 collective-permute-done.6.refs_3_.south_ref.below_ref
  47.0 0.3 all-to-all-done.1.got_ref
  47.2 2.3 %remap.1 = (bf16[128,128]{1,0:T(8,128)(2,1)S(1)}, bf16[512,128]{1,0:T(8,128)(2,1)S(1)}, bf16[512,128]{1,0:T(8,128)(2,1)S(1)}, bf16[64,8,128]{2,1,0:T(8,128)(2,1)}, bf16[3,16,128]{2,1,0:T(8,128)(2,1)S(1)}) custom-call(s32[8]{0:T(128)S(1)} %get-tuple-element.63.seam_ref, bf16[8,5,16,128]{3,2,1,0:T(8,128)(2,1)S(1)} %all-to-all-done.1.got_ref, ...), custom_call_target="tpu_custom_call" | custom-call | flops 1000000000 | bytes 3000000 | tf_op jit(solution)/shard_map/remap/pallas_call | solution.py:369
  49.6 10.3 %all-to-all-start.2 = ((bf16[64,8,128]{2,1,0:T(8,128)(2,1)}), bf16[64,8,128]{2,1,0:T(8,128)(2,1)S(1)}, u32[]{:S(2)}, u32[]{:S(2)}) async-start(bf16[64,8,128]{2,1,0:T(8,128)(2,1)} %get-tuple-element.80), calls=%async_computation.2 | async-start | bytes 262144 | tf_op jit(solution)/shard_map/all_to_all | solution.py:615
  59.9 0.4 collective-permute-start.10
  60.3 0.4 collective-permute-start.9
  60.7 4.4 %collective-permute-start.5 = (bf16[24,2048]{1,0:T(8,128)(2,1)S(1)}, bf16[24,2048]{1,0:T(8,128)(2,1)S(1)}, u32[]{:S(2)}, u32[]{:S(2)}) collective-permute-start(bf16[24,2048]{1,0:T(8,128)(2,1)S(1)} %get-tuple-element.61), channel_id=1, source_target_pairs={{0,128},{64,192},{128,0},{192,64},{1,129},{65,193},{129,1},{193,65... | collective-permute-start | bytes 294920 | tf_op jit(solution)/shard_map/ppermute | solution.py:611
  65.0 1.8 %conv_weights.1 = (bf16[3,256,256]{2,1,0:T(8,128)(2,1)S(1)}, bf16[3,256,256]{2,1,0:T(8,128)(2,1)S(1)}, bf16[384,768]{1,0:T(8,128)(2,1)S(1)}) custom-call(bf16[512,128]{1,0:T(8,128)(2,1)S(1)} %get-tuple-element.68.flux_ref, bf16[3,3,84,256]{3,2,1,0:T(8,128)(2,1)} %win_in.3, bf16[3,3,76,256]{3,2,1,0:T(8,128)(2,1)} %bitcast.7), custom_call_target="tpu_custom_call" | custom-call | flops 1000000000 | bytes 4000000 | tf_op jit(solution)/shard_map/conv_weights/pallas_call | solution.py:564
  66.9 1.1 %collective-permute-done.9.low_ref.west_ref = bf16[512,128]{1,0:T(8,128)(2,1)S(1)} collective-permute-done((bf16[512,128]{1,0:T(8,128)(2,1)S(1)}, bf16[512,128]{1,0:T(8,128)(2,1)S(1)}, u32[]{:S(2)}, u32[]{:S(2)}) %collective-permute-start.9) | collective-permute-done | bytes 131104 | tf_op jit(solution)/shard_map/ppermute | solution.py:606
  68.1 4.2 %collective-permute-start.11 = (bf16[16,256]{1,0:T(8,128)(2,1)S(1)}, bf16[16,256]{1,0:T(8,128)(2,1)S(1)}, u32[]{:S(2)}, u32[]{:S(2)}) collective-permute-start(bf16[16,256]{1,0:T(8,128)(2,1)S(1)} %get-tuple-element.78), channel_id=1, source_target_pairs={{0,64},{64,128},{128,192},{1,65},{65,129},{129,193},{2,66},{66,130... | collective-permute-start | bytes 24584 | tf_op jit(solution)/shard_map/ppermute | solution.py:606
  72.4 1.9 %collective-permute-start.12 = (bf16[16,256]{1,0:T(8,128)(2,1)S(1)}, bf16[16,256]{1,0:T(8,128)(2,1)S(1)}, u32[]{:S(2)}, u32[]{:S(2)}) collective-permute-start(bf16[16,256]{1,0:T(8,128)(2,1)S(1)} %get-tuple-element.79), channel_id=1, source_target_pairs={{64,0},{128,64},{192,128},{65,1},{129,65},{193,129},{66,2},{130,66... | collective-permute-start | bytes 24584 | tf_op jit(solution)/shard_map/ppermute | solution.py:606
  74.3 0.8 spread.1
  75.1 2.8 %collective-permute-done.12.north_ref = bf16[16,256]{1,0:T(8,128)(2,1)S(1)} collective-permute-done((bf16[16,256]{1,0:T(8,128)(2,1)S(1)}, bf16[16,256]{1,0:T(8,128)(2,1)S(1)}, u32[]{:S(2)}, u32[]{:S(2)}) %collective-permute-start.12) | collective-permute-done | bytes 8224 | tf_op jit(solution)/shard_map/ppermute | solution.py:606
  77.9 11.5 %convolutions.1 = bf16[76,16,128]{2,1,0:T(8,128)(2,1)} custom-call(s32[8]{0:T(128)S(1)} %get-tuple-element.63.seam_ref, bf16[16,128,128]{2,1,0:T(8,128)(2,1)S(1)} %get-tuple-element.58.state_ref, bf16[32,2048]{1,0:T(8,128)(2,1)S(1)} %collective-permute-done.6.refs_3_.south_ref.below_ref, ...), custom_call_target="tpu_custom_call" | custom-call | flops 8000000000 | bytes 8000000 | tf_op jit(solution)/shard_map/convolutions/pallas_call | solution.py:581
  (15 shorter events, 0.4 us)
Async XLA Ops:
  3.8 6.6 %collective-permute-start.3 = (bf16[1,16,128]{2,1,0:T(8,128)(2,1)S(1)}, bf16[1,16,128]{2,1,0:T(8,128)(2,1)S(1)}, u32[]{:S(2)}, u32[]{:S(2)}) collective-permute-start(bf16[1,16,128]{2,1,0:T(8,128)(2,1)S(1)} %get-tuple-element.57), channel_id=1, source_target_pairs={{0,2},{1,3},{2,0},{3,1},{4,6},{5,7},{6,4},{7,5},{8,10},{9,11},{10,... | collective-permute-start | bytes 12296 | tf_op jit(solution)/shard_map/ppermute | solution.py:649
  5.8 8.0 %collective-permute-start = (bf16[24,2048]{1,0:T(8,128)(2,1)S(1)}, bf16[24,2048]{1,0:T(8,128)(2,1)S(1)}, u32[]{:S(2)}, u32[]{:S(2)}) collective-permute-start(bf16[24,2048]{1,0:T(8,128)(2,1)S(1)} %get-tuple-element.48), channel_id=1, source_target_pairs={{0,64},{64,128},{128,192},{192,0},{1,65},{65,129},{129,193},{193,1... | collective-permute-start | bytes 294920 | tf_op jit(solution)/shard_map/ppermute | solution.py:611
  7.1 6.7 %collective-permute-start.1 = (bf16[24,2048]{1,0:T(8,128)(2,1)S(1)}, bf16[24,2048]{1,0:T(8,128)(2,1)S(1)}, u32[]{:S(2)}, u32[]{:S(2)}) collective-permute-start(bf16[24,2048]{1,0:T(8,128)(2,1)S(1)} %get-tuple-element.49), channel_id=1, source_target_pairs={{0,128},{64,192},{128,0},{192,64},{1,129},{65,193},{129,1},{193,65... | collective-permute-start | bytes 294920 | tf_op jit(solution)/shard_map/ppermute | solution.py:611
  7.7 6.3 %collective-permute-start.2 = (bf16[24,2048]{1,0:T(8,128)(2,1)S(1)}, bf16[24,2048]{1,0:T(8,128)(2,1)S(1)}, u32[]{:S(2)}, u32[]{:S(2)}) collective-permute-start(bf16[24,2048]{1,0:T(8,128)(2,1)S(1)} %get-tuple-element.50), channel_id=1, source_target_pairs={{0,192},{64,0},{128,64},{192,128},{1,193},{65,1},{129,65},{193,129... | collective-permute-start | bytes 294920 | tf_op jit(solution)/shard_map/ppermute | solution.py:611
  10.5 8.2 %collective-permute-start.7 = (bf16[2,16,128]{2,1,0:T(8,128)(2,1)S(1)}, bf16[2,16,128]{2,1,0:T(8,128)(2,1)S(1)}, u32[]{:S(2)}, u32[]{:S(2)}) collective-permute-start(bf16[2,16,128]{2,1,0:T(8,128)(2,1)S(1)} %pad_maximum_fusion), channel_id=1, source_target_pairs={{0,4},{1,5},{2,6},{3,7},{4,0},{5,1},{6,2},{7,3},{8,12},{9,13},{10,... | collective-permute-start | bytes 24584 | tf_op jit(solution)/shard_map/ppermute | solution.py:649
  14.0 33.2 %copy-start = (bf16[4,128,16,128]{3,2,1,0:T(8,128)(2,1)S(1)}, bf16[4,128,16,128]{3,2,1,0:T(8,128)(2,1)}, u32[]{:S(2)}) copy-start(bf16[4,128,16,128]{3,2,1,0:T(8,128)(2,1)} %param.28) | copy-start | bytes 6291460
  18.7 12.9 %all-to-all-start = ((bf16[8,11,16,128]{3,2,1,0:T(8,128)(2,1)}), bf16[8,11,16,128]{3,2,1,0:T(8,128)(2,1)S(1)}, u32[]{:S(2)}, u32[]{:S(2)}) async-start(bf16[8,11,16,128]{3,2,1,0:T(8,128)(2,1)} %get-tuple-element.67), calls=%async_computation | async-start | bytes 720896 | tf_op jit(solution)/shard_map/all_to_all | solution.py:615
  23.0 8.1 %collective-permute-start.8 = (bf16[4,16,128]{2,1,0:T(8,128)(2,1)S(1)}, bf16[4,16,128]{2,1,0:T(8,128)(2,1)S(1)}, u32[]{:S(2)}, u32[]{:S(2)}) collective-permute-start(bf16[4,16,128]{2,1,0:T(8,128)(2,1)S(1)} %constant_dynamic-update-slice_fusion.near_ref), channel_id=1, source_target_pairs={{0,8},{1,9},{2,10},{3,11},{4,12},{5,13},{6,14},{7,15},{8,0},{9,1},... | collective-permute-start | bytes 49160 | tf_op jit(solution)/shard_map/ppermute | solution.py:649
  33.1 14.1 %all-to-all-start.1 = ((bf16[8,5,16,128]{3,2,1,0:T(8,128)(2,1)}), bf16[8,5,16,128]{3,2,1,0:T(8,128)(2,1)S(1)}, u32[]{:S(2)}, u32[]{:S(2)}) async-start(bf16[8,5,16,128]{3,2,1,0:T(8,128)(2,1)} %pack.1), calls=%async_computation.1 | async-start | bytes 327680 | tf_op jit(solution)/shard_map/all_to_all | solution.py:615
  41.4 5.0 %collective-permute-start.4 = (bf16[32,2048]{1,0:T(8,128)(2,1)S(1)}, bf16[32,2048]{1,0:T(8,128)(2,1)S(1)}, u32[]{:S(2)}, u32[]{:S(2)}) collective-permute-start(bf16[32,2048]{1,0:T(8,128)(2,1)S(1)} %get-tuple-element.60), channel_id=1, source_target_pairs={{0,192},{64,0},{128,64},{192,128},{1,193},{65,1},{129,65},{193,129... | collective-permute-start | bytes 393224 | tf_op jit(solution)/shard_map/ppermute | solution.py:611
  42.0 5.0 %collective-permute-start.6 = (bf16[32,2048]{1,0:T(8,128)(2,1)S(1)}, bf16[32,2048]{1,0:T(8,128)(2,1)S(1)}, u32[]{:S(2)}, u32[]{:S(2)}) collective-permute-start(bf16[32,2048]{1,0:T(8,128)(2,1)S(1)} %get-tuple-element.62), channel_id=1, source_target_pairs={{0,64},{64,128},{128,192},{192,0},{1,65},{65,129},{129,193},{193,1... | collective-permute-start | bytes 393224 | tf_op jit(solution)/shard_map/ppermute | solution.py:611
  49.6 28.3 %all-to-all-start.2 = ((bf16[64,8,128]{2,1,0:T(8,128)(2,1)}), bf16[64,8,128]{2,1,0:T(8,128)(2,1)S(1)}, u32[]{:S(2)}, u32[]{:S(2)}) async-start(bf16[64,8,128]{2,1,0:T(8,128)(2,1)} %get-tuple-element.80), calls=%async_computation.2 | async-start | bytes 262144 | tf_op jit(solution)/shard_map/all_to_all | solution.py:615
  59.9 6.9 %collective-permute-start.10 = (bf16[512,128]{1,0:T(8,128)(2,1)S(1)}, bf16[512,128]{1,0:T(8,128)(2,1)S(1)}, u32[]{:S(2)}, u32[]{:S(2)}) collective-permute-start(bf16[512,128]{1,0:T(8,128)(2,1)S(1)} %get-tuple-element.69), channel_id=1, source_target_pairs={{1,0},{2,1},{3,2},{4,3},{5,4},{6,5},{7,6},{8,7},{9,8},{10,9},{11,1... | collective-permute-start | bytes 393224 | tf_op jit(solution)/shard_map/ppermute | solution.py:606
  60.3 7.7 %collective-permute-start.9 = (bf16[512,128]{1,0:T(8,128)(2,1)S(1)}, bf16[512,128]{1,0:T(8,128)(2,1)S(1)}, u32[]{:S(2)}, u32[]{:S(2)}) collective-permute-start(bf16[512,128]{1,0:T(8,128)(2,1)S(1)} %get-tuple-element.68.flux_ref), channel_id=1, source_target_pairs={{0,1},{1,2},{2,3},{3,4},{4,5},{5,6},{6,7},{7,8},{8,9},{9,10},{10,1... | collective-permute-start | bytes 393224 | tf_op jit(solution)/shard_map/ppermute | solution.py:606
  60.7 13.6 %collective-permute-start.5 = (bf16[24,2048]{1,0:T(8,128)(2,1)S(1)}, bf16[24,2048]{1,0:T(8,128)(2,1)S(1)}, u32[]{:S(2)}, u32[]{:S(2)}) collective-permute-start(bf16[24,2048]{1,0:T(8,128)(2,1)S(1)} %get-tuple-element.61), channel_id=1, source_target_pairs={{0,128},{64,192},{128,0},{192,64},{1,129},{65,193},{129,1},{193,65... | collective-permute-start | bytes 294920 | tf_op jit(solution)/shard_map/ppermute | solution.py:611
  68.1 7.0 %collective-permute-start.11 = (bf16[16,256]{1,0:T(8,128)(2,1)S(1)}, bf16[16,256]{1,0:T(8,128)(2,1)S(1)}, u32[]{:S(2)}, u32[]{:S(2)}) collective-permute-start(bf16[16,256]{1,0:T(8,128)(2,1)S(1)} %get-tuple-element.78), channel_id=1, source_target_pairs={{0,64},{64,128},{128,192},{1,65},{65,129},{129,193},{2,66},{66,130... | collective-permute-start | bytes 24584 | tf_op jit(solution)/shard_map/ppermute | solution.py:606
  72.4 5.5 %collective-permute-start.12 = (bf16[16,256]{1,0:T(8,128)(2,1)S(1)}, bf16[16,256]{1,0:T(8,128)(2,1)S(1)}, u32[]{:S(2)}, u32[]{:S(2)}) collective-permute-start(bf16[16,256]{1,0:T(8,128)(2,1)S(1)} %get-tuple-element.79), channel_id=1, source_target_pairs={{64,0},{128,64},{192,128},{65,1},{129,65},{193,129},{66,2},{130,66... | collective-permute-start | bytes 24584 | tf_op jit(solution)/shard_map/ppermute | solution.py:606

commit v4 on v3

--- a/solution.py
+++ b/solution.py
@@ -67,8 +67,8 @@
     return tile, lax.rem(tile // CS, ZS)
 
 
-def collect_kernel(atm_ref, surface_ref, *refs):
-    *out_refs, atm, surface, sems = refs
+def collect_kernel(count_ref, tile_in, block_in, fold_in, atm_ref, surface_ref, *refs):
+    *out_refs, ask_ref, seam_ref, tile_ref, block_ref, fold_ref, atm, surface, sems = refs
     levels, _, cols = atm_ref.shape
     parts = len(out_refs)
     size = cols // parts
@@ -76,10 +76,26 @@
     zero = jnp.zeros((1, size), F32)
     spans = [pl.ds(pl.multiple_of(lax.rem(lev + k, parts) * size, size), size) for k in range(parts)]
     order = (1, 2, 3, 0)
-    copies = fetch([(surface_ref, surface)] + [(atm_ref.at[:, :, spans[k]], atm.at[k]) for k in order], sems)
-    copies[0].wait()
+    tables = [(tile_in, tile_ref), (block_in, block_ref), (fold_in, fold_ref)]
+    copies = fetch(
+        tables + [(surface_ref, surface)] + [(atm_ref.at[:, :, spans[k]], atm.at[k]) for k in order], sems
+    )
+    for copy in copies[:3]:
+        copy.wait()
+    seam_ref[0] = fold_ref[0]
+    seam_ref[5] = count_ref[0, 0]
+    rows, zs = [], []
+    for p in range(4):
+        source, block = tile_ref[0, 0, p], block_ref[0, 0, p]
+        seam_ref[1 + p] = source
+        number = (source // (CS * ZS) * CS + lax.rem(source, CS)) * 16 + block
+        z = jnp.where(p < count_ref[0, 0], lax.rem(source // CS, ZS), -1)
+        rows.append(jnp.full((1, 128), number, I32))
+        zs.append(jnp.full((1, 128), z, I32))
+    ask_ref[0] = jnp.concatenate(rows + zs + [jnp.zeros((8, 128), I32)], axis=0).astype(F32).astype(BF)
+    copies[3].wait()
     for i, k in enumerate(order):
-        copies[1 + i].wait()
+        copies[4 + i].wait()
         rows = []
         for j in range(levels):
             extra = surface[:, spans[k]].astype(F32) if j == 0 else zero
@@ -87,22 +103,24 @@
         out_refs[k][...] = jnp.concatenate(rows, axis=0).astype(BF)
 
 
-def collect(atm, surface, parts):
+def collect(count, tile, block, fold_map, atm, surface, parts):
     levels, _, cols = atm.shape
     return pl.pallas_call(
         collect_kernel,
-        in_specs=hbm_specs(2),
-        out_specs=vmem_specs(parts),
-        out_shape=[jax.ShapeDtypeStruct((levels * SLAB, cols // parts), BF)] * parts,
-        scratch_shapes=[
+        in_specs=[smem_spec()] + hbm_specs(5),
+        out_specs=vmem_specs(parts + 1) + [smem_spec()],
+        out_shape=[jax.ShapeDtypeStruct((levels * SLAB, cols // parts), BF)] * parts
+        + [jax.ShapeDtypeStruct((1, 16, 128), BF), jax.ShapeDtypeStruct((8,), I32)],
+        scratch_shapes=[pltpu.SMEM(x.shape, I32) for x in (tile, block, fold_map)]
+        + [
             pltpu.VMEM((parts, levels, 6, cols // parts), BF),
             pltpu.VMEM((1, cols), BF),
-            pltpu.SemaphoreType.DMA((parts + 1,)),
+            pltpu.SemaphoreType.DMA((parts + 4,)),
         ],
         compiler_params=params(8),
         cost_estimate=pl.CostEstimate(flops=10**6, bytes_accessed=10**6, transcendentals=0),
         name="collect",
-    )(*in_hbm(atm, surface))
+    )(count, *in_hbm(tile, block, fold_map, atm, surface))
 
 
 def spread_kernel(*refs):
@@ -127,38 +145,6 @@
         cost_estimate=pl.CostEstimate(flops=10**6, bytes_accessed=10**6, transcendentals=0),
         name="spread",
     )(*back)
-
-
-def asking_kernel(count_ref, tile_in, block_in, fold_in, out_ref, seam_ref, tile_ref, block_ref, fold_ref, sems):
-    pairs = [(tile_in, tile_ref), (block_in, block_ref), (fold_in, fold_ref)]
-    for copy in fetch(pairs, sems):
-        copy.wait()
-    seam_ref[0] = fold_ref[0]
-    for p in range(4):
-        seam_ref[1 + p] = tile_ref[0, 0, p]
-    seam_ref[5] = count_ref[0, 0]
-    rows, zs = [], []
-    for p in range(4):
-        source, block = tile_ref[0, 0, p], block_ref[0, 0, p]
-        number = (source // (CS * ZS) * CS + lax.rem(source, CS)) * 16 + block
-        z = jnp.where(p < count_ref[0, 0], lax.rem(source // CS, ZS), -1)
-        rows.append(jnp.full((1, 128), number, I32))
-        zs.append(jnp.full((1, 128), z, I32))
-    out_ref[0] = jnp.concatenate(rows + zs + [jnp.zeros((8, 128), I32)], axis=0).astype(F32).astype(BF)
-
-
-def asking(tile, block, count, fold_map):
-    return pl.pallas_call(
-        asking_kernel,
-        in_specs=[smem_spec()] + hbm_specs(3),
-        out_specs=vmem_specs(1) + [smem_spec()],
-        out_shape=[jax.ShapeDtypeStruct((1, 16, 128), BF), jax.ShapeDtypeStruct((8,), I32)],
-        scratch_shapes=[pltpu.SMEM(x.shape, I32) for x in (tile, block, fold_map)]
-        + [pltpu.SemaphoreType.DMA((3,))],
-        compiler_params=params(4),
-        cost_estimate=pl.CostEstimate(flops=10**6, bytes_accessed=10**5, transcendentals=0),
-        name="asking",
-    )(count, *in_hbm(tile, block, fold_map))
 
 
 def prepare_kernel(
@@ -231,7 +217,7 @@
     z_refs, up_refs, send_ref = (z0_ref, z1_ref, z2_ref, z3_ref), out_refs[:4], out_refs[4]
     size, cols = z0_ref.shape
     rows = 4 * size
-    step = 512
+    step = 1024
     w1, w2, w3 = w1_ref[...], w2_ref[...], w3_ref[...]
     for c in range(0, cols, step):
         z = jnp.concatenate([ref[:, c : c + step].astype(F32) for ref in z_refs], axis=0)
@@ -288,11 +274,9 @@
             zs.append(jnp.broadcast_to(ask[4 + p : 5 + p], (8, 128)))
     number, zs = jnp.concatenate(number, axis=0), jnp.concatenate(zs, axis=0)
     wanted = jnp.where(zs == z_me, number * 8 + iota((256, 128), 0) % 8, -1)
-    total = None
-    for j in range(8):
-        pick = (wanted == iota((256, 128), 1) + 128 * j).astype(BF)
-        term = dot(pick, got_ref[j, 0:8].reshape(128, 128))
-        total = term if total is None else total + term
+    pick = [(wanted == iota((256, 128), 1) + 128 * j).astype(BF) for j in range(8)]
+    blocks = jnp.concatenate([got_ref[j, 0:8].reshape(128, 128) for j in range(8)], axis=0)
+    total = dot(jnp.concatenate(pick, axis=1), blocks)
     total = total.astype(BF).reshape(ZS, 2, 16, 128)
     for m in range(ZS):
         send_ref[ZS - 1 - (z_me ^ m), 0:2] = total[m]
@@ -469,7 +453,7 @@
         m = masks[x, lo : lo + size]
         return jnp.concatenate([m, m], axis=1)
 
-    chunk = 2
+    chunk = 4
     for c0 in range(0, n1, chunk):
         left = jnp.concatenate([v3[c0 + a : c0 + a + chunk].reshape(chunk * PITCH, 256) for a in range(3)], axis=1)
         acc = dot(left, w1_ref[...].reshape(768, 256))
@@ -641,14 +625,13 @@
     along_z = [[(x * ZS + z) * CS + c for z in reversed(range(ZS))] for x in range(tiles // (ZS * CS)) for c in range(CS)]
     same_z = [[(x * ZS + z) * CS + c for x in range(tiles // (ZS * CS)) for c in range(CS)] for z in range(ZS)]
 
-    pieces = collect(atm_state, surface, groups)
-    *pieces, tile_of, state_in = lax.optimization_barrier((*pieces, pair_tile, ocean_state))
+    *pieces, asks, seam = collect(pair_count, pair_tile, pair_block, fold_map, atm_state, surface, groups)
+    *pieces, asks, state_in = lax.optimization_barrier((*pieces, asks, ocean_state))
     pieces = [pieces[0]] + [turned(pieces[k], "lev", k) for k in range(1, groups)]
 
     def across(asks, bit):
         return lax.ppermute(asks, "tile", [(t, t ^ (CS * bit)) for t in range(tiles)])
 
-    asks, seam = asking(tile_of, pair_block, pair_count, fold_map)
     asks = jnp.concatenate([asks, across(asks, 1)], axis=0)
 
     state, *weights = prepare(state_in, ocean_mask, mlp_in, mlp_mid, mlp_out.T, mlp_flux.T)

time: 90.1 us -> 88.1 us (0.978)
  Pallas kernels: 27 us -> 25 us
    pallas_call x2 -> x1, Pallas kernels: 2.53 us -> 1.72 us  [collect(): pl.pallas_call(collect_kernel, in_specs=[smem_spec()] + hbm_specs(5), out...]
  transfers between devices with their start and end apart: 16 -> 16, of which waited for: 8 -> 8; matrix products, arithmetic and copies ran while one was open for 0% -> 0% of each run, Pallas kernels for 10% -> 9%
where the time goes in v4:
time: 88.1 us; the launch traced here: 87.6 us
  starting transfers between devices  50.9 us (58%)
  Pallas kernels  25 us (28%)
  waiting for transfers between devices  10.2 us (12%)
  between operations  1.54 us (2%)
    all_to_all x3, starting transfers between devices, per_tile(): lax.all_to_all(x, 'tile', split_axis=0, concat_axis=0, tiled=True, axis_i...  22.9 us
    ppermute x3, starting transfers between devices, across(): return lax.ppermute(asks, 'tile', [(t, t ^ CS * bit) for t in range(tiles)])  11.7 us
    pallas_call x1, Pallas kernels, convolutions(): pl.pallas_call(conv_kernel, in_specs=[smem_spec()] + vmem_specs(len(args)...  11.2 us
    ppermute x6, starting transfers between devices, turned(): return lax.ppermute(x, axis, [(i, (i + by) % count) for i in range(count)])  9.34 us
    ppermute x2, starting transfers between devices, shifted(): lax.ppermute(forth, axis, forward)  4.61 us
    pallas_call x1, Pallas kernels, column_model(): pl.pallas_call(mlp_kernel, in_specs=vmem_specs(8), out_specs=vmem_specs(5...  3.86 us
    ppermute x6, waiting for transfers between devices, turned(): return lax.ppermute(x, axis, [(i, (i + by) % count) for i in range(count)])  3.74 us
    ppermute x2, waiting for transfers between devices, shifted(): lax.ppermute(back, axis, backward)  2.82 us
  transfers between devices with their start and end apart: 16, of which 8 were waited for; matrix products, arithmetic and copies ran while one was open for 0% of the time, Pallas kernels for 9%

profile of v4, /device:TPU:16, one launch (start us, length us, event | category | flops | bytes accessed | tf_op | source)
XLA Modules:
  0.0 87.6 jit_solution(1126057570659724622)
XLA Ops:
  1.3 1.7 %collect.1 = (bf16[24,2048]{1,0:T(8,128)(2,1)S(1)}, bf16[24,2048]{1,0:T(8,128)(2,1)S(1)}, bf16[24,2048]{1,0:T(8,128)(2,1)S(1)}, bf16[24,2048]{1,0:T(8,128)(2,1)S...) custom-call(s32[1,1]{1,0:T(1,128)S(6)} %copy.19.count_ref, s32[1,1,4]{2,1,0:T(1,128)} %tile_in.1, ...), custom_call_target="tpu_custom_call" | custom-call | flops 1000000 | bytes 1000000 | tf_op jit(solution)/shard_map/collect/pallas_call | solution.py:108
  3.0 2.0 %collective-permute-start.3 = (bf16[1,16,128]{2,1,0:T(8,128)(2,1)S(1)}, bf16[1,16,128]{2,1,0:T(8,128)(2,1)S(1)}, u32[]{:S(2)}, u32[]{:S(2)}) collective-permute-start(bf16[1,16,128]{2,1,0:T(8,128)(2,1)S(1)} %get-tuple-element.57), channel_id=1, source_target_pairs={{0,2},{1,3},{2,0},{3,1},{4,6},{5,7},{6,4},{7,5},{8,10},{9,11},{10,... | collective-permute-start | bytes 12296 | tf_op jit(solution)/shard_map/ppermute | solution.py:633
  5.0 1.3 %collective-permute-start = (bf16[24,2048]{1,0:T(8,128)(2,1)S(1)}, bf16[24,2048]{1,0:T(8,128)(2,1)S(1)}, u32[]{:S(2)}, u32[]{:S(2)}) collective-permute-start(bf16[24,2048]{1,0:T(8,128)(2,1)S(1)} %get-tuple-element.49), channel_id=1, source_target_pairs={{0,64},{64,128},{128,192},{192,0},{1,65},{65,129},{129,193},{193,1... | collective-permute-start | bytes 294920 | tf_op jit(solution)/shard_map/ppermute | solution.py:595
  6.3 0.6 collective-permute-start.1
  6.9 1.1 %collective-permute-start.2 = (bf16[24,2048]{1,0:T(8,128)(2,1)S(1)}, bf16[24,2048]{1,0:T(8,128)(2,1)S(1)}, u32[]{:S(2)}, u32[]{:S(2)}) collective-permute-start(bf16[24,2048]{1,0:T(8,128)(2,1)S(1)} %get-tuple-element.51), channel_id=1, source_target_pairs={{0,192},{64,0},{128,64},{192,128},{1,193},{65,1},{129,65},{193,129... | collective-permute-start | bytes 294920 | tf_op jit(solution)/shard_map/ppermute | solution.py:595
  8.0 1.7 %prepare.1 = (bf16[16,128,128]{2,1,0:T(8,128)(2,1)S(1)}, bf16[512,96]{1,0:T(8,128)(2,1)S(1)}, bf16[512,512]{1,0:T(8,128)(2,1)S(1)}, bf16[104,512]{1,0:T(8,128)(2,1)S(1)}) custom-call(bf16[76,16,128]{2,1,0:T(8,128)(2,1)} %state_in, s32[16,128]{1,0:T(8,128)} %mask_in.1, bf16[76,512]{1,0:T(8,128)(2,1)} %win_in.2, bf16[512,512]{1,0:T(8,128)(2,1)} %wmid_in.1, ...), custom_call_target="tpu_custom_call" | custom-call | flops 1000000000 | bytes 1000000 | tf_op jit(solution)/shard_map/prepare/pallas_call | solution.py:197
  9.7 3.4 %collective-permute-start.7 = (bf16[2,16,128]{2,1,0:T(8,128)(2,1)S(1)}, bf16[2,16,128]{2,1,0:T(8,128)(2,1)S(1)}, u32[]{:S(2)}, u32[]{:S(2)}) collective-permute-start(bf16[2,16,128]{2,1,0:T(8,128)(2,1)S(1)} %pad_maximum_fusion), channel_id=1, source_target_pairs={{0,4},{1,5},{2,6},{3,7},{4,0},{5,1},{6,2},{7,3},{8,12},{9,13},{10,... | collective-permute-start | bytes 24584 | tf_op jit(solution)/shard_map/ppermute | solution.py:633
  13.0 0.2 collective-permute-done.2.z3_ref
  13.2 3.9 %column_model.1 = (bf16[24,2048]{1,0:T(8,128)(2,1)S(1)}, bf16[32,2048]{1,0:T(8,128)(2,1)S(1)}, bf16[24,2048]{1,0:T(8,128)(2,1)S(1)}, bf16[32,2048]{1,0:T(8,128)(2,1)S(1)}, bf16[8,11,16,128]{3,2,1,0:T(8,128)(2,1)}) custom-call(bf16[24,2048]{1,0:T(8,128)(2,1)S(1)} %get-tuple-element.48.z0_ref, bf16[24,2048]{1,0:T(8,128)(2,1)S(1)} %collective-permute-done.z1_ref, ...), custom_call_target="tpu_custom_call" | custom-call | flops 3000000000 | bytes 2000000 | tf_op jit(solution)/shard_map/column_model/pallas_call | solution.py:250
  17.1 4.3 %all-to-all-start = ((bf16[8,11,16,128]{3,2,1,0:T(8,128)(2,1)}), bf16[8,11,16,128]{3,2,1,0:T(8,128)(2,1)S(1)}, u32[]{:S(2)}, u32[]{:S(2)}) async-start(bf16[8,11,16,128]{3,2,1,0:T(8,128)(2,1)} %get-tuple-element.67), calls=%async_computation | async-start | bytes 720896 | tf_op jit(solution)/shard_map/all_to_all | solution.py:599
  21.4 6.4 %collective-permute-start.8 = (bf16[4,16,128]{2,1,0:T(8,128)(2,1)S(1)}, bf16[4,16,128]{2,1,0:T(8,128)(2,1)S(1)}, u32[]{:S(2)}, u32[]{:S(2)}) collective-permute-start(bf16[4,16,128]{2,1,0:T(8,128)(2,1)S(1)} %constant_dynamic-update-slice_fusion.near_ref), channel_id=1, source_target_pairs={{0,8},{1,9},{2,10},{3,11},{4,12},{5,13},{6,14},{7,15},{8,0},{9,1},... | collective-permute-start | bytes 49160 | tf_op jit(solution)/shard_map/ppermute | solution.py:633
  27.8 1.7 %collective-permute-done.8.far_ref = bf16[4,16,128]{2,1,0:T(8,128)(2,1)S(1)} collective-permute-done((bf16[4,16,128]{2,1,0:T(8,128)(2,1)S(1)}, bf16[4,16,128]{2,1,0:T(8,128)(2,1)S(1)}, u32[]{:S(2)}, u32[]{:S(2)}) %collective-permute-start.8) | collective-permute-done | bytes 16416 | tf_op jit(solution)/shard_map/ppermute | solution.py:633
  29.5 0.5 all-to-all-done.got_ref
  30.0 1.5 %pack.1 = bf16[8,5,16,128]{3,2,1,0:T(8,128)(2,1)} custom-call(s32[8]{0:T(128)S(1)} %get-tuple-element.63.seam_ref, bf16[4,16,128]{2,1,0:T(8,128)(2,1)S(1)} %constant_dynamic-update-slice_fusion.near_ref, bf16[4,16,128]{2,1,0:T(8,128)(2,1)S(1)} %collective-permute-done.8.far_ref, bf16[8,11,16,128]{3,2,1,0:T(8,128)(2,1)S(1)} %all-to-all-done.got_ref), custom_call_target="tpu_custom_call" | custom-call | flops 100000000 | bytes 1000000 | tf_op jit(solution)/shard_map/pack/pallas_call | solution.py:293
  31.5 8.3 %all-to-all-start.1 = ((bf16[8,5,16,128]{3,2,1,0:T(8,128)(2,1)}), bf16[8,5,16,128]{3,2,1,0:T(8,128)(2,1)S(1)}, u32[]{:S(2)}, u32[]{:S(2)}) async-start(bf16[8,5,16,128]{3,2,1,0:T(8,128)(2,1)} %pack.1), calls=%async_computation.1 | async-start | bytes 327680 | tf_op jit(solution)/shard_map/all_to_all | solution.py:599
  39.8 0.6 collective-permute-start.4
  40.4 1.4 %collective-permute-start.6 = (bf16[32,2048]{1,0:T(8,128)(2,1)S(1)}, bf16[32,2048]{1,0:T(8,128)(2,1)S(1)}, u32[]{:S(2)}, u32[]{:S(2)}) collective-permute-start(bf16[32,2048]{1,0:T(8,128)(2,1)S(1)} %get-tuple-element.62), channel_id=1, source_target_pairs={{0,64},{64,128},{128,192},{192,0},{1,65},{65,129},{129,193},{193,1... | collective-permute-start | bytes 393224 | tf_op jit(solution)/shard_map/ppermute | solution.py:595
  41.8 2.9 %collective-permute-done.4.refs_1_.north_ref.above_ref = bf16[32,2048]{1,0:T(8,128)(2,1)S(1)} collective-permute-done((bf16[32,2048]{1,0:T(8,128)(2,1)S(1)}, bf16[32,2048]{1,0:T(8,128)(2,1)S(1)}, u32[]{:S(2)}, u32[]{:S(2)}) %collective-permute-start.4) | collective-permute-done | bytes 131104 | tf_op jit(solution)/shard_map/ppermute | solution.py:595
  44.8 0.6 collective-permute-done.6.refs_3_.south_ref.below_ref
  45.4 0.3 all-to-all-done.1.got_ref
  45.7 2.3 %remap.1 = (bf16[128,128]{1,0:T(8,128)(2,1)S(1)}, bf16[512,128]{1,0:T(8,128)(2,1)S(1)}, bf16[512,128]{1,0:T(8,128)(2,1)S(1)}, bf16[64,8,128]{2,1,0:T(8,128)(2,1)}, bf16[3,16,128]{2,1,0:T(8,128)(2,1)S(1)}) custom-call(s32[8]{0:T(128)S(1)} %get-tuple-element.63.seam_ref, bf16[8,5,16,128]{3,2,1,0:T(8,128)(2,1)S(1)} %all-to-all-done.1.got_ref, ...), custom_call_target="tpu_custom_call" | custom-call | flops 1000000000 | bytes 3000000 | tf_op jit(solution)/shard_map/remap/pallas_call | solution.py:353
  48.0 10.3 %all-to-all-start.2 = ((bf16[64,8,128]{2,1,0:T(8,128)(2,1)}), bf16[64,8,128]{2,1,0:T(8,128)(2,1)S(1)}, u32[]{:S(2)}, u32[]{:S(2)}) async-start(bf16[64,8,128]{2,1,0:T(8,128)(2,1)} %get-tuple-element.80), calls=%async_computation.2 | async-start | bytes 262144 | tf_op jit(solution)/shard_map/all_to_all | solution.py:599
  58.3 0.4 collective-permute-start.10
  58.7 0.4 collective-permute-start.9
  59.1 4.3 %collective-permute-start.5 = (bf16[24,2048]{1,0:T(8,128)(2,1)S(1)}, bf16[24,2048]{1,0:T(8,128)(2,1)S(1)}, u32[]{:S(2)}, u32[]{:S(2)}) collective-permute-start(bf16[24,2048]{1,0:T(8,128)(2,1)S(1)} %get-tuple-element.61), channel_id=1, source_target_pairs={{0,128},{64,192},{128,0},{192,64},{1,129},{65,193},{129,1},{193,65... | collective-permute-start | bytes 294920 | tf_op jit(solution)/shard_map/ppermute | solution.py:595
  63.4 1.8 %conv_weights.1 = (bf16[3,256,256]{2,1,0:T(8,128)(2,1)S(1)}, bf16[3,256,256]{2,1,0:T(8,128)(2,1)S(1)}, bf16[384,768]{1,0:T(8,128)(2,1)S(1)}) custom-call(bf16[512,128]{1,0:T(8,128)(2,1)S(1)} %get-tuple-element.68.flux_ref, bf16[3,3,84,256]{3,2,1,0:T(8,128)(2,1)} %win_in.3, bf16[3,3,76,256]{3,2,1,0:T(8,128)(2,1)} %bitcast.7), custom_call_target="tpu_custom_call" | custom-call | flops 1000000000 | bytes 4000000 | tf_op jit(solution)/shard_map/conv_weights/pallas_call | solution.py:548
  65.3 1.1 %collective-permute-done.9.low_ref.west_ref = bf16[512,128]{1,0:T(8,128)(2,1)S(1)} collective-permute-done((bf16[512,128]{1,0:T(8,128)(2,1)S(1)}, bf16[512,128]{1,0:T(8,128)(2,1)S(1)}, u32[]{:S(2)}, u32[]{:S(2)}) %collective-permute-start.9) | collective-permute-done | bytes 131104 | tf_op jit(solution)/shard_map/ppermute | solution.py:590
  66.5 4.2 %collective-permute-start.11 = (bf16[16,256]{1,0:T(8,128)(2,1)S(1)}, bf16[16,256]{1,0:T(8,128)(2,1)S(1)}, u32[]{:S(2)}, u32[]{:S(2)}) collective-permute-start(bf16[16,256]{1,0:T(8,128)(2,1)S(1)} %get-tuple-element.78), channel_id=1, source_target_pairs={{0,64},{64,128},{128,192},{1,65},{65,129},{129,193},{2,66},{66,130... | collective-permute-start | bytes 24584 | tf_op jit(solution)/shard_map/ppermute | solution.py:590
  70.8 1.9 %collective-permute-start.12 = (bf16[16,256]{1,0:T(8,128)(2,1)S(1)}, bf16[16,256]{1,0:T(8,128)(2,1)S(1)}, u32[]{:S(2)}, u32[]{:S(2)}) collective-permute-start(bf16[16,256]{1,0:T(8,128)(2,1)S(1)} %get-tuple-element.79), channel_id=1, source_target_pairs={{64,0},{128,64},{192,128},{65,1},{129,65},{193,129},{66,2},{130,66... | collective-permute-start | bytes 24584 | tf_op jit(solution)/shard_map/ppermute | solution.py:590
  72.7 0.8 spread.1
  73.5 2.8 %collective-permute-done.12.north_ref = bf16[16,256]{1,0:T(8,128)(2,1)S(1)} collective-permute-done((bf16[16,256]{1,0:T(8,128)(2,1)S(1)}, bf16[16,256]{1,0:T(8,128)(2,1)S(1)}, u32[]{:S(2)}, u32[]{:S(2)}) %collective-permute-start.12) | collective-permute-done | bytes 8224 | tf_op jit(solution)/shard_map/ppermute | solution.py:590
  76.3 11.2 %convolutions.1 = bf16[76,16,128]{2,1,0:T(8,128)(2,1)} custom-call(s32[8]{0:T(128)S(1)} %get-tuple-element.63.seam_ref, bf16[16,128,128]{2,1,0:T(8,128)(2,1)S(1)} %get-tuple-element.58.state_ref, bf16[32,2048]{1,0:T(8,128)(2,1)S(1)} %collective-permute-done.6.refs_3_.south_ref.below_ref, ...), custom_call_target="tpu_custom_call" | custom-call | flops 8000000000 | bytes 8000000 | tf_op jit(solution)/shard_map/convolutions/pallas_call | solution.py:565
  (14 shorter events, 0.2 us)
Async XLA Ops:
  3.0 6.6 %collective-permute-start.3 = (bf16[1,16,128]{2,1,0:T(8,128)(2,1)S(1)}, bf16[1,16,128]{2,1,0:T(8,128)(2,1)S(1)}, u32[]{:S(2)}, u32[]{:S(2)}) collective-permute-start(bf16[1,16,128]{2,1,0:T(8,128)(2,1)S(1)} %get-tuple-element.57), channel_id=1, source_target_pairs={{0,2},{1,3},{2,0},{3,1},{4,6},{5,7},{6,4},{7,5},{8,10},{9,11},{10,... | collective-permute-start | bytes 12296 | tf_op jit(solution)/shard_map/ppermute | solution.py:633
  5.0 8.0 %collective-permute-start = (bf16[24,2048]{1,0:T(8,128)(2,1)S(1)}, bf16[24,2048]{1,0:T(8,128)(2,1)S(1)}, u32[]{:S(2)}, u32[]{:S(2)}) collective-permute-start(bf16[24,2048]{1,0:T(8,128)(2,1)S(1)} %get-tuple-element.49), channel_id=1, source_target_pairs={{0,64},{64,128},{128,192},{192,0},{1,65},{65,129},{129,193},{193,1... | collective-permute-start | bytes 294920 | tf_op jit(solution)/shard_map/ppermute | solution.py:595
  6.3 6.7 %collective-permute-start.1 = (bf16[24,2048]{1,0:T(8,128)(2,1)S(1)}, bf16[24,2048]{1,0:T(8,128)(2,1)S(1)}, u32[]{:S(2)}, u32[]{:S(2)}) collective-permute-start(bf16[24,2048]{1,0:T(8,128)(2,1)S(1)} %get-tuple-element.50), channel_id=1, source_target_pairs={{0,128},{64,192},{128,0},{192,64},{1,129},{65,193},{129,1},{193,65... | collective-permute-start | bytes 294920 | tf_op jit(solution)/shard_map/ppermute | solution.py:595
  6.9 6.3 %collective-permute-start.2 = (bf16[24,2048]{1,0:T(8,128)(2,1)S(1)}, bf16[24,2048]{1,0:T(8,128)(2,1)S(1)}, u32[]{:S(2)}, u32[]{:S(2)}) collective-permute-start(bf16[24,2048]{1,0:T(8,128)(2,1)S(1)} %get-tuple-element.51), channel_id=1, source_target_pairs={{0,192},{64,0},{128,64},{192,128},{1,193},{65,1},{129,65},{193,129... | collective-permute-start | bytes 294920 | tf_op jit(solution)/shard_map/ppermute | solution.py:595
  9.7 7.4 %collective-permute-start.7 = (bf16[2,16,128]{2,1,0:T(8,128)(2,1)S(1)}, bf16[2,16,128]{2,1,0:T(8,128)(2,1)S(1)}, u32[]{:S(2)}, u32[]{:S(2)}) collective-permute-start(bf16[2,16,128]{2,1,0:T(8,128)(2,1)S(1)} %pad_maximum_fusion), channel_id=1, source_target_pairs={{0,4},{1,5},{2,6},{3,7},{4,0},{5,1},{6,2},{7,3},{8,12},{9,13},{10,... | collective-permute-start | bytes 24584 | tf_op jit(solution)/shard_map/ppermute | solution.py:633
  13.2 32.5 %copy-start = (bf16[4,128,16,128]{3,2,1,0:T(8,128)(2,1)S(1)}, bf16[4,128,16,128]{3,2,1,0:T(8,128)(2,1)}, u32[]{:S(2)}) copy-start(bf16[4,128,16,128]{3,2,1,0:T(8,128)(2,1)} %param.28) | copy-start | bytes 6291460
  17.1 12.9 %all-to-all-start = ((bf16[8,11,16,128]{3,2,1,0:T(8,128)(2,1)}), bf16[8,11,16,128]{3,2,1,0:T(8,128)(2,1)S(1)}, u32[]{:S(2)}, u32[]{:S(2)}) async-start(bf16[8,11,16,128]{3,2,1,0:T(8,128)(2,1)} %get-tuple-element.67), calls=%async_computation | async-start | bytes 720896 | tf_op jit(solution)/shard_map/all_to_all | solution.py:599
  21.4 8.1 %collective-permute-start.8 = (bf16[4,16,128]{2,1,0:T(8,128)(2,1)S(1)}, bf16[4,16,128]{2,1,0:T(8,128)(2,1)S(1)}, u32[]{:S(2)}, u32[]{:S(2)}) collective-permute-start(bf16[4,16,128]{2,1,0:T(8,128)(2,1)S(1)} %constant_dynamic-update-slice_fusion.near_ref), channel_id=1, source_target_pairs={{0,8},{1,9},{2,10},{3,11},{4,12},{5,13},{6,14},{7,15},{8,0},{9,1},... | collective-permute-start | bytes 49160 | tf_op jit(solution)/shard_map/ppermute | solution.py:633
  31.5 14.1 %all-to-all-start.1 = ((bf16[8,5,16,128]{3,2,1,0:T(8,128)(2,1)}), bf16[8,5,16,128]{3,2,1,0:T(8,128)(2,1)S(1)}, u32[]{:S(2)}, u32[]{:S(2)}) async-start(bf16[8,5,16,128]{3,2,1,0:T(8,128)(2,1)} %pack.1), calls=%async_computation.1 | async-start | bytes 327680 | tf_op jit(solution)/shard_map/all_to_all | solution.py:599
  39.8 5.0 %collective-permute-start.4 = (bf16[32,2048]{1,0:T(8,128)(2,1)S(1)}, bf16[32,2048]{1,0:T(8,128)(2,1)S(1)}, u32[]{:S(2)}, u32[]{:S(2)}) collective-permute-start(bf16[32,2048]{1,0:T(8,128)(2,1)S(1)} %get-tuple-element.60), channel_id=1, source_target_pairs={{0,192},{64,0},{128,64},{192,128},{1,193},{65,1},{129,65},{193,129... | collective-permute-start | bytes 393224 | tf_op jit(solution)/shard_map/ppermute | solution.py:595
  40.4 5.0 %collective-permute-start.6 = (bf16[32,2048]{1,0:T(8,128)(2,1)S(1)}, bf16[32,2048]{1,0:T(8,128)(2,1)S(1)}, u32[]{:S(2)}, u32[]{:S(2)}) collective-permute-start(bf16[32,2048]{1,0:T(8,128)(2,1)S(1)} %get-tuple-element.62), channel_id=1, source_target_pairs={{0,64},{64,128},{128,192},{192,0},{1,65},{65,129},{129,193},{193,1... | collective-permute-start | bytes 393224 | tf_op jit(solution)/shard_map/ppermute | solution.py:595
  48.0 28.3 %all-to-all-start.2 = ((bf16[64,8,128]{2,1,0:T(8,128)(2,1)}), bf16[64,8,128]{2,1,0:T(8,128)(2,1)S(1)}, u32[]{:S(2)}, u32[]{:S(2)}) async-start(bf16[64,8,128]{2,1,0:T(8,128)(2,1)} %get-tuple-element.80), calls=%async_computation.2 | async-start | bytes 262144 | tf_op jit(solution)/shard_map/all_to_all | solution.py:599
  58.3 6.9 %collective-permute-start.10 = (bf16[512,128]{1,0:T(8,128)(2,1)S(1)}, bf16[512,128]{1,0:T(8,128)(2,1)S(1)}, u32[]{:S(2)}, u32[]{:S(2)}) collective-permute-start(bf16[512,128]{1,0:T(8,128)(2,1)S(1)} %get-tuple-element.69), channel_id=1, source_target_pairs={{1,0},{2,1},{3,2},{4,3},{5,4},{6,5},{7,6},{8,7},{9,8},{10,9},{11,1... | collective-permute-start | bytes 393224 | tf_op jit(solution)/shard_map/ppermute | solution.py:590
  58.7 7.7 %collective-permute-start.9 = (bf16[512,128]{1,0:T(8,128)(2,1)S(1)}, bf16[512,128]{1,0:T(8,128)(2,1)S(1)}, u32[]{:S(2)}, u32[]{:S(2)}) collective-permute-start(bf16[512,128]{1,0:T(8,128)(2,1)S(1)} %get-tuple-element.68.flux_ref), channel_id=1, source_target_pairs={{0,1},{1,2},{2,3},{3,4},{4,5},{5,6},{6,7},{7,8},{8,9},{9,10},{10,1... | collective-permute-start | bytes 393224 | tf_op jit(solution)/shard_map/ppermute | solution.py:590
  59.1 13.6 %collective-permute-start.5 = (bf16[24,2048]{1,0:T(8,128)(2,1)S(1)}, bf16[24,2048]{1,0:T(8,128)(2,1)S(1)}, u32[]{:S(2)}, u32[]{:S(2)}) collective-permute-start(bf16[24,2048]{1,0:T(8,128)(2,1)S(1)} %get-tuple-element.61), channel_id=1, source_target_pairs={{0,128},{64,192},{128,0},{192,64},{1,129},{65,193},{129,1},{193,65... | collective-permute-start | bytes 294920 | tf_op jit(solution)/shard_map/ppermute | solution.py:595
  66.5 7.0 %collective-permute-start.11 = (bf16[16,256]{1,0:T(8,128)(2,1)S(1)}, bf16[16,256]{1,0:T(8,128)(2,1)S(1)}, u32[]{:S(2)}, u32[]{:S(2)}) collective-permute-start(bf16[16,256]{1,0:T(8,128)(2,1)S(1)} %get-tuple-element.78), channel_id=1, source_target_pairs={{0,64},{64,128},{128,192},{1,65},{65,129},{129,193},{2,66},{66,130... | collective-permute-start | bytes 24584 | tf_op jit(solution)/shard_map/ppermute | solution.py:590
  70.8 5.5 %collective-permute-start.12 = (bf16[16,256]{1,0:T(8,128)(2,1)S(1)}, bf16[16,256]{1,0:T(8,128)(2,1)S(1)}, u32[]{:S(2)}, u32[]{:S(2)}) collective-permute-start(bf16[16,256]{1,0:T(8,128)(2,1)S(1)} %get-tuple-element.79), channel_id=1, source_target_pairs={{64,0},{128,64},{192,128},{65,1},{129,65},{193,129},{66,2},{130,66... | collective-permute-start | bytes 24584 | tf_op jit(solution)/shard_map/ppermute | solution.py:590

commit v5 on v4

--- a/solution.py
+++ b/solution.py
@@ -275,7 +275,7 @@
     number, zs = jnp.concatenate(number, axis=0), jnp.concatenate(zs, axis=0)
     wanted = jnp.where(zs == z_me, number * 8 + iota((256, 128), 0) % 8, -1)
     pick = [(wanted == iota((256, 128), 1) + 128 * j).astype(BF) for j in range(8)]
-    blocks = jnp.concatenate([got_ref[j, 0:8].reshape(128, 128) for j in range(8)], axis=0)
+    blocks = jnp.concatenate([got_ref[7 - j, 0:8].reshape(128, 128) for j in range(8)], axis=0)
     total = dot(jnp.concatenate(pick, axis=1), blocks)
     total = total.astype(BF).reshape(ZS, 2, 16, 128)
     for m in range(ZS):
@@ -284,7 +284,7 @@
     core = lax.rem(tile, CS)
     z_to = lax.rem(key - lax.rem(key - core, CS) - CS * z_me, CS * ZS) // CS
     source = lax.rem(key - (tile - CS * z_me + CS * z_to), 64)
-    strip = got_ref[source // (CS * ZS) * CS + lax.rem(source, CS), 8:11]
+    strip = got_ref[7 - (source // (CS * ZS) * CS + lax.rem(source, CS)), 8:11]
     for z in range(ZS):
         send_ref[z, 2:5] = strip
 
@@ -623,7 +623,7 @@
     _, span_x, span_y = ocean_state.shape
     pairs, blk = margin.shape[0], margin.shape[1]
     along_z = [[(x * ZS + z) * CS + c for z in reversed(range(ZS))] for x in range(tiles // (ZS * CS)) for c in range(CS)]
-    same_z = [[(x * ZS + z) * CS + c for x in range(tiles // (ZS * CS)) for c in range(CS)] for z in range(ZS)]
+    same_z = [[(x * ZS + z) * CS + c for x in range(tiles // (ZS * CS)) for c in range(CS)][::-1] for z in range(ZS)]
 
     *pieces, asks, seam = collect(pair_count, pair_tile, pair_block, fold_map, atm_state, surface, groups)
     *pieces, asks, state_in = lax.optimization_barrier((*pieces, asks, ocean_state))

time: 88.1 us -> 87.9 us (level)
  transfers between devices with their start and end apart: 16 -> 16, of which waited for: 8 -> 7; matrix products, arithmetic and copies ran while one was open for 0% -> 0% of each run, Pallas kernels for 9% -> 9%
where the time goes in v5:
time: 87.9 us; the launch traced here: 87.4 us
  starting transfers between devices  50.5 us (57%)
  Pallas kernels  25 us (28%)
  waiting for transfers between devices  10.4 us (12%)
  between operations  1.54 us (2%)
    all_to_all x3, starting transfers between devices, per_tile(): lax.all_to_all(x, 'tile', split_axis=0, concat_axis=0, tiled=True, axis_i...  22.4 us
    ppermute x3, starting transfers between devices, across(): return lax.ppermute(asks, 'tile', [(t, t ^ CS * bit) for t in range(tiles)])  11.7 us
    pallas_call x1, Pallas kernels, convolutions(): pl.pallas_call(conv_kernel, in_specs=[smem_spec()] + vmem_specs(len(args)...  11.2 us
    ppermute x6, starting transfers between devices, turned(): return lax.ppermute(x, axis, [(i, (i + by) % count) for i in range(count)])  9.38 us
    ppermute x2, starting transfers between devices, shifted(): lax.ppermute(forth, axis, forward)  4.64 us
    pallas_call x1, Pallas kernels, column_model(): pl.pallas_call(mlp_kernel, in_specs=vmem_specs(8), out_specs=vmem_specs(5...  3.86 us
    ppermute x6, waiting for transfers between devices, turned(): return lax.ppermute(x, axis, [(i, (i + by) % count) for i in range(count)])  3.76 us
    ppermute x2, waiting for transfers between devices, shifted(): lax.ppermute(back, axis, backward)  2.82 us
  transfers between devices with their start and end apart: 16, of which 7 were waited for; matrix products, arithmetic and copies ran while one was open for 0% of the time, Pallas kernels for 9%

profile of v5, /device:TPU:16, one launch (start us, length us, event | category | flops | bytes accessed | tf_op | source)
XLA Modules:
  0.0 87.4 jit_solution(7904276815402179980)
XLA Ops:
  1.3 1.7 %collect.1 = (bf16[24,2048]{1,0:T(8,128)(2,1)S(1)}, bf16[24,2048]{1,0:T(8,128)(2,1)S(1)}, bf16[24,2048]{1,0:T(8,128)(2,1)S(1)}, bf16[24,2048]{1,0:T(8,128)(2,1)S...) custom-call(s32[1,1]{1,0:T(1,128)S(6)} %copy.19.count_ref, s32[1,1,4]{2,1,0:T(1,128)} %tile_in.1, ...), custom_call_target="tpu_custom_call" | custom-call | flops 1000000 | bytes 1000000 | tf_op jit(solution)/shard_map/collect/pallas_call | solution.py:108
  3.0 2.0 %collective-permute-start.3 = (bf16[1,16,128]{2,1,0:T(8,128)(2,1)S(1)}, bf16[1,16,128]{2,1,0:T(8,128)(2,1)S(1)}, u32[]{:S(2)}, u32[]{:S(2)}) collective-permute-start(bf16[1,16,128]{2,1,0:T(8,128)(2,1)S(1)} %get-tuple-element.57), channel_id=1, source_target_pairs={{0,2},{1,3},{2,0},{3,1},{4,6},{5,7},{6,4},{7,5},{8,10},{9,11},{10,... | collective-permute-start | bytes 12296 | tf_op jit(solution)/shard_map/ppermute | solution.py:633
  5.0 1.3 %collective-permute-start = (bf16[24,2048]{1,0:T(8,128)(2,1)S(1)}, bf16[24,2048]{1,0:T(8,128)(2,1)S(1)}, u32[]{:S(2)}, u32[]{:S(2)}) collective-permute-start(bf16[24,2048]{1,0:T(8,128)(2,1)S(1)} %get-tuple-element.49), channel_id=1, source_target_pairs={{0,64},{64,128},{128,192},{192,0},{1,65},{65,129},{129,193},{193,1... | collective-permute-start | bytes 294920 | tf_op jit(solution)/shard_map/ppermute | solution.py:595
  6.3 0.6 collective-permute-start.1
  6.9 1.1 %collective-permute-start.2 = (bf16[24,2048]{1,0:T(8,128)(2,1)S(1)}, bf16[24,2048]{1,0:T(8,128)(2,1)S(1)}, u32[]{:S(2)}, u32[]{:S(2)}) collective-permute-start(bf16[24,2048]{1,0:T(8,128)(2,1)S(1)} %get-tuple-element.51), channel_id=1, source_target_pairs={{0,192},{64,0},{128,64},{192,128},{1,193},{65,1},{129,65},{193,129... | collective-permute-start | bytes 294920 | tf_op jit(solution)/shard_map/ppermute | solution.py:595
  8.0 1.7 %prepare.1 = (bf16[16,128,128]{2,1,0:T(8,128)(2,1)S(1)}, bf16[512,96]{1,0:T(8,128)(2,1)S(1)}, bf16[512,512]{1,0:T(8,128)(2,1)S(1)}, bf16[104,512]{1,0:T(8,128)(2,1)S(1)}) custom-call(bf16[76,16,128]{2,1,0:T(8,128)(2,1)} %state_in, s32[16,128]{1,0:T(8,128)} %mask_in.1, bf16[76,512]{1,0:T(8,128)(2,1)} %win_in.2, bf16[512,512]{1,0:T(8,128)(2,1)} %wmid_in.1, ...), custom_call_target="tpu_custom_call" | custom-call | flops 1000000000 | bytes 1000000 | tf_op jit(solution)/shard_map/prepare/pallas_call | solution.py:197
  9.7 3.4 %collective-permute-start.7 = (bf16[2,16,128]{2,1,0:T(8,128)(2,1)S(1)}, bf16[2,16,128]{2,1,0:T(8,128)(2,1)S(1)}, u32[]{:S(2)}, u32[]{:S(2)}) collective-permute-start(bf16[2,16,128]{2,1,0:T(8,128)(2,1)S(1)} %pad_maximum_fusion), channel_id=1, source_target_pairs={{0,4},{1,5},{2,6},{3,7},{4,0},{5,1},{6,2},{7,3},{8,12},{9,13},{10,... | collective-permute-start | bytes 24584 | tf_op jit(solution)/shard_map/ppermute | solution.py:633
  13.0 0.2 collective-permute-done.2.z3_ref
  13.2 3.9 %column_model.1 = (bf16[24,2048]{1,0:T(8,128)(2,1)S(1)}, bf16[32,2048]{1,0:T(8,128)(2,1)S(1)}, bf16[24,2048]{1,0:T(8,128)(2,1)S(1)}, bf16[32,2048]{1,0:T(8,128)(2,1)S(1)}, bf16[8,11,16,128]{3,2,1,0:T(8,128)(2,1)}) custom-call(bf16[24,2048]{1,0:T(8,128)(2,1)S(1)} %get-tuple-element.48.z0_ref, bf16[24,2048]{1,0:T(8,128)(2,1)S(1)} %collective-permute-done.z1_ref, ...), custom_call_target="tpu_custom_call" | custom-call | flops 3000000000 | bytes 2000000 | tf_op jit(solution)/shard_map/column_model/pallas_call | solution.py:250
  17.1 5.2 %all-to-all-start = ((bf16[8,11,16,128]{3,2,1,0:T(8,128)(2,1)}), bf16[8,11,16,128]{3,2,1,0:T(8,128)(2,1)S(1)}, u32[]{:S(2)}, u32[]{:S(2)}) async-start(bf16[8,11,16,128]{3,2,1,0:T(8,128)(2,1)} %get-tuple-element.67), calls=%async_computation | async-start | bytes 720896 | tf_op jit(solution)/shard_map/all_to_all | solution.py:599
  22.3 6.4 %collective-permute-start.8 = (bf16[4,16,128]{2,1,0:T(8,128)(2,1)S(1)}, bf16[4,16,128]{2,1,0:T(8,128)(2,1)S(1)}, u32[]{:S(2)}, u32[]{:S(2)}) collective-permute-start(bf16[4,16,128]{2,1,0:T(8,128)(2,1)S(1)} %constant_dynamic-update-slice_fusion.near_ref), channel_id=1, source_target_pairs={{0,8},{1,9},{2,10},{3,11},{4,12},{5,13},{6,14},{7,15},{8,0},{9,1},... | collective-permute-start | bytes 49160 | tf_op jit(solution)/shard_map/ppermute | solution.py:633
  28.7 1.7 %collective-permute-done.8.far_ref = bf16[4,16,128]{2,1,0:T(8,128)(2,1)S(1)} collective-permute-done((bf16[4,16,128]{2,1,0:T(8,128)(2,1)S(1)}, bf16[4,16,128]{2,1,0:T(8,128)(2,1)S(1)}, u32[]{:S(2)}, u32[]{:S(2)}) %collective-permute-start.8) | collective-permute-done | bytes 16416 | tf_op jit(solution)/shard_map/ppermute | solution.py:633
  30.4 1.5 %pack.1 = bf16[8,5,16,128]{3,2,1,0:T(8,128)(2,1)} custom-call(s32[8]{0:T(128)S(1)} %get-tuple-element.63.seam_ref, bf16[4,16,128]{2,1,0:T(8,128)(2,1)S(1)} %constant_dynamic-update-slice_fusion.near_ref, bf16[4,16,128]{2,1,0:T(8,128)(2,1)S(1)} %collective-permute-done.8.far_ref, bf16[8,11,16,128]{3,2,1,0:T(8,128)(2,1)S(1)} %all-to-all-done.got_ref), custom_call_target="tpu_custom_call" | custom-call | flops 100000000 | bytes 1000000 | tf_op jit(solution)/shard_map/pack/pallas_call | solution.py:293
  31.9 7.9 %all-to-all-start.1 = ((bf16[8,5,16,128]{3,2,1,0:T(8,128)(2,1)}), bf16[8,5,16,128]{3,2,1,0:T(8,128)(2,1)S(1)}, u32[]{:S(2)}, u32[]{:S(2)}) async-start(bf16[8,5,16,128]{3,2,1,0:T(8,128)(2,1)} %pack.1), calls=%async_computation.1 | async-start | bytes 327680 | tf_op jit(solution)/shard_map/all_to_all | solution.py:599
  39.8 0.6 collective-permute-start.4
  40.5 1.4 %collective-permute-start.6 = (bf16[32,2048]{1,0:T(8,128)(2,1)S(1)}, bf16[32,2048]{1,0:T(8,128)(2,1)S(1)}, u32[]{:S(2)}, u32[]{:S(2)}) collective-permute-start(bf16[32,2048]{1,0:T(8,128)(2,1)S(1)} %get-tuple-element.62), channel_id=1, source_target_pairs={{0,64},{64,128},{128,192},{192,0},{1,65},{65,129},{129,193},{193,1... | collective-permute-start | bytes 393224 | tf_op jit(solution)/shard_map/ppermute | solution.py:595
  41.9 2.9 %collective-permute-done.4.refs_1_.north_ref.above_ref = bf16[32,2048]{1,0:T(8,128)(2,1)S(1)} collective-permute-done((bf16[32,2048]{1,0:T(8,128)(2,1)S(1)}, bf16[32,2048]{1,0:T(8,128)(2,1)S(1)}, u32[]{:S(2)}, u32[]{:S(2)}) %collective-permute-start.4) | collective-permute-done | bytes 131104 | tf_op jit(solution)/shard_map/ppermute | solution.py:595
  44.8 0.6 collective-permute-done.6.refs_3_.south_ref.below_ref
  45.5 0.9 %all-to-all-done.1.got_ref = bf16[8,5,16,128]{3,2,1,0:T(8,128)(2,1)S(1)} async-done(((bf16[8,5,16,128]{3,2,1,0:T(8,128)(2,1)}), bf16[8,5,16,128]{3,2,1,0:T(8,128)(2,1)S(1)}, u32[]{:S(2)}, u32[]{:S(2)}) %all-to-all-start.1) | async-done | bytes 163872 | tf_op jit(solution)/shard_map/all_to_all | solution.py:599
  46.4 2.3 %remap.1 = (bf16[128,128]{1,0:T(8,128)(2,1)S(1)}, bf16[512,128]{1,0:T(8,128)(2,1)S(1)}, bf16[512,128]{1,0:T(8,128)(2,1)S(1)}, bf16[64,8,128]{2,1,0:T(8,128)(2,1)}, bf16[3,16,128]{2,1,0:T(8,128)(2,1)S(1)}) custom-call(s32[8]{0:T(128)S(1)} %get-tuple-element.63.seam_ref, bf16[8,5,16,128]{3,2,1,0:T(8,128)(2,1)S(1)} %all-to-all-done.1.got_ref, ...), custom_call_target="tpu_custom_call" | custom-call | flops 1000000000 | bytes 3000000 | tf_op jit(solution)/shard_map/remap/pallas_call | solution.py:353
  48.7 9.3 %all-to-all-start.2 = ((bf16[64,8,128]{2,1,0:T(8,128)(2,1)}), bf16[64,8,128]{2,1,0:T(8,128)(2,1)S(1)}, u32[]{:S(2)}, u32[]{:S(2)}) async-start(bf16[64,8,128]{2,1,0:T(8,128)(2,1)} %get-tuple-element.80), calls=%async_computation.2 | async-start | bytes 262144 | tf_op jit(solution)/shard_map/all_to_all | solution.py:599
  58.0 0.4 collective-permute-start.10
  58.4 0.4 collective-permute-start.9
  58.8 4.4 %collective-permute-start.5 = (bf16[24,2048]{1,0:T(8,128)(2,1)S(1)}, bf16[24,2048]{1,0:T(8,128)(2,1)S(1)}, u32[]{:S(2)}, u32[]{:S(2)}) collective-permute-start(bf16[24,2048]{1,0:T(8,128)(2,1)S(1)} %get-tuple-element.61), channel_id=1, source_target_pairs={{0,128},{64,192},{128,0},{192,64},{1,129},{65,193},{129,1},{193,65... | collective-permute-start | bytes 294920 | tf_op jit(solution)/shard_map/ppermute | solution.py:595
  63.2 1.8 %conv_weights.1 = (bf16[3,256,256]{2,1,0:T(8,128)(2,1)S(1)}, bf16[3,256,256]{2,1,0:T(8,128)(2,1)S(1)}, bf16[384,768]{1,0:T(8,128)(2,1)S(1)}) custom-call(bf16[512,128]{1,0:T(8,128)(2,1)S(1)} %get-tuple-element.68.flux_ref, bf16[3,3,84,256]{3,2,1,0:T(8,128)(2,1)} %win_in.3, bf16[3,3,76,256]{3,2,1,0:T(8,128)(2,1)} %bitcast.7), custom_call_target="tpu_custom_call" | custom-call | flops 1000000000 | bytes 4000000 | tf_op jit(solution)/shard_map/conv_weights/pallas_call | solution.py:548
  65.0 1.1 %collective-permute-done.9.low_ref.west_ref = bf16[512,128]{1,0:T(8,128)(2,1)S(1)} collective-permute-done((bf16[512,128]{1,0:T(8,128)(2,1)S(1)}, bf16[512,128]{1,0:T(8,128)(2,1)S(1)}, u32[]{:S(2)}, u32[]{:S(2)}) %collective-permute-start.9) | collective-permute-done | bytes 131104 | tf_op jit(solution)/shard_map/ppermute | solution.py:590
  66.1 0.1 rim.1
  66.2 4.2 %collective-permute-start.11 = (bf16[16,256]{1,0:T(8,128)(2,1)S(1)}, bf16[16,256]{1,0:T(8,128)(2,1)S(1)}, u32[]{:S(2)}, u32[]{:S(2)}) collective-permute-start(bf16[16,256]{1,0:T(8,128)(2,1)S(1)} %get-tuple-element.78), channel_id=1, source_target_pairs={{0,64},{64,128},{128,192},{1,65},{65,129},{129,193},{2,66},{66,130... | collective-permute-start | bytes 24584 | tf_op jit(solution)/shard_map/ppermute | solution.py:590
  70.5 1.9 %collective-permute-start.12 = (bf16[16,256]{1,0:T(8,128)(2,1)S(1)}, bf16[16,256]{1,0:T(8,128)(2,1)S(1)}, u32[]{:S(2)}, u32[]{:S(2)}) collective-permute-start(bf16[16,256]{1,0:T(8,128)(2,1)S(1)} %get-tuple-element.79), channel_id=1, source_target_pairs={{64,0},{128,64},{192,128},{65,1},{129,65},{193,129},{66,2},{130,66... | collective-permute-start | bytes 24584 | tf_op jit(solution)/shard_map/ppermute | solution.py:590
  72.4 0.8 spread.1
  73.2 2.8 %collective-permute-done.12.north_ref = bf16[16,256]{1,0:T(8,128)(2,1)S(1)} collective-permute-done((bf16[16,256]{1,0:T(8,128)(2,1)S(1)}, bf16[16,256]{1,0:T(8,128)(2,1)S(1)}, u32[]{:S(2)}, u32[]{:S(2)}) %collective-permute-start.12) | collective-permute-done | bytes 8224 | tf_op jit(solution)/shard_map/ppermute | solution.py:590
  76.0 11.2 %convolutions.1 = bf16[76,16,128]{2,1,0:T(8,128)(2,1)} custom-call(s32[8]{0:T(128)S(1)} %get-tuple-element.63.seam_ref, bf16[16,128,128]{2,1,0:T(8,128)(2,1)S(1)} %get-tuple-element.58.state_ref, bf16[32,2048]{1,0:T(8,128)(2,1)S(1)} %collective-permute-done.6.refs_3_.south_ref.below_ref, ...), custom_call_target="tpu_custom_call" | custom-call | flops 8000000000 | bytes 8000000 | tf_op jit(solution)/shard_map/convolutions/pallas_call | solution.py:565
  (14 shorter events, 0.0 us)
Async XLA Ops:
  3.0 6.6 %collective-permute-start.3 = (bf16[1,16,128]{2,1,0:T(8,128)(2,1)S(1)}, bf16[1,16,128]{2,1,0:T(8,128)(2,1)S(1)}, u32[]{:S(2)}, u32[]{:S(2)}) collective-permute-start(bf16[1,16,128]{2,1,0:T(8,128)(2,1)S(1)} %get-tuple-element.57), channel_id=1, source_target_pairs={{0,2},{1,3},{2,0},{3,1},{4,6},{5,7},{6,4},{7,5},{8,10},{9,11},{10,... | collective-permute-start | bytes 12296 | tf_op jit(solution)/shard_map/ppermute | solution.py:633
  5.0 8.0 %collective-permute-start = (bf16[24,2048]{1,0:T(8,128)(2,1)S(1)}, bf16[24,2048]{1,0:T(8,128)(2,1)S(1)}, u32[]{:S(2)}, u32[]{:S(2)}) collective-permute-start(bf16[24,2048]{1,0:T(8,128)(2,1)S(1)} %get-tuple-element.49), channel_id=1, source_target_pairs={{0,64},{64,128},{128,192},{192,0},{1,65},{65,129},{129,193},{193,1... | collective-permute-start | bytes 294920 | tf_op jit(solution)/shard_map/ppermute | solution.py:595
  6.3 6.7 %collective-permute-start.1 = (bf16[24,2048]{1,0:T(8,128)(2,1)S(1)}, bf16[24,2048]{1,0:T(8,128)(2,1)S(1)}, u32[]{:S(2)}, u32[]{:S(2)}) collective-permute-start(bf16[24,2048]{1,0:T(8,128)(2,1)S(1)} %get-tuple-element.50), channel_id=1, source_target_pairs={{0,128},{64,192},{128,0},{192,64},{1,129},{65,193},{129,1},{193,65... | collective-permute-start | bytes 294920 | tf_op jit(solution)/shard_map/ppermute | solution.py:595
  6.9 6.3 %collective-permute-start.2 = (bf16[24,2048]{1,0:T(8,128)(2,1)S(1)}, bf16[24,2048]{1,0:T(8,128)(2,1)S(1)}, u32[]{:S(2)}, u32[]{:S(2)}) collective-permute-start(bf16[24,2048]{1,0:T(8,128)(2,1)S(1)} %get-tuple-element.51), channel_id=1, source_target_pairs={{0,192},{64,0},{128,64},{192,128},{1,193},{65,1},{129,65},{193,129... | collective-permute-start | bytes 294920 | tf_op jit(solution)/shard_map/ppermute | solution.py:595
  9.7 7.4 %collective-permute-start.7 = (bf16[2,16,128]{2,1,0:T(8,128)(2,1)S(1)}, bf16[2,16,128]{2,1,0:T(8,128)(2,1)S(1)}, u32[]{:S(2)}, u32[]{:S(2)}) collective-permute-start(bf16[2,16,128]{2,1,0:T(8,128)(2,1)S(1)} %pad_maximum_fusion), channel_id=1, source_target_pairs={{0,4},{1,5},{2,6},{3,7},{4,0},{5,1},{6,2},{7,3},{8,12},{9,13},{10,... | collective-permute-start | bytes 24584 | tf_op jit(solution)/shard_map/ppermute | solution.py:633
  13.2 33.2 %copy-start = (bf16[4,128,16,128]{3,2,1,0:T(8,128)(2,1)S(1)}, bf16[4,128,16,128]{3,2,1,0:T(8,128)(2,1)}, u32[]{:S(2)}) copy-start(bf16[4,128,16,128]{3,2,1,0:T(8,128)(2,1)} %param.28) | copy-start | bytes 6291460
  17.1 13.3 %all-to-all-start = ((bf16[8,11,16,128]{3,2,1,0:T(8,128)(2,1)}), bf16[8,11,16,128]{3,2,1,0:T(8,128)(2,1)S(1)}, u32[]{:S(2)}, u32[]{:S(2)}) async-start(bf16[8,11,16,128]{3,2,1,0:T(8,128)(2,1)} %get-tuple-element.67), calls=%async_computation | async-start | bytes 720896 | tf_op jit(solution)/shard_map/all_to_all | solution.py:599
  22.3 8.1 %collective-permute-start.8 = (bf16[4,16,128]{2,1,0:T(8,128)(2,1)S(1)}, bf16[4,16,128]{2,1,0:T(8,128)(2,1)S(1)}, u32[]{:S(2)}, u32[]{:S(2)}) collective-permute-start(bf16[4,16,128]{2,1,0:T(8,128)(2,1)S(1)} %constant_dynamic-update-slice_fusion.near_ref), channel_id=1, source_target_pairs={{0,8},{1,9},{2,10},{3,11},{4,12},{5,13},{6,14},{7,15},{8,0},{9,1},... | collective-permute-start | bytes 49160 | tf_op jit(solution)/shard_map/ppermute | solution.py:633
  31.9 14.5 %all-to-all-start.1 = ((bf16[8,5,16,128]{3,2,1,0:T(8,128)(2,1)}), bf16[8,5,16,128]{3,2,1,0:T(8,128)(2,1)S(1)}, u32[]{:S(2)}, u32[]{:S(2)}) async-start(bf16[8,5,16,128]{3,2,1,0:T(8,128)(2,1)} %pack.1), calls=%async_computation.1 | async-start | bytes 327680 | tf_op jit(solution)/shard_map/all_to_all | solution.py:599
  39.8 5.0 %collective-permute-start.4 = (bf16[32,2048]{1,0:T(8,128)(2,1)S(1)}, bf16[32,2048]{1,0:T(8,128)(2,1)S(1)}, u32[]{:S(2)}, u32[]{:S(2)}) collective-permute-start(bf16[32,2048]{1,0:T(8,128)(2,1)S(1)} %get-tuple-element.60), channel_id=1, source_target_pairs={{0,192},{64,0},{128,64},{192,128},{1,193},{65,1},{129,65},{193,129... | collective-permute-start | bytes 393224 | tf_op jit(solution)/shard_map/ppermute | solution.py:595
  40.5 5.0 %collective-permute-start.6 = (bf16[32,2048]{1,0:T(8,128)(2,1)S(1)}, bf16[32,2048]{1,0:T(8,128)(2,1)S(1)}, u32[]{:S(2)}, u32[]{:S(2)}) collective-permute-start(bf16[32,2048]{1,0:T(8,128)(2,1)S(1)} %get-tuple-element.62), channel_id=1, source_target_pairs={{0,64},{64,128},{128,192},{192,0},{1,65},{65,129},{129,193},{193,1... | collective-permute-start | bytes 393224 | tf_op jit(solution)/shard_map/ppermute | solution.py:595
  48.7 27.3 %all-to-all-start.2 = ((bf16[64,8,128]{2,1,0:T(8,128)(2,1)}), bf16[64,8,128]{2,1,0:T(8,128)(2,1)S(1)}, u32[]{:S(2)}, u32[]{:S(2)}) async-start(bf16[64,8,128]{2,1,0:T(8,128)(2,1)} %get-tuple-element.80), calls=%async_computation.2 | async-start | bytes 262144 | tf_op jit(solution)/shard_map/all_to_all | solution.py:599
  58.0 7.0 %collective-permute-start.10 = (bf16[512,128]{1,0:T(8,128)(2,1)S(1)}, bf16[512,128]{1,0:T(8,128)(2,1)S(1)}, u32[]{:S(2)}, u32[]{:S(2)}) collective-permute-start(bf16[512,128]{1,0:T(8,128)(2,1)S(1)} %get-tuple-element.69), channel_id=1, source_target_pairs={{1,0},{2,1},{3,2},{4,3},{5,4},{6,5},{7,6},{8,7},{9,8},{10,9},{11,1... | collective-permute-start | bytes 393224 | tf_op jit(solution)/shard_map/ppermute | solution.py:590
  58.4 7.7 %collective-permute-start.9 = (bf16[512,128]{1,0:T(8,128)(2,1)S(1)}, bf16[512,128]{1,0:T(8,128)(2,1)S(1)}, u32[]{:S(2)}, u32[]{:S(2)}) collective-permute-start(bf16[512,128]{1,0:T(8,128)(2,1)S(1)} %get-tuple-element.68.flux_ref), channel_id=1, source_target_pairs={{0,1},{1,2},{2,3},{3,4},{4,5},{5,6},{6,7},{7,8},{8,9},{9,10},{10,1... | collective-permute-start | bytes 393224 | tf_op jit(solution)/shard_map/ppermute | solution.py:590
  58.8 13.6 %collective-permute-start.5 = (bf16[24,2048]{1,0:T(8,128)(2,1)S(1)}, bf16[24,2048]{1,0:T(8,128)(2,1)S(1)}, u32[]{:S(2)}, u32[]{:S(2)}) collective-permute-start(bf16[24,2048]{1,0:T(8,128)(2,1)S(1)} %get-tuple-element.61), channel_id=1, source_target_pairs={{0,128},{64,192},{128,0},{192,64},{1,129},{65,193},{129,1},{193,65... | collective-permute-start | bytes 294920 | tf_op jit(solution)/shard_map/ppermute | solution.py:595
  66.2 7.0 %collective-permute-start.11 = (bf16[16,256]{1,0:T(8,128)(2,1)S(1)}, bf16[16,256]{1,0:T(8,128)(2,1)S(1)}, u32[]{:S(2)}, u32[]{:S(2)}) collective-permute-start(bf16[16,256]{1,0:T(8,128)(2,1)S(1)} %get-tuple-element.78), channel_id=1, source_target_pairs={{0,64},{64,128},{128,192},{1,65},{65,129},{129,193},{2,66},{66,130... | collective-permute-start | bytes 24584 | tf_op jit(solution)/shard_map/ppermute | solution.py:590
  70.5 5.5 %collective-permute-start.12 = (bf16[16,256]{1,0:T(8,128)(2,1)S(1)}, bf16[16,256]{1,0:T(8,128)(2,1)S(1)}, u32[]{:S(2)}, u32[]{:S(2)}) collective-permute-start(bf16[16,256]{1,0:T(8,128)(2,1)S(1)} %get-tuple-element.79), channel_id=1, source_target_pairs={{64,0},{128,64},{192,128},{65,1},{129,65},{193,129},{66,2},{130,66... | collective-permute-start | bytes 24584 | tf_op jit(solution)/shard_map/ppermute | solution.py:590
